TPU v7x, 32 devices: a whole 2x2x4 slice. The times are simulated.
32 devices in a mesh: gz: 8 (over y, x, core), gy: 4 (over z).
Axes of the slice: x: 2, y: 2, z: 4, core: 2. Of those that a mesh axis runs over, the one named last changes fastest.
Arguments:
- init: float32 [128, 512, 512], P('gz', None, 'gy'), may hold values from -6 to 6
- measured: float32 [4, 128, 512, 512], P(None, None, 'gz', 'gy'), may hold values from -70 to 70
- mask: int32 [8, 8], replicated, may hold values from 0 to 1, as said below
- kernel_index: int32 [4, 8, 8], replicated, may hold values from 0 to 15
- kernels: float32 [16, 31], replicated, may hold values from 0.02 to 0.3
Outputs:
- solved: float32 [128, 512, 512], P('gz', None, 'gy')
Inputs may be any that keep to these rules, and one draw needn't show every extreme that they name: `mask`: 1 marks a tissue block; in each aligned region of 64 x 128 lateral cells, whose blocks start at multiples of 64 and 128, exactly 1 block is 1.
All inputs are finite; a program needn't handle non-finite values.
Results may differ from a plain program's by a relative error of at most 0.0003.
Values sent between devices are 32-bit elements; how exact they have to be, the bound alone decides.
No kernel may reach another device: no remote copies, remote signals or barrier semaphores. Data moves between devices by JAX's collectives and lax.ppermute only.
A program may use at most 128 MiB of HBM per device.

v0:
```python
import jax
import jax.numpy as jnp
from jax import lax
from jax.sharding import PartitionSpec as P

NZ = 128
XT = 64
YD = 128
BX = 64
BY = 64
ZBW = 16
TAPS = 31
VIEWS = 4
NK = 16
ITERS = 4
HALF = 15


HIGHEST = lax.Precision.HIGHEST
damping = 1.0


def blur_tables(kernel_index, kernels):
    onehot = (kernel_index[..., None] == jnp.arange(NK, dtype=jnp.int32)).astype(jnp.float32)
    tap_values = jnp.einsum("vabk,kt->vabt", onehot, kernels, precision=HIGHEST)
    row_taps = jnp.repeat(tap_values, ZBW, axis=1)
    depths = jnp.arange(NZ, dtype=jnp.int32)
    offset = depths[None, :] - depths[:, None] + HALF
    tap_select = (offset[:, :, None] == jnp.arange(TAPS, dtype=jnp.int32)).astype(jnp.float32)
    return jnp.einsum("vzbt,zwt->vbzw", row_taps, tap_select, precision=HIGHEST)


def conjugate(start_field, residual, operate):
    solved = start_field
    direction = residual
    norm_now = lax.psum(jnp.sum(residual * residual), ("gz", "gy"))
    for iteration in range(ITERS):
        image_field = operate(direction)
        curvature, cross_term, square = lax.psum(
            (
                jnp.sum(direction * image_field),
                jnp.sum(residual * image_field),
                jnp.sum(image_field * image_field),
            ),
            ("gz", "gy"),
        )
        step_size = norm_now / curvature
        norm_next = norm_now - 2.0 * step_size * cross_term + step_size * step_size * square
        solved = solved + step_size * direction
        residual = residual - step_size * image_field
        direction = residual + norm_next / norm_now * direction
        norm_now = norm_next
    return solved


def local(init, measured, mask, kernel_index, kernels):
    bands_here = XT // BX
    yblock_count = YD // BY
    tile_index = lax.axis_index("gz")
    row_index = lax.axis_index("gy")
    local_index = lax.dynamic_slice_in_dim(kernel_index, tile_index * bands_here, bands_here, 2)
    blur_mats = blur_tables(local_index, kernels)
    gram_mats = jnp.einsum("vbzw,vbzu->bwu", blur_mats, blur_mats, precision=HIGHEST)
    start_field = lax.all_to_all(init, "gz", split_axis=1, concat_axis=0, tiled=True)
    mask_block = lax.dynamic_slice(
        mask, (tile_index * bands_here, row_index * yblock_count), (bands_here, yblock_count)
    )
    tissue = jnp.repeat(jnp.repeat(mask_block.astype(jnp.float32), BX, axis=0), BY, axis=1)
    view_data = measured.reshape(VIEWS, NZ, bands_here, BX, YD)
    projected = jnp.einsum("vbzw,vzbxy->wbxy", blur_mats, view_data, precision=HIGHEST).reshape(
        NZ, XT, YD
    )

    def apply_gram(field):
        product = jnp.einsum(
            "bwz,zbxy->wbxy", gram_mats, field.reshape(NZ, bands_here, BX, YD), precision=HIGHEST
        )
        return product.reshape(NZ, XT, YD)

    def operate(field):
        return damping * field + tissue * apply_gram(field)

    residual = tissue * (projected - apply_gram(start_field))
    solved = conjugate(start_field, residual, operate)
    return lax.all_to_all(solved, "gz", split_axis=0, concat_axis=1, tiled=True)


def solution(mesh):
    return jax.shard_map(
        local,
        mesh=mesh,
        in_specs=(P("gz", None, "gy"), P(None, None, "gz", "gy"), P(), P(), P()),
        out_specs=P("gz", None, "gy"),
        check_vma=False,
    )
```

profile of v0, /device:TPU:0, one launch (start us, length us, event | category | flops | bytes accessed | tf_op | source)
XLA Modules:
  0.0 368.0 jit_solution(6625780845463033477)
XLA Ops:
  0.0 0.0 copy-start
  0.0 6.6 %copy.36 = f32[16,512,128]{2,0,1:T(8,128)} copy(f32[16,512,128]{2,1,0:T(8,128)} %param.5) | data formatting | bytes 8388608 | tf_op args[0]
  6.6 0.0 copy-start.5
  6.6 5.5 %all-to-all-start = ((f32[16,512,128]{2,0,1:T(8,128)}), f32[16,512,128]{2,0,1:T(8,128)}, u32[]{:S(2)}, u32[]{:S(2)}) async-start(f32[16,512,128]{2,0,1:T(8,128)} %copy.36), calls=%async_computation | async-start | bytes 8388608 | tf_op jit(solution)/shard_map/all_to_all | solution.py:64
  12.1 0.8 convert_bitcast_fusion
  12.9 0.1 broadcast_in_dim.8
  13.0 0.1 broadcast_in_dim.18
  13.1 0.0 copy-done
  13.1 0.2 dynamic-slice_reduce_fusion
  13.3 0.1 iota_compare_fusion.4
  13.4 0.0 copy-done.5
  13.4 0.1 fusion.39
  13.6 1.2 fusion.36
  14.8 0.1 copy.39
  14.9 0.4 fusion.47
  15.3 20.2 %fusion = f32[128,64,128,1]{2,0,3,1:T(8,128)} fusion(f32[4,128,64,128]{3,2,1,0:T(8,128)} %param.6, f32[4,128,128]{1,2,0:T(8,128)S(1)} %copy.39), kind=kOutput, calls=%fused_computation | convolution fusion | flops 6442450944 | bytes 21233664 | tf_op jit(solution)/shard_map/vbzw,vzbxy->wbxy/dot_general | solution.py:70
  35.5 25.8 %all-to-all-done = f32[16,512,128]{2,0,1:T(8,128)} async-done(((f32[16,512,128]{2,0,1:T(8,128)}), f32[16,512,128]{2,0,1:T(8,128)}, u32[]{:S(2)}, u32[]{:S(2)}) %all-to-all-start) | async-done | bytes 4194336 | tf_op jit(solution)/shard_map/all_to_all | solution.py:64
  61.3 0.0 copy-start.3
  61.3 2.9 copy.37
  64.3 0.0 copy-start.2
  64.3 0.5 copy-done.3
  64.8 3.8 %bitcast_subtract_fusion = f32[128,64,128]{2,0,1:T(8,128)S(1)} fusion(f32[128,64,128,1]{2,0,3,1:T(8,128)S(1)} %copy-done.3, f32[128,128,1]{1,0,2:T(8,128)S(1)} %fusion.47, f32[128,64,128]{2,0,1:T(8,128)S(1)} %bitcast.281), kind=kOutput, calls=%fused_computation.35 | convolution fusion | flops 1611661312 | bytes 12648448 | tf_op jit(solution)/shard_map/bwz,zbxy->wbxy/dot_general | solution.py:75
  68.5 0.0 copy-done.2
  68.5 0.0 copy-start.4
  68.5 7.4 %multiply_reduce_fusion.6 = (f32[]{:T(128)}, f32[]{:T(128)}, f32[]{:T(128)}, f32[64,128,128]{1,2,0:T(8,128)}) fusion(f32[128,64,128]{2,0,1:T(8,128)S(1)} %bitcast_subtract_fusion, f32[128]{0:T(128)S(1)} %broadcast_in_dim.18, f32[128,128,1]{1,0,2:T(8,128)S(1)} %fusion.47), kind=kOutput, calls=%fused_computation.50 | convolution fusion | flops 1621098496 | bytes 8454668 | tf_op jit(solution)/shard_map/bwz,zbxy->wbxy/dot_general | solution.py:75
  76.0 0.0 copy-done.4
  76.0 40.4 %all-reduce.2 = (f32[]{:T(128)}, f32[]{:T(128)}, f32[]{:T(128)}) all-reduce(f32[]{:T(128)} %get-tuple-element.13, f32[]{:T(128)} %get-tuple-element.12, f32[]{:T(128)} %get-tuple-element.11), channel_id=1, replica_groups=mesh['gz'=8,'gy'=4] {'gz','gy'}, use_global_device_ids=true, to_apply=%region_1.0 | all-reduce | flops 3 | bytes 24 | tf_op jit(solution)/shard_map/psum | solution.py:36
  120.1 14.4 %multiply_reduce_fusion.3 = (f32[]{:T(128)}, f32[]{:T(128)}, f32[]{:T(128)}, f32[64,128,128]{1,2,0:T(8,128)}) fusion(f32[128]{0:T(128)S(1)} %broadcast_in_dim.18, f32[]{:T(128)S(6)} %div.22, f32[64,128,128]{1,2,0:T(8,128)} %get-tuple-element.23, f32[]{:T(128)S(6)} %div.21, f32[128,64,128]{2,0,1:T(8,128)} %copy-done.4, f32[128,128,1]{1,0,2:T(8,128)S(1)} %fusion.47), kind=kOutput, calls=%fused_computation.45 | convolution fusion | flops 1633681408 | bytes 12648980 | tf_op jit(solution)/shard_map/bwz,zbxy->wbxy/dot_general | solution.py:75
  134.6 40.7 %all-reduce.1 = (f32[]{:T(128)}, f32[]{:T(128)}, f32[]{:T(128)}) all-reduce(f32[]{:T(128)} %get-tuple-element.10, f32[]{:T(128)} %get-tuple-element.9, f32[]{:T(128)} %get-tuple-element.8), channel_id=1, replica_groups=mesh['gz'=8,'gy'=4] {'gz','gy'}, use_global_device_ids=true, to_apply=%region_7.0 | all-reduce | flops 3 | bytes 24 | tf_op jit(solution)/shard_map/psum | solution.py:39
  177.3 18.9 %multiply_reduce_fusion = (f32[]{:T(128)}, f32[]{:T(128)}, f32[]{:T(128)}, f32[64,128,128]{1,2,0:T(8,128)}) fusion(f32[128]{0:T(128)S(1)} %broadcast_in_dim.18, f32[]{:T(128)S(6)} %div.24, f32[]{:T(128)S(6)} %div.22, f32[64,128,128]{1,2,0:T(8,128)} %get-tuple-element.23, f32[]{:T(128)S(6)} %div.21, f32[128,64,128]{2,0,1:T(8,128)} %copy-done.4, ...), kind=kOutput, calls=%fused_computation.39 | convolution fusion | flops 1646264320 | bytes 16843292 | tf_op jit(solution)/shard_map/bwz,zbxy->wbxy/dot_general | solution.py:75
  196.2 40.6 %all-reduce = (f32[]{:T(128)}, f32[]{:T(128)}, f32[]{:T(128)}) all-reduce(f32[]{:T(128)} %get-tuple-element.7, f32[]{:T(128)} %get-tuple-element.6, f32[]{:T(128)} %get-tuple-element.5), channel_id=1, replica_groups=mesh['gz'=8,'gy'=4] {'gz','gy'}, use_global_device_ids=true, to_apply=%region_13.0 | all-reduce | flops 3 | bytes 24 | tf_op jit(solution)/shard_map/psum | solution.py:39
  238.8 20.4 %fusion.2 = f32[]{:T(128)} fusion(f32[128]{0:T(128)S(1)} %broadcast_in_dim.18, f32[128,128,1]{1,0,2:T(8,128)S(1)} %fusion.47, f32[64,128,128]{1,2,0:T(8,128)} %get-tuple-element.25, f32[]{:T(128)S(6)} %div.26, f32[]{:T(128)S(6)} %div.25, f32[]{:T(128)S(6)} %div.24, f32[64,128,128]{1,2,0:T(8,128)} %get-tuple-element.24, ...), kind=kOutput, calls=%fused_computation.3 | convolution fusion | flops 1654652928 | bytes 16843292 | tf_op jit(solution)/shard_map/bwz,zbxy->wbxy/dot_general | solution.py:75
  259.1 40.6 %psum.82 = f32[]{:T(128)} all-reduce(f32[]{:T(128)} %fusion.2), channel_id=1, replica_groups=mesh['gz'=8,'gy'=4] {'gz','gy'}, use_global_device_ids=true, to_apply=%region_19.0 | all-reduce | flops 1 | bytes 8 | tf_op jit(solution)/shard_map/psum | solution.py:39
  300.3 8.9 %multiply_add_fusion = f32[128,64,128]{2,0,1:T(8,128)S(1)} fusion(f32[128,64,128]{2,0,1:T(8,128)} %copy-done.4, f32[]{:T(128)S(6)} %div.27, f32[]{:T(128)S(6)} %div.25, f32[]{:T(128)S(6)} %div.23, f32[]{:T(128)S(6)} %div.21, f32[128]{0:T(128)S(1)} %broadcast_in_dim.18, f32[]{:T(128)S(6)} %div.26, f32[]{:T(128)S(6)} %div.24, ...), kind=kLoop, calls=%fused_computation.36 | loop fusion | flops 28311552 | bytes 25166364 | tf_op jit(solution)/shard_map/add | solution.py:49
  309.2 2.4 copy.51
  311.7 53.6 %all_to_all.36 = f32[128,64,128]{2,1,0:T(8,128)S(1)} all-to-all(f32[128,64,128]{2,1,0:T(8,128)S(1)} %copy.51), channel_id=1, replica_groups=mesh['gz'=8,'gy'=4] {'gz'}, dimensions={0} | all-to-all | bytes 8388608 | tf_op jit(solution)/shard_map/all_to_all | solution.py:85
  365.2 0.0 copy-start.1
  365.2 2.3 copy.52
  367.6 0.0 copy-done.1
  (2 shorter events, 0.0 us)
Async XLA Ops:
  0.0 13.1 %copy-start = (s32[4,8,8]{2,1,0:T(8,128)S(1)}, s32[4,8,8]{2,1,0:T(8,128)}, u32[]{:S(2)}) copy-start(s32[4,8,8]{2,1,0:T(8,128)} %param.8) | copy-start | bytes 3076
  6.6 6.8 %copy-start.5 = (f32[16,31]{1,0:T(8,128)S(1)}, f32[16,31]{1,0:T(8,128)}, u32[]{:S(2)}) copy-start(f32[16,31]{1,0:T(8,128)} %param.9) | copy-start | bytes 5956
  6.6 54.7 %all-to-all-start = ((f32[16,512,128]{2,0,1:T(8,128)}), f32[16,512,128]{2,0,1:T(8,128)}, u32[]{:S(2)}, u32[]{:S(2)}) async-start(f32[16,512,128]{2,0,1:T(8,128)} %copy.36), calls=%async_computation | async-start | bytes 8388608 | tf_op jit(solution)/shard_map/all_to_all | solution.py:64
  61.3 3.4 copy-start.3
  64.3 4.3 %copy-start.2 = (f32[16,8,64,128]{3,0,1,2:T(8,128)}, f32[16,8,64,128]{3,0,1,2:T(8,128)S(1)}, u32[]{:S(2)}) copy-start(f32[16,8,64,128]{3,0,1,2:T(8,128)S(1)} %copy.37) | copy-start | bytes 12582916
  68.5 7.4 %copy-start.4 = (f32[128,64,128]{2,0,1:T(8,128)}, f32[128,64,128]{2,0,1:T(8,128)S(1)}, u32[]{:S(2)}) copy-start(f32[128,64,128]{2,0,1:T(8,128)S(1)} %bitcast_subtract_fusion) | copy-start | bytes 12582916
  365.2 2.3 copy-start.1
where the time goes:
time: 372 us; the launch traced here: 368 us
  blocking collectives  216 us (58%)
  matrix products  86.8 us (23%)
  waiting for transfers between devices  25.8 us (7%)
  local copies, waits for them, and re-layouts  15.3 us (4%)
  other arithmetic  9.76 us (3%)
  between operations  8.86 us (2%)
  starting transfers between devices  5.53 us (1%)
    psum x3, blocking collectives, conjugate(): lax.psum((jnp.sum(direction * image_field), jnp.sum(residual * image_fiel...  122 us
    dot_general x5, matrix products, apply_gram(): jnp.einsum('bwz,zbxy->wbxy', gram_mats, field.reshape(NZ, bands_here, BX,...  64.9 us
    all_to_all x1, blocking collectives, local(): return lax.all_to_all(solved, 'gz', split_axis=0, concat_axis=1, tiled=True)  53.6 us
    psum x1, blocking collectives, conjugate(): norm_now = lax.psum(jnp.sum(residual * residual), ('gz', 'gy'))  40.4 us
    all_to_all x1, waiting for transfers between devices, local(): lax.all_to_all(init, 'gz', split_axis=1, concat_axis=0, tiled=True)  25.8 us
    dot_general x1, matrix products, local(): jnp.einsum('vbzw,vzbxy->wbxy', blur_mats, view_data, precision=HIGHEST)  20.2 us
    add x1, other arithmetic, conjugate(): solved = solved + step_size * direction  8.91 us
  transfers between devices with their start and end apart: 1, of which 1 were waited for; matrix products, arithmetic and copies ran while one was open for 6% of the time, Pallas kernels for 0%

commit v1 on v0

v1 whole, which is shorter than its diff:
```python
import functools

import jax
import jax.numpy as jnp
from jax import lax
from jax.experimental import pallas as pl
from jax.experimental.pallas import tpu as pltpu
from jax.sharding import PartitionSpec as P

ITERS = 4
MOMENTS = 2 * ITERS

HIGHEST = lax.Precision.HIGHEST
damping = 1.0
MIB = 1 << 20


def blur_tables(kernel_index, kernels, depth):
    bank, taps = kernels.shape
    width = depth // kernel_index.shape[1]
    onehot = (kernel_index[..., None] == jnp.arange(bank, dtype=jnp.int32)).astype(jnp.float32)
    tap_values = jnp.einsum("vabk,kt->vabt", onehot, kernels, precision=HIGHEST)
    row_taps = jnp.repeat(tap_values, width, axis=1)
    depths = jnp.arange(depth, dtype=jnp.int32)
    offset = depths[None, :] - depths[:, None] + taps // 2
    tap_select = (offset[:, :, None] == jnp.arange(taps, dtype=jnp.int32)).astype(jnp.float32)
    return jnp.einsum("vzbt,zwt->vbzw", row_taps, tap_select, precision=HIGHEST)


def split(x):
    high = x.astype(jnp.bfloat16)
    return high, (x - high.astype(jnp.float32)).astype(jnp.bfloat16)


def left_operand(matrix):
    high, low = split(matrix)
    return jnp.concatenate(
        [jnp.concatenate([high, high], axis=1), jnp.concatenate([low, low], axis=1)], axis=0
    )


def right_operand(matrix):
    return jnp.concatenate(split(matrix), axis=0)


def product(left, right):
    both = jnp.dot(left, right, preferred_element_type=jnp.float32)
    rows = both.shape[0] // 2
    return both[:rows] + both[rows:]


def tissue_half(mask_ref, tile):
    return mask_ref[tile, 2 * lax.axis_index("gy") + 1]


def tissue_lanes(shape, half):
    lane = lax.broadcasted_iota(jnp.int32, shape, len(shape) - 1)
    return (lane >= shape[-1] // 2) == (half == 1)


def pack_kernel(mask_ref, init_ref, *refs):
    count = len(refs) - 2
    out_refs, staged, sems = refs[:count], refs[count], refs[count + 1]
    slab, columns, lanes = out_refs[0].shape
    width = 2 * columns
    me = lax.axis_index("gz")

    def copy(k):
        tile = jnp.bitwise_xor(me, k)
        start = pl.multiple_of(tile * width, width)
        return pltpu.make_async_copy(
            init_ref.at[:, pl.ds(start, width), :], staged.at[k], sems.at[k]
        )

    for k in range(count):
        copy(k).start()
    for k in range(count):
        copy(k).wait()
        half = tissue_half(mask_ref, jnp.bitwise_xor(me, k))
        here = tissue_lanes((slab, columns, lanes), half)
        first = staged[k, :, :columns, :]
        second = pltpu.roll(staged[k, :, columns:, :], lanes // 2, 2)
        out_refs[k][...] = jnp.where(here, first, second)


def project_kernel(mask_ref, blur_ref, first_ref, second_ref, out_ref, left_ref):
    views, depth, columns, lanes = first_ref.shape

    @pl.when(pl.program_id(0) == 0)
    def _():
        for v in range(views):
            left_ref[:, 2 * depth * v : 2 * depth * (v + 1)] = left_operand(blur_ref[v].T)

    half = tissue_half(mask_ref, lax.axis_index("gz"))
    here = tissue_lanes((depth, lanes), half)
    rows = views * depth * columns
    first = first_ref.reshape(rows, lanes)
    second = second_ref.reshape(rows, lanes)

    def packed(v, x):
        at = pl.ds(v * depth * columns + x, depth, stride=columns)
        return jnp.where(here, first[at, :], pltpu.roll(second[at, :], lanes // 2, 1))

    for x in range(0, columns, 2):
        parts = []
        for v in range(views):
            parts.append(right_operand(jnp.concatenate([packed(v, x), packed(v, x + 1)], axis=1)))
        result = product(left_ref[...], jnp.concatenate(parts, axis=0))
        out_ref[x] = result[:, :lanes]
        out_ref[x + 1] = result[:, lanes:]


def residual_kernel(gram_ref, poly_ref, projected_ref, *refs):
    count = len(refs) - 4
    chunks, residual_ref, moments_ref, left_ref, square_ref = (
        refs[:count],
        refs[count],
        refs[count + 1],
        refs[count + 2],
        refs[count + 3],
    )
    slab, columns, lanes = chunks[0].shape
    left_ref[...] = left_operand(gram_ref[...])
    square_ref[...] = jnp.zeros_like(square_ref)
    flat = [chunk.reshape(slab * columns, lanes) for chunk in chunks]

    def field(x):
        return jnp.concatenate([ref[pl.ds(x, slab, stride=columns), :] for ref in flat], axis=0)

    @pl.loop(0, columns // 2)
    def _(pair):
        x = 2 * pair
        image = product(
            left_ref[...], right_operand(jnp.concatenate([field(x), field(x + 1)], axis=1))
        )
        start = jnp.concatenate([projected_ref[x], projected_ref[x + 1]], axis=1)
        both = right_operand(start - image)
        residual_ref[pair] = both
        square_ref[...] += lax.dot_general(
            both, both, (((1,), (1,)), ((), ())), preferred_element_type=jnp.float32
        )

    depth = gram_ref.shape[0]
    square = square_ref[...]
    square = (square[:depth, :depth] + square[depth:, depth:]) + (
        square[:depth, depth:] + square[depth:, :depth]
    )
    lane = lax.broadcasted_iota(jnp.int32, (1, lanes), 1)
    row = jnp.zeros((1, lanes), jnp.float32)
    for k in range(poly_ref.shape[0]):
        total = jnp.sum(jnp.sum(square * poly_ref[k], axis=0, keepdims=True), axis=1, keepdims=True)
        row = jnp.where(lane == k, total, row)
    moments_ref[...] = jnp.broadcast_to(row, moments_ref.shape)


def conjugate(moments, centre, radius):
    def inner(p, q):
        total = None
        for i, a in enumerate(p):
            for j, b in enumerate(q):
                term = a * b * (0.5 * (moments[i + j] + moments[abs(i - j)]))
                total = term if total is None else total + term
        return total

    def operate(p):
        image = [centre * a for a in p] + [None]

        def put(i, value):
            image[i] = value if image[i] is None else image[i] + value

        for j, a in enumerate(p):
            if j == 0:
                put(1, radius * a)
            else:
                put(j + 1, 0.5 * radius * a)
                put(j - 1, 0.5 * radius * a)
        return image

    one = jnp.ones_like(moments[0])
    residual, direction = [one], [one]
    solved = []
    norm_now = moments[0]
    for iteration in range(ITERS):
        image = operate(direction)
        step_size = norm_now / inner(direction, image)
        solved = [s + step_size * d for s, d in zip(solved, direction)] + [
            step_size * d for d in direction[len(solved) :]
        ]
        if iteration == ITERS - 1:
            break
        residual = [r - step_size * i for r, i in zip(residual, image)] + [
            -step_size * i for i in image[len(residual) :]
        ]
        norm_next = inner(residual, residual)
        ratio = norm_next / norm_now
        direction = [r + ratio * d for r, d in zip(residual, direction)] + residual[len(direction) :]
        norm_now = norm_next
    return solved


def correct_kernel(top_ref, moments_ref, poly_ref, residual_ref, *refs):
    count = len(refs) - 1
    out_refs, left_ref = refs[:count], refs[count]
    slab, columns, lanes = out_refs[0].shape
    row = jnp.sum(moments_ref[...], axis=0, keepdims=True)
    lane = lax.broadcasted_iota(jnp.int32, row.shape, 1)
    moments = [
        jnp.sum(jnp.where(lane == k, row, 0.0), axis=1, keepdims=True) for k in range(MOMENTS)
    ]
    radius = 0.5 * top_ref[...]
    coefficients = conjugate(moments, damping + radius, radius)
    matrix = coefficients[0] * poly_ref[0]
    for k in range(1, ITERS):
        matrix = matrix + coefficients[k] * poly_ref[k]
    left_ref[...] = left_operand(matrix)
    flat = [ref.reshape(slab * columns, lanes) for ref in out_refs]

    @pl.loop(0, columns // 2)
    def _(pair):
        result = product(left_ref[...], residual_ref[pair])
        for k in range(count):
            rows = result[slab * k : slab * (k + 1)]
            for side in range(2):
                flat[k][pl.ds(2 * pair + side, slab, stride=columns), :] = rows[
                    :, lanes * side : lanes * (side + 1)
                ]


def unpack_kernel(group, aliased, mask_ref, init_ref, *refs):
    if aliased:
        refs = refs[1:]
    chunks, (out_ref, staged, in_sems, out_sems) = refs[:-4], refs[-4:]
    slab, columns, lanes = chunks[0].shape
    width = 2 * columns
    me = lax.axis_index("gz")

    def tile(k):
        return jnp.bitwise_xor(me, k)

    def columns_of(ref, k):
        return ref.at[:, pl.ds(pl.multiple_of(tile(k) * width, width), width), :]

    loads = [
        pltpu.make_async_copy(columns_of(init_ref, k), staged.at[n], in_sems.at[n])
        for n, k in enumerate(group)
    ]
    stores = [
        pltpu.make_async_copy(staged.at[n], columns_of(out_ref, k), out_sems.at[n])
        for n, k in enumerate(group)
    ]
    for load in loads:
        load.start()
    for n, k in enumerate(group):
        here = tissue_lanes((slab, columns, lanes), tissue_half(mask_ref, tile(k)))
        change = chunks[n][...]
        loads[n].wait()
        staged[n, :, :columns, :] += jnp.where(here, change, 0.0)
        staged[n, :, columns:, :] += pltpu.roll(jnp.where(here, 0.0, change), lanes // 2, 2)
        stores[n].start()
    for store in stores:
        store.wait()


SMEM = pl.BlockSpec(memory_space=pltpu.SMEM)
VMEM = pl.BlockSpec(memory_space=pltpu.VMEM)
ANY = pl.BlockSpec(memory_space=pl.ANY)


def local(init, measured, mask, kernel_index, kernels):
    tiles, rows = lax.axis_size("gz"), lax.axis_size("gy")
    slab, _, lanes = init.shape
    views, depth, width, _ = measured.shape
    columns = width // 2
    me = lax.axis_index("gz")
    f32 = jnp.float32
    chunk = jax.ShapeDtypeStruct((slab, columns, lanes), f32)

    def exchange(chunks):
        return [chunks[0]] + [
            lax.ppermute(chunks[k], "gz", [(j, j ^ k) for j in range(tiles)])
            for k in range(1, tiles)
        ]

    packed = pl.pallas_call(
        pack_kernel,
        name="pack_blocks",
        out_shape=[chunk] * tiles,
        in_specs=[SMEM, ANY],
        out_specs=[VMEM] * tiles,
        scratch_shapes=[
            pltpu.VMEM((tiles, slab, width, lanes), f32),
            pltpu.SemaphoreType.DMA((tiles,)),
        ],
        compiler_params=pltpu.CompilerParams(vmem_limit_bytes=32 * MIB),
        cost_estimate=pl.CostEstimate(
            flops=init.size, bytes_accessed=6 * init.size, transcendentals=0
        ),
    )(mask, init)
    fields = exchange(packed)

    blurs = blur_tables(kernel_index, kernels, depth)
    row_sums = jnp.sum(blurs, axis=3)
    top = jnp.max(jnp.sum(blurs * row_sums[..., None], axis=(0, 2)))
    blur = lax.dynamic_index_in_dim(blurs, me, 1, False)
    gram = jnp.einsum("vzw,vzu->wu", blur, blur, precision=HIGHEST)

    step = 8
    projected = pl.pallas_call(
        project_kernel,
        name="project_views",
        grid=(columns // step,),
        out_shape=jax.ShapeDtypeStruct((columns, depth, lanes), f32),
        in_specs=[
            SMEM,
            pl.BlockSpec((views, depth, depth), lambda i: (0, 0, 0)),
            pl.BlockSpec((views, depth, step, lanes), lambda i: (0, 0, i, 0)),
            pl.BlockSpec((views, depth, step, lanes), lambda i: (0, 0, i + columns // step, 0)),
        ],
        out_specs=pl.BlockSpec((step, depth, lanes), lambda i: (i, 0, 0)),
        scratch_shapes=[pltpu.VMEM((2 * depth, 2 * views * depth), jnp.bfloat16)],
        compiler_params=pltpu.CompilerParams(vmem_limit_bytes=32 * MIB),
        cost_estimate=pl.CostEstimate(
            flops=8 * views * depth * depth * columns * lanes,
            bytes_accessed=4 * measured.size,
            transcendentals=0,
        ),
    )(mask, blur, measured, measured)

    eye = jnp.eye(depth, dtype=f32)
    poly = [eye, gram * (2.0 / top) - eye]
    for k in range(2, MOMENTS):
        half = k // 2
        other = k - half
        poly.append(
            2.0 * jnp.dot(poly[other], poly[half], precision=HIGHEST) - poly[other - half]
        )
    depths = jnp.arange(depth, dtype=jnp.int32)
    source = jnp.bitwise_xor(me, depths // slab) * slab + depths % slab
    order = (source[:, None] == depths[None, :]).astype(f32)
    gram_in = jnp.dot(gram, order.T, precision=HIGHEST)
    poly_out = jnp.stack(
        [jnp.dot(order, poly[k], precision=HIGHEST) for k in range(ITERS)]
    )
    poly = jnp.stack(poly)

    everyone = tiles * rows
    pairs = columns // 2
    residual, moments = pl.pallas_call(
        residual_kernel,
        name="first_residual",
        out_shape=[
            jax.ShapeDtypeStruct((pairs, 2 * depth, 2 * lanes), jnp.bfloat16),
            jax.ShapeDtypeStruct((everyone, lanes), f32),
        ],
        in_specs=[VMEM] * (3 + tiles),
        out_specs=[VMEM] * 2,
        scratch_shapes=[
            pltpu.VMEM((2 * depth, 2 * depth), jnp.bfloat16),
            pltpu.VMEM((2 * depth, 2 * depth), f32),
        ],
        compiler_params=pltpu.CompilerParams(vmem_limit_bytes=32 * MIB),
        cost_estimate=pl.CostEstimate(
            flops=16 * depth * depth * columns * lanes,
            bytes_accessed=12 * depth * columns * lanes,
            transcendentals=0,
        ),
    )(gram_in, poly, projected, *fields)

    moments = lax.all_to_all(moments, ("gz", "gy"), split_axis=0, concat_axis=0, tiled=True)

    changes = pl.pallas_call(
        correct_kernel,
        name="correction",
        out_shape=[chunk] * tiles,
        in_specs=[VMEM] * 4,
        out_specs=[VMEM] * tiles,
        scratch_shapes=[pltpu.VMEM((2 * depth, 2 * depth), jnp.bfloat16)],
        compiler_params=pltpu.CompilerParams(vmem_limit_bytes=32 * MIB),
        cost_estimate=pl.CostEstimate(
            flops=8 * depth * depth * columns * lanes,
            bytes_accessed=8 * depth * columns * lanes,
            transcendentals=0,
        ),
    )(top.reshape(1, 1), moments, poly_out, residual)
    changes = exchange(changes)

    solved = None
    group_size = max(1, tiles // 4)
    for first in range(0, tiles, group_size):
        group = list(range(first, first + group_size))
        solved = pl.pallas_call(
            functools.partial(unpack_kernel, group, solved is not None),
            name="add_correction",
            out_shape=jax.ShapeDtypeStruct(init.shape, f32),
            in_specs=[SMEM, ANY] + [ANY] * (solved is not None) + [VMEM] * group_size,
            out_specs=ANY,
            input_output_aliases={} if solved is None else {2: 0},
            scratch_shapes=[
                pltpu.VMEM((group_size, slab, width, lanes), f32),
                pltpu.SemaphoreType.DMA((group_size,)),
                pltpu.SemaphoreType.DMA((group_size,)),
            ],
            compiler_params=pltpu.CompilerParams(vmem_limit_bytes=32 * MIB),
            cost_estimate=pl.CostEstimate(
                flops=init.size, bytes_accessed=10 * init.size // 4, transcendentals=0
            ),
        )(mask, init, *([] if solved is None else [solved]), *[changes[k] for k in group])
    return solved


def solution(mesh):
    return jax.shard_map(
        local,
        mesh=mesh,
        in_specs=(P("gz", None, "gy"), P(None, None, "gz", "gy"), P(), P(), P()),
        out_specs=P("gz", None, "gy"),
        check_vma=False,
    )
```

time: 372 us -> 115 us (0.31)
  blocking collectives: 216 us -> 0 us
  matrix products: 86.8 us -> 8.54 us
  Pallas kernels: 0 us -> 31 us
  starting transfers between devices: 5.53 us -> 18 us
  between operations: 8.86 us -> 0.95 us
  waiting for transfers between devices: 25.8 us -> 31.6 us
  other arithmetic: 9.76 us -> 4.43 us
  local copies, waits for them, and re-layouts: 15.3 us -> 19.6 us
    psum x4 -> x0, blocking collectives: 162 us -> none  [the longest x3 122 us: conjugate(): lax.psum((jnp.sum(direction * image_field), jnp.sum(residual * image_fiel...]
    dot_general x7 -> x12, matrix products: 85.5 us -> 5.28 us  [the longest x4 2.14 us: local(): jnp.dot(order, poly[k], precision=HIGHEST)]
    all_to_all x1 -> x0, blocking collectives: 53.6 us -> none  [local(): return lax.all_to_all(solved, 'gz', split_axis=0, concat_axis=1, tiled=True)]
    pallas_call x0 -> x8, Pallas kernels: none -> 31 us  [the longest x1 8.55 us: local(): pl.pallas_call(residual_kernel, name='first_residual', out_shape=[jax.Sha...]
    ppermute x0 -> x14, waiting for transfers between devices: none -> 25.4 us  [exchange(): lax.ppermute(chunks[k], 'gz', [(j, j ^ k) for j in range(tiles)])]
    all_to_all x1, waiting for transfers between devices: 25.8 us -> 6.2 us  [local(): lax.all_to_all(moments, ('gz', 'gy'), split_axis=0, concat_axis=0, tiled=...]
    ppermute x0 -> x14, starting transfers between devices: none -> 11.9 us  [exchange(): lax.ppermute(chunks[k], 'gz', [(j, j ^ k) for j in range(tiles)])]
    unnamed x13 -> x27, local copies, waits for them, and re-layouts: 7.12 us -> 16.8 us
  transfers between devices with their start and end apart: 1 -> 15, of which waited for: 1 -> 6; matrix products, arithmetic and copies ran while one was open for 6% -> 15% of each run, Pallas kernels for 0% -> 11%
where the time goes in v1:
time: 115 us; the launch traced here: 114 us
  waiting for transfers between devices  31.6 us (27%)
  Pallas kernels  31 us (27%)
  local copies, waits for them, and re-layouts  19.6 us (17%)
  starting transfers between devices  18 us (16%)
  matrix products  8.54 us (7%)
  other arithmetic  4.43 us (4%)
    ppermute x14, waiting for transfers between devices, exchange(): lax.ppermute(chunks[k], 'gz', [(j, j ^ k) for j in range(tiles)])  25.4 us
    unnamed x27, local copies, waits for them, and re-layouts  16.8 us
    ppermute x14, starting transfers between devices, exchange(): lax.ppermute(chunks[k], 'gz', [(j, j ^ k) for j in range(tiles)])  11.9 us
    pallas_call x1, Pallas kernels, local(): pl.pallas_call(residual_kernel, name='first_residual', out_shape=[jax.Sha...  8.55 us
    pallas_call x1, Pallas kernels, local(): pl.pallas_call(project_kernel, name='project_views', grid=(columns // ste...  7.5 us
    pallas_call x4, Pallas kernels, local(): pl.pallas_call(functools.partial(unpack_kernel, group, solved is not None...  7.35 us
    all_to_all x1, waiting for transfers between devices, local(): lax.all_to_all(moments, ('gz', 'gy'), split_axis=0, concat_axis=0, tiled=...  6.2 us
    all_to_all x1, starting transfers between devices, local(): lax.all_to_all(moments, ('gz', 'gy'), split_axis=0, concat_axis=0, tiled=...  6.09 us
  transfers between devices with their start and end apart: 15, of which 6 were waited for; matrix products, arithmetic and copies ran while one was open for 15% of the time, Pallas kernels for 11%

profile of v1, /device:TPU:0, one launch (start us, length us, event | category | flops | bytes accessed | tf_op | source)
XLA Modules:
  0.0 114.1 jit_solution(7065543598866815226)
XLA Ops:
  0.0 2.2 %copy-done.1 = f32[16,512,128]{2,1,0:T(8,128)S(1)} copy-done((f32[16,512,128]{2,1,0:T(8,128)S(1)}, f32[16,512,128]{2,1,0:T(8,128)}, u32[]{:S(2)}) %copy-start.1) | copy-done | bytes 4194328
  2.2 0.7 copy-done.10
  2.9 2.8 %pack_blocks.1 = (f32[16,32,128]{2,1,0:T(8,128)S(1)}, f32[16,32,128]{2,1,0:T(8,128)}, f32[16,32,128]{2,1,0:T(8,128)}, f32[16,32,128]{2,1,0:T(8,128)}, f32[16,32,...) custom-call(s32[8,8]{1,0:T(8,128)S(1)} %copy-done.10, ...), custom_call_target="tpu_custom_call" | custom-call | flops 1048576 | bytes 6291456 | tf_op jit(solution)/shard_map/pack_blocks/pallas_call | solution.py:284
  5.7 0.5 collective-permute-start
  6.2 2.6 %collective-permute-start.1 = (f32[16,32,128]{2,1,0:T(8,128)}, f32[16,32,128]{2,1,0:T(8,128)S(1)}, u32[]{:S(2)}, u32[]{:S(2)}) collective-permute-start(f32[16,32,128]{2,1,0:T(8,128)} %get-tuple-element.25), channel_id=1, source_target_pairs={{0,8},{4,12},{8,0},{12,4},{16,24},{20,28},{24,16},{28,20},{1,9},{5... | collective-permute-start | bytes 786440 | tf_op jit(solution)/shard_map/ppermute | solution.py:280
  8.8 0.1 collective-permute-start.2
  8.9 1.8 %collective-permute-start.3 = (f32[16,32,128]{2,1,0:T(8,128)S(1)}, f32[16,32,128]{2,1,0:T(8,128)S(1)}, u32[]{:S(2)}, u32[]{:S(2)}) collective-permute-start(f32[16,32,128]{2,1,0:T(8,128)S(1)} %get-tuple-element.27), channel_id=1, source_target_pairs={{0,16},{4,20},{8,24},{12,28},{16,0},{20,4},{24,8},{28,12},{1,17},{... | collective-permute-start | bytes 786440 | tf_op jit(solution)/shard_map/ppermute | solution.py:280
  10.6 0.0 collective-permute-start.4
  10.7 0.3 fusion.19
  11.0 0.3 broadcast_in_dim.2
  11.2 3.0 %fusion.4 = f32[128,128,4,8]{1,3,2,0:T(8,128)} fusion(f32[4,128,8,31]{3,2,0,1:T(8,128)S(1)} %bitcast.76, s32[128,128]{1,0:T(8,128)S(1)} %subtract_add_fusion), kind=kOutput, calls=%fused_computation.7 | convolution fusion | flops 195543040 | bytes 2670592 | tf_op jit(solution)/shard_map/vzbt,zwt->vbzw/dot_general | solution.py:27
  14.2 2.8 %fusion.2 = f32[8,128]{1,0:T(8,128)S(1)} fusion(f32[128,128,4,8]{1,3,2,0:T(8,128)} %fusion.4), kind=kOutput, calls=%fused_computation.4 | output fusion | flops 1051775 | bytes 2101248 | tf_op jit(solution)/shard_map/mul | solution.py:303
  17.1 2.5 %constant_dynamic-slice_fusion = f32[128,128,4,1]{1,3,2,0:T(1,128)} fusion(f32[128,128,4,8]{1,3,2,0:T(8,128)} %fusion.4, s32[]{:T(128)S(6)} %select_n.24), kind=kLoop, calls=%fused_computation.62 | loop fusion | bytes 524292 | tf_op jit(solution)/shard_map/dynamic-slice
  19.7 1.0 copy.31
  20.6 0.7 reduce_max.9
  21.9 1.6 %bitcast_dynamic-update-slice_fusion.3 = (f32[8,128,128]{2,1,0:T(8,128)S(1)}, f32[128,128]{1,0:T(8,128)S(1)}) fusion(f32[8,128,128]{2,1,0:T(8,128)S(1)} %convert_dynamic-update-slice_fusion, f32[]{:T(128)S(6)} %div.13, f32[128,128,4,1]{1,3,2,0:T(1,128)} %constant_dynamic-slice_fusion), kind=kOutput, calls=%fused_computation.41 | convolution fusion | flops 100728832 | bytes 393220 | tf_op jit(solution)/shard_map/vzw,vzu->wu/dot_general | solution.py:305
  23.6 0.2 convolution_bitcast_fusion.2
  23.8 0.3 fusion.21.gram_ref
  24.1 0.2 bitcast_dynamic-update-slice_fusion.2
  24.3 0.2 convolution_bitcast_fusion.1
  24.6 0.2 bitcast_dynamic-update-slice_fusion.1
  24.8 0.2 bitcast_dynamic-update-slice_fusion
  25.0 0.2 fusion.14
  25.2 0.0 copy-start.3
  25.2 5.8 %copy-done.3 = f32[4,128,64,128]{3,2,1,0:T(8,128)S(1)} copy-done((f32[4,128,64,128]{3,2,1,0:T(8,128)S(1)}, f32[4,128,64,128]{3,2,1,0:T(8,128)}, u32[]{:S(2)}) %copy-start.3) | copy-done | bytes 16777240
  31.0 7.5 %project_views.1.projected_ref = f32[32,128,128]{2,1,0:T(8,128)S(1)} custom-call(s32[8,8]{1,0:T(8,128)S(1)} %copy-done.11, f32[4,128,128]{2,1,0:T(8,128)S(1)} %bitcast.74, f32[4,128,64,128]{3,2,1,0:T(8,128)S(1)} %copy-done.3, f32[4,128,64,128]{3,2,1,0:T(8,128)S(1)} %copy-done.3), custom_call_target="tpu_custom_call" | custom-call | flops 2147483648 | bytes 16777216 | tf_op jit(solution)/shard_map/project_views/pallas_call | solution.py:308
  38.5 0.8 convolution_bitcast_fusion
  39.3 0.2 fusion.11
  39.6 0.0 collective-permute-done.refs_1_
  39.6 2.7 %collective-permute-start.5 = (f32[16,32,128]{2,1,0:T(8,128)S(1)}, f32[16,32,128]{2,1,0:T(8,128)S(1)}, u32[]{:S(2)}, u32[]{:S(2)}) collective-permute-start(f32[16,32,128]{2,1,0:T(8,128)S(1)} %get-tuple-element.29), channel_id=1, source_target_pairs={{0,24},{4,28},{8,16},{12,20},{16,8},{20,12},{24,0},{28,4},{1,25},{... | collective-permute-start | bytes 786440 | tf_op jit(solution)/shard_map/ppermute | solution.py:280
  42.2 0.0 collective-permute-done.1.refs_2_
  42.2 0.1 collective-permute-start.6
  42.4 0.8 convolution_bitcast_fusion.3
  43.2 0.2 fusion.8.poly_ref
  43.4 0.0 collective-permute-done.2.refs_3_
  43.4 0.0 copy-start.4
  43.5 0.7 copy-done.4
  44.2 0.7 copy-done.6
  44.9 0.7 copy-done.8
  45.6 4.1 %collective-permute-done.5.refs_6_ = f32[16,32,128]{2,1,0:T(8,128)S(1)} collective-permute-done((f32[16,32,128]{2,1,0:T(8,128)S(1)}, f32[16,32,128]{2,1,0:T(8,128)S(1)}, u32[]{:S(2)}, u32[]{:S(2)}) %collective-permute-start.5) | collective-permute-done | bytes 262176 | tf_op jit(solution)/shard_map/ppermute | solution.py:280
  49.7 4.6 %collective-permute-done.6.refs_7_ = f32[16,32,128]{2,1,0:T(8,128)S(1)} collective-permute-done((f32[16,32,128]{2,1,0:T(8,128)S(1)}, f32[16,32,128]{2,1,0:T(8,128)S(1)}, u32[]{:S(2)}, u32[]{:S(2)}) %collective-permute-start.6) | collective-permute-done | bytes 262176 | tf_op jit(solution)/shard_map/ppermute | solution.py:280
  54.3 0.9 copy-done.5
  55.2 0.9 copy-done.7
  56.2 0.9 copy-done.9
  57.1 8.6 %first_residual.1 = (bf16[16,256,256]{2,1,0:T(8,128)(2,1)S(1)}, f32[32,128]{1,0:T(8,128)}) custom-call(f32[128,128]{1,0:T(8,128)S(1)} %fusion.21.gram_ref, f32[8,128,128]{2,1,0:T(8,128)S(1)} %fusion.8.poly_ref, f32[32,128,128]{2,1,0:T(8,128)S(1)} %project_views.1.projected_ref, f32[16,32,128]{2,1,0:T(8,128)S(1)} %get-tuple-element.23.refs_0_, ...), custom_call_target="tpu_custom_call" | custom-call | flops 1073741824 | bytes 6291456 | tf_op jit(solution)/shard_map/first_residual/pallas_call | solution.py:348
  65.7 6.1 %all-to-all-start = ((f32[32,1,128]{2,1,0:T(1,128)}), f32[32,1,128]{2,1,0:T(1,128)S(1)}, u32[]{:S(2)}, u32[]{:S(2)}) async-start(f32[32,1,128]{2,1,0:T(1,128)} %bitcast.18), calls=%async_computation | async-start | bytes 32768 | tf_op jit(solution)/shard_map/all_to_all | solution.py:369
  71.8 0.9 pad_maximum_fusion.poly_ref
  72.7 6.2 %all-to-all-done = f32[32,1,128]{2,1,0:T(1,128)S(1)} async-done(((f32[32,1,128]{2,1,0:T(1,128)}), f32[32,1,128]{2,1,0:T(1,128)S(1)}, u32[]{:S(2)}, u32[]{:S(2)}) %all-to-all-start) | async-done | bytes 16416 | tf_op jit(solution)/shard_map/all_to_all | solution.py:369
  78.9 4.8 %correction.1 = (f32[16,32,128]{2,1,0:T(8,128)S(1)}, f32[16,32,128]{2,1,0:T(8,128)S(1)}, f32[16,32,128]{2,1,0:T(8,128)S(1)}, f32[16,32,128]{2,1,0:T(8,128)S(1)},...) custom-call(f32[1,1]{1,0:T(1,128)} %bitcast.5.top_ref, ...), custom_call_target="tpu_custom_call" | custom-call | flops 536870912 | bytes 4194304 | tf_op jit(solution)/shard_map/correction/pallas_call | solution.py:371
  83.6 0.1 collective-permute-start.7
  83.7 0.6 collective-permute-start.8
  84.4 1.2 %collective-permute-start.9 = (f32[16,32,128]{2,1,0:T(8,128)S(1)}, f32[16,32,128]{2,1,0:T(8,128)S(1)}, u32[]{:S(2)}, u32[]{:S(2)}) collective-permute-start(f32[16,32,128]{2,1,0:T(8,128)S(1)} %get-tuple-element.36), channel_id=1, source_target_pairs={{0,12},{4,8},{8,4},{12,0},{16,28},{20,24},{24,20},{28,16},{1,13},{... | collective-permute-start | bytes 786440 | tf_op jit(solution)/shard_map/ppermute | solution.py:280
  85.6 0.6 collective-permute-start.10
  86.2 1.1 collective-permute-start.11
  87.3 0.5 collective-permute-start.12
  87.8 5.1 %collective-permute-done.8.refs_1_ = f32[16,32,128]{2,1,0:T(8,128)S(1)} collective-permute-done((f32[16,32,128]{2,1,0:T(8,128)S(1)}, f32[16,32,128]{2,1,0:T(8,128)S(1)}, u32[]{:S(2)}, u32[]{:S(2)}) %collective-permute-start.8) | collective-permute-done | bytes 262176 | tf_op jit(solution)/shard_map/ppermute | solution.py:280
  92.9 0.0 collective-permute-start.13
  92.9 2.2 %copy-done.2 = f32[16,512,128]{2,1,0:T(8,128)S(1)} copy-done((f32[16,512,128]{2,1,0:T(8,128)S(1)}, f32[16,512,128]{2,1,0:T(8,128)}, u32[]{:S(2)}) %copy-start.2) | copy-done | bytes 4194328
  95.1 1.8 %add_correction.4.refs_0_ = f32[16,512,128]{2,1,0:T(8,128)} custom-call(s32[8,8]{1,0:T(8,128)S(1)} %copy-done.11, f32[16,512,128]{2,1,0:T(8,128)S(1)} %copy-done.2, f32[16,32,128]{2,1,0:T(8,128)S(1)} %get-tuple-element.33.refs_0_, f32[16,32,128]{2,1,0:T(8,128)S(1)} %collective-permute-done.7.refs_1_), custom_call_target="tpu_custom_call" | custom-call | flops 1048576 | bytes 2621440 | tf_op jit(solution)/shard_map/add_correction/pallas_call | solution.py:391
  96.9 0.7 collective-permute-done.9.refs_2_
  97.6 1.8 %add_correction.5.refs_0_ = f32[16,512,128]{2,1,0:T(8,128)} custom-call(s32[8,8]{1,0:T(8,128)S(1)} %copy-done.11, f32[16,512,128]{2,1,0:T(8,128)S(1)} %copy-done.2, f32[16,512,128]{2,1,0:T(8,128)} %add_correction.4.refs_0_, f32[16,32,128]{2,1,0:T(8,128)S(1)} %collective-permute-done.8.refs_1_, ...), custom_call_target="tpu_custom_call", output_to_operand_aliasing={{}: (2, {})} | custom-call | flops 1048576 | bytes 2621440 | tf_op jit(solution)/shard_map/add_correction/pallas_call | solution.py:391
  99.5 11.0 %collective-permute-done.11.refs_2_ = f32[16,32,128]{2,1,0:T(8,128)S(1)} collective-permute-done((f32[16,32,128]{2,1,0:T(8,128)S(1)}, f32[16,32,128]{2,1,0:T(8,128)S(1)}, u32[]{:S(2)}, u32[]{:S(2)}) %collective-permute-start.11) | collective-permute-done | bytes 262176 | tf_op jit(solution)/shard_map/ppermute | solution.py:280
  110.4 1.8 %add_correction.6.refs_0_ = f32[16,512,128]{2,1,0:T(8,128)} custom-call(s32[8,8]{1,0:T(8,128)S(1)} %copy-done.11, f32[16,512,128]{2,1,0:T(8,128)S(1)} %copy-done.2, f32[16,512,128]{2,1,0:T(8,128)} %add_correction.5.refs_0_, f32[16,32,128]{2,1,0:T(8,128)S(1)} %collective-permute-done.10.refs_1_, ...), custom_call_target="tpu_custom_call", output_to_operand_aliasing={{}: (2, {})} | custom-call | flops 1048576 | bytes 2621440 | tf_op jit(solution)/shard_map/add_correction/pallas_call | solution.py:391
  112.3 1.8 %add_correction.7 = f32[16,512,128]{2,1,0:T(8,128)} custom-call(s32[8,8]{1,0:T(8,128)S(1)} %copy-done.11, f32[16,512,128]{2,1,0:T(8,128)S(1)} %copy-done.2, f32[16,512,128]{2,1,0:T(8,128)} %add_correction.6.refs_0_, f32[16,32,128]{2,1,0:T(8,128)S(1)} %collective-permute-done.12.refs_1_, ...), custom_call_target="tpu_custom_call", output_to_operand_aliasing={{}: (2, {})} | custom-call | flops 1048576 | bytes 2621440 | tf_op jit(solution)/shard_map/add_correction/pallas_call | solution.py:391
  (23 shorter events, 0.1 us)
Async XLA Ops:
  0.0 10.7 %copy-start = (f32[16,31]{1,0:T(8,128)S(1)}, f32[16,31]{1,0:T(8,128)}, u32[]{:S(2)}) copy-start(f32[16,31]{1,0:T(8,128)} %param.9) | copy-start | bytes 5956
  0.0 2.2 %copy-start.1 = (f32[16,512,128]{2,1,0:T(8,128)S(1)}, f32[16,512,128]{2,1,0:T(8,128)}, u32[]{:S(2)}) copy-start(f32[16,512,128]{2,1,0:T(8,128)} %init_ref.9) | copy-start | bytes 12582916
  2.2 0.7 copy-start.10
  2.9 7.8 %copy-start.12 = (s32[4,8,8]{2,1,0:T(8,128)S(1)}, s32[4,8,8]{2,1,0:T(8,128)}, u32[]{:S(2)}) copy-start(s32[4,8,8]{2,1,0:T(8,128)} %param.8) | copy-start | bytes 3076
  5.7 33.8 %collective-permute-start = (f32[16,32,128]{2,1,0:T(8,128)}, f32[16,32,128]{2,1,0:T(8,128)S(1)}, u32[]{:S(2)}, u32[]{:S(2)}) collective-permute-start(f32[16,32,128]{2,1,0:T(8,128)} %get-tuple-element.24), channel_id=1, source_target_pairs={{0,4},{4,0},{8,12},{12,8},{16,20},{20,16},{24,28},{28,24},{1,5},{5... | collective-permute-start | bytes 786440 | tf_op jit(solution)/shard_map/ppermute | solution.py:280
  6.2 36.0 %collective-permute-start.1 = (f32[16,32,128]{2,1,0:T(8,128)}, f32[16,32,128]{2,1,0:T(8,128)S(1)}, u32[]{:S(2)}, u32[]{:S(2)}) collective-permute-start(f32[16,32,128]{2,1,0:T(8,128)} %get-tuple-element.25), channel_id=1, source_target_pairs={{0,8},{4,12},{8,0},{12,4},{16,24},{20,28},{24,16},{28,20},{1,9},{5... | collective-permute-start | bytes 786440 | tf_op jit(solution)/shard_map/ppermute | solution.py:280
  8.8 34.6 %collective-permute-start.2 = (f32[16,32,128]{2,1,0:T(8,128)}, f32[16,32,128]{2,1,0:T(8,128)S(1)}, u32[]{:S(2)}, u32[]{:S(2)}) collective-permute-start(f32[16,32,128]{2,1,0:T(8,128)} %get-tuple-element.26), channel_id=1, source_target_pairs={{0,12},{4,8},{8,4},{12,0},{16,28},{20,24},{24,20},{28,16},{1,13},{... | collective-permute-start | bytes 786440 | tf_op jit(solution)/shard_map/ppermute | solution.py:280
  8.9 35.3 %collective-permute-start.3 = (f32[16,32,128]{2,1,0:T(8,128)S(1)}, f32[16,32,128]{2,1,0:T(8,128)S(1)}, u32[]{:S(2)}, u32[]{:S(2)}) collective-permute-start(f32[16,32,128]{2,1,0:T(8,128)S(1)} %get-tuple-element.27), channel_id=1, source_target_pairs={{0,16},{4,20},{8,24},{12,28},{16,0},{20,4},{24,8},{28,12},{1,17},{... | collective-permute-start | bytes 786440 | tf_op jit(solution)/shard_map/ppermute | solution.py:280
  10.6 34.2 %collective-permute-start.4 = (f32[16,32,128]{2,1,0:T(8,128)S(1)}, f32[16,32,128]{2,1,0:T(8,128)S(1)}, u32[]{:S(2)}, u32[]{:S(2)}) collective-permute-start(f32[16,32,128]{2,1,0:T(8,128)S(1)} %get-tuple-element.28), channel_id=1, source_target_pairs={{0,20},{4,16},{8,28},{12,24},{16,4},{20,0},{24,12},{28,8},{1,21},{... | collective-permute-start | bytes 786440 | tf_op jit(solution)/shard_map/ppermute | solution.py:280
  14.2 11.0 %copy-start.11 = (s32[8,8]{1,0:T(8,128)S(1)}, s32[8,8]{1,0:T(8,128)}, u32[]{:S(2)}) copy-start(s32[8,8]{1,0:T(8,128)} %mask_ref.11) | copy-start | bytes 772
  25.2 5.8 %copy-start.3 = (f32[4,128,64,128]{3,2,1,0:T(8,128)S(1)}, f32[4,128,64,128]{3,2,1,0:T(8,128)}, u32[]{:S(2)}) copy-start(f32[4,128,64,128]{3,2,1,0:T(8,128)} %second_ref.1) | copy-start | bytes 50331652
  39.6 10.1 %collective-permute-start.5 = (f32[16,32,128]{2,1,0:T(8,128)S(1)}, f32[16,32,128]{2,1,0:T(8,128)S(1)}, u32[]{:S(2)}, u32[]{:S(2)}) collective-permute-start(f32[16,32,128]{2,1,0:T(8,128)S(1)} %get-tuple-element.29), channel_id=1, source_target_pairs={{0,24},{4,28},{8,16},{12,20},{16,8},{20,12},{24,0},{28,4},{1,25},{... | collective-permute-start | bytes 786440 | tf_op jit(solution)/shard_map/ppermute | solution.py:280
  42.2 12.0 %collective-permute-start.6 = (f32[16,32,128]{2,1,0:T(8,128)S(1)}, f32[16,32,128]{2,1,0:T(8,128)S(1)}, u32[]{:S(2)}, u32[]{:S(2)}) collective-permute-start(f32[16,32,128]{2,1,0:T(8,128)S(1)} %get-tuple-element.30), channel_id=1, source_target_pairs={{0,28},{4,24},{8,20},{12,16},{16,12},{20,8},{24,4},{28,0},{1,29},{... | collective-permute-start | bytes 786440 | tf_op jit(solution)/shard_map/ppermute | solution.py:280
  43.4 0.7 copy-start.4
  44.2 0.7 copy-start.6
  44.9 0.7 copy-start.8
  54.3 1.0 copy-start.5
  55.2 0.9 copy-start.7
  56.2 0.9 copy-start.9
  65.7 13.2 %all-to-all-start = ((f32[32,1,128]{2,1,0:T(1,128)}), f32[32,1,128]{2,1,0:T(1,128)S(1)}, u32[]{:S(2)}, u32[]{:S(2)}) async-start(f32[32,1,128]{2,1,0:T(1,128)} %bitcast.18), calls=%async_computation | async-start | bytes 32768 | tf_op jit(solution)/shard_map/all_to_all | solution.py:369
  83.6 3.6 %collective-permute-start.7 = (f32[16,32,128]{2,1,0:T(8,128)S(1)}, f32[16,32,128]{2,1,0:T(8,128)S(1)}, u32[]{:S(2)}, u32[]{:S(2)}) collective-permute-start(f32[16,32,128]{2,1,0:T(8,128)S(1)} %get-tuple-element.34), channel_id=1, source_target_pairs={{0,4},{4,0},{8,12},{12,8},{16,20},{20,16},{24,28},{28,24},{1,5},{5... | collective-permute-start | bytes 786440 | tf_op jit(solution)/shard_map/ppermute | solution.py:280
  83.7 9.2 %collective-permute-start.8 = (f32[16,32,128]{2,1,0:T(8,128)S(1)}, f32[16,32,128]{2,1,0:T(8,128)S(1)}, u32[]{:S(2)}, u32[]{:S(2)}) collective-permute-start(f32[16,32,128]{2,1,0:T(8,128)S(1)} %get-tuple-element.35), channel_id=1, source_target_pairs={{0,8},{4,12},{8,0},{12,4},{16,24},{20,28},{24,16},{28,20},{1,9},{5... | collective-permute-start | bytes 786440 | tf_op jit(solution)/shard_map/ppermute | solution.py:280
  84.4 13.2 %collective-permute-start.9 = (f32[16,32,128]{2,1,0:T(8,128)S(1)}, f32[16,32,128]{2,1,0:T(8,128)S(1)}, u32[]{:S(2)}, u32[]{:S(2)}) collective-permute-start(f32[16,32,128]{2,1,0:T(8,128)S(1)} %get-tuple-element.36), channel_id=1, source_target_pairs={{0,12},{4,8},{8,4},{12,0},{16,28},{20,24},{24,20},{28,16},{1,13},{... | collective-permute-start | bytes 786440 | tf_op jit(solution)/shard_map/ppermute | solution.py:280
  85.6 13.9 %collective-permute-start.10 = (f32[16,32,128]{2,1,0:T(8,128)S(1)}, f32[16,32,128]{2,1,0:T(8,128)S(1)}, u32[]{:S(2)}, u32[]{:S(2)}) collective-permute-start(f32[16,32,128]{2,1,0:T(8,128)S(1)} %get-tuple-element.37), channel_id=1, source_target_pairs={{0,16},{4,20},{8,24},{12,28},{16,0},{20,4},{24,8},{28,12},{1,17},{... | collective-permute-start | bytes 786440 | tf_op jit(solution)/shard_map/ppermute | solution.py:280
  86.2 24.2 %collective-permute-start.11 = (f32[16,32,128]{2,1,0:T(8,128)S(1)}, f32[16,32,128]{2,1,0:T(8,128)S(1)}, u32[]{:S(2)}, u32[]{:S(2)}) collective-permute-start(f32[16,32,128]{2,1,0:T(8,128)S(1)} %get-tuple-element.38), channel_id=1, source_target_pairs={{0,20},{4,16},{8,28},{12,24},{16,4},{20,0},{24,12},{28,8},{1,21},{... | collective-permute-start | bytes 786440 | tf_op jit(solution)/shard_map/ppermute | solution.py:280
  87.3 25.0 %collective-permute-start.12 = (f32[16,32,128]{2,1,0:T(8,128)S(1)}, f32[16,32,128]{2,1,0:T(8,128)S(1)}, u32[]{:S(2)}, u32[]{:S(2)}) collective-permute-start(f32[16,32,128]{2,1,0:T(8,128)S(1)} %get-tuple-element.39), channel_id=1, source_target_pairs={{0,24},{4,28},{8,16},{12,20},{16,8},{20,12},{24,0},{28,4},{1,25},{... | collective-permute-start | bytes 786440 | tf_op jit(solution)/shard_map/ppermute | solution.py:280
  92.9 19.4 %collective-permute-start.13 = (f32[16,32,128]{2,1,0:T(8,128)S(1)}, f32[16,32,128]{2,1,0:T(8,128)S(1)}, u32[]{:S(2)}, u32[]{:S(2)}) collective-permute-start(f32[16,32,128]{2,1,0:T(8,128)S(1)} %get-tuple-element.40), channel_id=1, source_target_pairs={{0,28},{4,24},{8,20},{12,16},{16,12},{20,8},{24,4},{28,0},{1,29},{... | collective-permute-start | bytes 786440 | tf_op jit(solution)/shard_map/ppermute | solution.py:280
  92.9 2.2 %copy-start.2 = (f32[16,512,128]{2,1,0:T(8,128)S(1)}, f32[16,512,128]{2,1,0:T(8,128)}, u32[]{:S(2)}) copy-start(f32[16,512,128]{2,1,0:T(8,128)} %init_ref.9) | copy-start | bytes 12582916

commit v2 on v1

v2 whole, which is shorter than its diff:
```python
import functools

import jax
import jax.numpy as jnp
from jax import lax
from jax.experimental import pallas as pl
from jax.experimental.pallas import tpu as pltpu
from jax.sharding import PartitionSpec as P

ITERS = 4
MOMENTS = 2 * ITERS

HIGHEST = lax.Precision.HIGHEST
damping = 1.0
MIB = 1 << 20
UNROLL = 4
IN_FLIGHT = 5


def split(x):
    high = x.astype(jnp.bfloat16)
    return high, (x - high.astype(jnp.float32)).astype(jnp.bfloat16)


def left_operand(matrix):
    high, low = split(matrix)
    return jnp.concatenate(
        [jnp.concatenate([high, high], axis=1), jnp.concatenate([low, low], axis=1)], axis=0
    )


def right_operand(matrix):
    return jnp.concatenate(split(matrix), axis=0)


def product(left, right):
    both = jnp.dot(left, right, preferred_element_type=jnp.float32)
    rows = both.shape[0] // 2
    return both[:rows] + both[rows:]


def tissue_half(mask_ref, tile):
    return mask_ref[tile, 2 * lax.axis_index("gy") + 1]


def tissue_lanes(shape, half):
    lane = lax.broadcasted_iota(jnp.int32, shape, len(shape) - 1)
    return (lane >= shape[-1] // 2) == (half == 1)


def pack_kernel(mask_ref, init_ref, *refs):
    count = len(refs) - 4
    out_refs, (staged, flags, sems, flag_sem) = refs[:count], refs[count:]
    slab, columns, lanes = out_refs[0].shape
    width = 2 * columns
    me = lax.axis_index("gz")

    def copy(k):
        start = pl.multiple_of(jnp.bitwise_xor(me, k) * width, width)
        return pltpu.make_async_copy(
            init_ref.at[:, pl.ds(start, width), :], staged.at[k], sems.at[k]
        )

    flag_copy = pltpu.make_async_copy(mask_ref, flags, flag_sem)
    flag_copy.start()
    for k in range(count):
        copy(k).start()
    flag_copy.wait()
    for k in range(count):
        copy(k).wait()
        half = tissue_half(flags, jnp.bitwise_xor(me, k))
        here = tissue_lanes((slab, columns, lanes), half)
        first = staged[k, :, :columns, :]
        second = pltpu.roll(staged[k, :, columns:, :], lanes // 2, 2)
        out_refs[k][...] = jnp.where(here, first, second)


def tables_kernel(
    index_ref, kernels_ref, left_ref, gram_ref, poly_ref, top_ref, bank, boxes, blur, square
):
    views, zbands, xbands = index_ref.shape
    taps = kernels_ref.shape[1]
    depth = poly_ref.shape[-1]
    zwidth = depth // zbands
    reach = taps // 2
    me = lax.axis_index("gz")

    def pick(ref, v, zband, xband):
        return ref[pl.ds(index_ref[v, zband, xband], 1), :]

    bank[...] = jnp.zeros_like(bank)
    bank[:, :taps] = kernels_ref[...]
    rows = bank[...]
    box = rows
    for r in range(1, zwidth):
        box = box + pltpu.roll(rows, r, 1)
    boxes[...] = box * jnp.sum(rows, axis=1, keepdims=True)

    def row_sums(xband, largest):
        total = jnp.zeros((1, depth), jnp.float32)
        for zband in range(zbands):
            part = pick(boxes, 0, zband, xband)
            for v in range(1, views):
                part = part + pick(boxes, v, zband, xband)
            total = total + pltpu.roll(part, (zband * zwidth - reach) % depth, 1)
        return jnp.maximum(largest, total)

    largest = lax.fori_loop(0, xbands, row_sums, jnp.zeros((1, depth), jnp.float32))
    top = jnp.max(largest, axis=1, keepdims=True)
    top_ref[...] = jnp.broadcast_to(top, top_ref.shape)

    z = lax.broadcasted_iota(jnp.int32, (zwidth, depth), 0)
    w = lax.broadcasted_iota(jnp.int32, (zwidth, depth), 1)
    for v in range(views):
        for zband in range(zbands):
            first = zband * zwidth
            row = jnp.broadcast_to(pick(bank, v, zband, me), (zwidth, depth))
            row = pltpu.roll(row, (first - reach) % depth, 1, stride=1, stride_axis=0)
            blur[v * depth + first : v * depth + first + zwidth, :] = jnp.where(
                jnp.abs(w - z - first) <= reach, row, 0.0
            )
    across = blur[...].T
    for v in range(views):
        left_ref[:, 2 * depth * v : 2 * depth * (v + 1)] = left_operand(
            across[:, depth * v : depth * (v + 1)]
        )
    gram = jnp.dot(across, blur[...], precision=HIGHEST, preferred_element_type=jnp.float32)
    square[...] = gram
    tiles = xbands
    slab = depth // tiles
    swapped = jnp.concatenate(
        [square[pl.ds(pl.multiple_of(jnp.bitwise_xor(me, k) * slab, slab), slab), :] for k in range(tiles)],
        axis=0,
    )
    gram_ref[...] = left_operand(swapped.T)

    eye = jnp.where(
        lax.broadcasted_iota(jnp.int32, (depth, depth), 0)
        == lax.broadcasted_iota(jnp.int32, (depth, depth), 1),
        1.0,
        0.0,
    )
    poly = [eye, gram * (2.0 / top) - eye]
    for k in range(2, MOMENTS):
        half = k // 2
        other = k - half
        poly.append(
            2.0
            * jnp.dot(
                poly[other], poly[half], precision=HIGHEST, preferred_element_type=jnp.float32
            )
            - poly[other - half]
        )
    for k in range(MOMENTS):
        poly_ref[k] = poly[k]


def project_kernel(mask_ref, left_ref, measured_ref, out_ref, staged, sems):
    _, _, views, depth, step, lanes = staged.shape
    columns = out_ref.shape[0]
    steps = columns // step

    def copy(i, side):
        start = pl.multiple_of(i * step + side * columns, step)
        return pltpu.make_async_copy(
            measured_ref.at[:, :, pl.ds(start, step), :],
            staged.at[i % 2, side],
            sems.at[i % 2, side],
        )

    for side in range(2):
        copy(0, side).start()
    half = tissue_half(mask_ref, lax.axis_index("gz"))
    here = tissue_lanes((depth, lanes), half)
    flat = staged.reshape(2 * 2 * views * depth * step, lanes)

    @pl.loop(0, steps)
    def _(i):
        @pl.when(i + 1 < steps)
        def _():
            for side in range(2):
                copy(i + 1, side).start()

        for side in range(2):
            copy(i, side).wait()

        def read(side, v, x):
            start = (((i % 2) * 2 + side) * views + v) * (depth * step) + x
            return flat[pl.ds(start, depth, stride=step), :]

        def packed(v, x):
            return jnp.where(here, read(0, v, x), pltpu.roll(read(1, v, x), lanes // 2, 1))

        for x in range(0, step, 2):
            parts = []
            for v in range(views):
                parts.append(
                    right_operand(jnp.concatenate([packed(v, x), packed(v, x + 1)], axis=1))
                )
            result = product(left_ref[...], jnp.concatenate(parts, axis=0))
            out_ref[i * step + x] = result[:, :lanes]
            out_ref[i * step + x + 1] = result[:, lanes:]


def residual_kernel(gram_ref, poly_ref, projected_ref, *refs):
    count = len(refs) - 3
    chunks, (residual_ref, moments_ref, square_ref) = refs[:count], refs[count:]
    slab, columns, lanes = chunks[0].shape
    depth = poly_ref.shape[-1]
    square_ref[...] = jnp.zeros_like(square_ref)
    flat = [chunk.reshape(slab * columns, lanes) for chunk in chunks]

    def field(x):
        return jnp.concatenate([ref[pl.ds(x, slab, stride=columns), :] for ref in flat], axis=0)

    @pl.loop(0, columns // 2, step=UNROLL)
    def _(first):
        total = None
        for i in range(UNROLL):
            pair = first + i
            x = 2 * pair
            image = product(
                gram_ref[...], right_operand(jnp.concatenate([field(x), field(x + 1)], axis=1))
            )
            start = jnp.concatenate([projected_ref[x], projected_ref[x + 1]], axis=1)
            both = right_operand(start - image)
            residual_ref[pair] = both
            square = lax.dot_general(
                both, both, (((1,), (1,)), ((), ())), preferred_element_type=jnp.float32
            )
            total = square if total is None else total + square
        square_ref[...] += total

    square = square_ref[...]
    square = (square[:depth, :depth] + square[depth:, depth:]) + (
        square[:depth, depth:] + square[depth:, :depth]
    )
    count = poly_ref.shape[0]
    sums = jnp.concatenate(
        [jnp.sum(square * poly_ref[k], axis=0, keepdims=True) for k in range(count)], axis=0
    )
    sums = jnp.sum(sums, axis=1, keepdims=True)
    lane = lax.broadcasted_iota(jnp.int32, (count, lanes), 1)
    order = lax.broadcasted_iota(jnp.int32, (count, lanes), 0)
    row = jnp.sum(jnp.where(lane == order, sums, 0.0), axis=0, keepdims=True)
    moments_ref[...] = jnp.broadcast_to(row, moments_ref.shape)


def conjugate(moments, centre, radius):
    def inner(p, q):
        total = None
        for i, a in enumerate(p):
            for j, b in enumerate(q):
                term = a * b * (0.5 * (moments[i + j] + moments[abs(i - j)]))
                total = term if total is None else total + term
        return total

    def operate(p):
        image = [centre * a for a in p] + [None]

        def put(i, value):
            image[i] = value if image[i] is None else image[i] + value

        for j, a in enumerate(p):
            if j == 0:
                put(1, radius * a)
            else:
                put(j + 1, 0.5 * radius * a)
                put(j - 1, 0.5 * radius * a)
        return image

    one = jnp.ones_like(moments[0])
    residual, direction = [one], [one]
    solved = []
    norm_now = moments[0]
    for iteration in range(ITERS):
        image = operate(direction)
        step_size = norm_now / inner(direction, image)
        solved = [s + step_size * d for s, d in zip(solved, direction)] + [
            step_size * d for d in direction[len(solved) :]
        ]
        if iteration == ITERS - 1:
            break
        residual = [r - step_size * i for r, i in zip(residual, image)] + [
            -step_size * i for i in image[len(residual) :]
        ]
        norm_next = inner(residual, residual)
        ratio = norm_next / norm_now
        direction = [r + ratio * d for r, d in zip(residual, direction)] + residual[len(direction) :]
        norm_now = norm_next
    return solved


def correct_kernel(top_ref, moments_ref, poly_ref, residual_ref, *refs):
    count = len(refs) - 2
    out_refs, (matrix_ref, left_ref) = refs[:count], refs[count:]
    slab, columns, lanes = out_refs[0].shape
    me = lax.axis_index("gz")
    row = jnp.sum(moments_ref[...], axis=0, keepdims=True)
    lane = lax.broadcasted_iota(jnp.int32, row.shape, 1)
    moments = [
        jnp.sum(jnp.where(lane == k, row, 0.0), axis=1, keepdims=True) for k in range(MOMENTS)
    ]
    radius = 0.5 * top_ref[:1, :1]
    coefficients = conjugate(moments, damping + radius, radius)
    matrix = coefficients[0] * poly_ref[0]
    for k in range(1, ITERS):
        matrix = matrix + coefficients[k] * poly_ref[k]
    matrix_ref[...] = matrix
    left_ref[...] = left_operand(
        jnp.concatenate(
            [
                matrix_ref[pl.ds(pl.multiple_of(jnp.bitwise_xor(me, k) * slab, slab), slab), :]
                for k in range(count)
            ],
            axis=0,
        )
    )
    flat = [ref.reshape(slab * columns, lanes) for ref in out_refs]

    @pl.loop(0, columns // 2, step=UNROLL)
    def _(first):
        for i in range(UNROLL):
            pair = first + i
            result = product(left_ref[...], residual_ref[pair])
            for k in range(count):
                rows = result[slab * k : slab * (k + 1)]
                for side in range(2):
                    flat[k][pl.ds(2 * pair + side, slab, stride=columns), :] = rows[
                        :, lanes * side : lanes * (side + 1)
                    ]


def unpack_kernel(group, aliased, mask_ref, init_ref, *refs):
    if aliased:
        refs = refs[1:]
    chunks, (out_ref, staged, in_sems, out_sems) = refs[:-4], refs[-4:]
    slab, columns, lanes = chunks[0].shape
    width = 2 * columns
    me = lax.axis_index("gz")

    def tile(k):
        return jnp.bitwise_xor(me, k)

    def columns_of(ref, k):
        return ref.at[:, pl.ds(pl.multiple_of(tile(k) * width, width), width), :]

    loads = [
        pltpu.make_async_copy(columns_of(init_ref, k), staged.at[n], in_sems.at[n])
        for n, k in enumerate(group)
    ]
    stores = [
        pltpu.make_async_copy(staged.at[n], columns_of(out_ref, k), out_sems.at[n])
        for n, k in enumerate(group)
    ]
    for load in loads:
        load.start()
    for n, k in enumerate(group):
        here = tissue_lanes((slab, columns, lanes), tissue_half(mask_ref, tile(k)))
        change = chunks[n][...]
        loads[n].wait()
        staged[n, :, :columns, :] += jnp.where(here, change, 0.0)
        staged[n, :, columns:, :] += pltpu.roll(jnp.where(here, 0.0, change), lanes // 2, 2)
        stores[n].start()
    for store in stores:
        store.wait()


SMEM = pl.BlockSpec(memory_space=pltpu.SMEM)
VMEM = pl.BlockSpec(memory_space=pltpu.VMEM)
HBM = pl.BlockSpec(memory_space=pltpu.HBM)
ANY = pl.BlockSpec(memory_space=pl.ANY)


def cost(flops, read, transcendentals=0):
    return pl.CostEstimate(
        flops=int(flops), bytes_accessed=int(read), transcendentals=transcendentals
    )


def local(init, measured, mask, kernel_index, kernels):
    tiles, rows = lax.axis_size("gz"), lax.axis_size("gy")
    slab, _, lanes = init.shape
    views, depth, width, _ = measured.shape
    columns = width // 2
    f32, bf16 = jnp.float32, jnp.bfloat16
    shape = jax.ShapeDtypeStruct
    chunk = shape((slab, columns, lanes), f32)

    def send(block, k):
        return lax.ppermute(block, "gz", [(j, j ^ k) for j in range(tiles)])

    packed = pl.pallas_call(
        pack_kernel,
        name="pack_blocks",
        out_shape=[chunk] * tiles,
        in_specs=[HBM, HBM],
        out_specs=[VMEM] * tiles,
        scratch_shapes=[
            pltpu.VMEM((tiles, slab, width, lanes), f32),
            pltpu.SMEM(mask.shape, jnp.int32),
            pltpu.SemaphoreType.DMA((tiles,)),
            pltpu.SemaphoreType.DMA,
        ],
        compiler_params=pltpu.CompilerParams(vmem_limit_bytes=60 * MIB),
        cost_estimate=cost(init.size, 6 * init.size),
    )(mask, init)

    order = [1] + [k for k in range(tiles - 2, 1, -1) if k % 2 == 0]
    order += [k for k in range(tiles - 1, 1, -1) if k % 2 == 1]
    fields = [packed[0]] + [None] * (tiles - 1)
    for n, k in enumerate(order):
        block = packed[k]
        if n >= IN_FLIGHT:
            before = order[n - IN_FLIGHT]
            block, fields[before] = lax.optimization_barrier((block, fields[before]))
        fields[k] = send(block, k)

    poly_shape = shape((MOMENTS, depth, depth), f32)
    left, gram, poly, top = pl.pallas_call(
        tables_kernel,
        name="blur_tables",
        out_shape=[
            shape((2 * depth, 2 * views * depth), bf16),
            shape((2 * depth, 2 * depth), bf16),
            poly_shape,
            shape((8, lanes), f32),
        ],
        in_specs=[SMEM, VMEM],
        out_specs=[VMEM] * 4,
        scratch_shapes=[
            pltpu.VMEM((kernels.shape[0], depth), f32),
            pltpu.VMEM((kernels.shape[0], depth), f32),
            pltpu.VMEM((views * depth, depth), f32),
            pltpu.VMEM((depth, depth), f32),
        ],
        compiler_params=pltpu.CompilerParams(vmem_limit_bytes=8 * MIB),
        cost_estimate=cost(12 * 20 * depth**3, 4 * MIB),
    )(kernel_index, kernels)

    step = 8
    projected = pl.pallas_call(
        project_kernel,
        name="project_views",
        out_shape=shape((columns, depth, lanes), f32),
        in_specs=[SMEM, VMEM, HBM],
        out_specs=VMEM,
        scratch_shapes=[
            pltpu.VMEM((2, 2, views, depth, step, lanes), f32),
            pltpu.SemaphoreType.DMA((2, 2)),
        ],
        compiler_params=pltpu.CompilerParams(vmem_limit_bytes=48 * MIB),
        cost_estimate=cost(8 * views * depth * depth * columns * lanes, 4 * measured.size),
    )(mask, left, measured)

    everyone = tiles * rows
    pairs = columns // 2
    residual, moments = pl.pallas_call(
        residual_kernel,
        name="first_residual",
        out_shape=[
            shape((pairs, 2 * depth, 2 * lanes), bf16),
            shape((everyone, lanes), f32),
        ],
        in_specs=[VMEM] * (3 + tiles),
        out_specs=[VMEM] * 2,
        scratch_shapes=[pltpu.VMEM((2 * depth, 2 * depth), f32)],
        compiler_params=pltpu.CompilerParams(vmem_limit_bytes=16 * MIB),
        cost_estimate=cost(
            16 * depth * depth * columns * lanes, 12 * depth * columns * lanes
        ),
    )(gram, poly, projected, *fields)

    moments = lax.all_to_all(moments, ("gz", "gy"), split_axis=0, concat_axis=0, tiled=True)

    changes = pl.pallas_call(
        correct_kernel,
        name="correction",
        out_shape=[chunk] * tiles,
        in_specs=[VMEM] * 4,
        out_specs=[VMEM] * tiles,
        scratch_shapes=[
            pltpu.VMEM((depth, depth), f32),
            pltpu.VMEM((2 * depth, 2 * depth), bf16),
        ],
        compiler_params=pltpu.CompilerParams(vmem_limit_bytes=16 * MIB),
        cost_estimate=cost(8 * depth * depth * columns * lanes, 8 * depth * columns * lanes),
    )(top, moments, poly, residual)
    changes = [changes[0]] + [send(changes[k], k) for k in range(1, tiles)]

    cut = [0, tiles // 2, tiles // 2 + 1, tiles]
    groups = [list(range(first, last)) for first, last in zip(cut, cut[1:])]
    solved = None
    for group in groups:
        size = len(group)
        solved = pl.pallas_call(
            functools.partial(unpack_kernel, group, solved is not None),
            name="add_correction",
            out_shape=shape(init.shape, f32),
            in_specs=[SMEM, ANY] + [ANY] * (solved is not None) + [VMEM] * size,
            out_specs=ANY,
            input_output_aliases={} if solved is None else {2: 0},
            scratch_shapes=[
                pltpu.VMEM((size, slab, width, lanes), f32),
                pltpu.SemaphoreType.DMA((size,)),
                pltpu.SemaphoreType.DMA((size,)),
            ],
            compiler_params=pltpu.CompilerParams(vmem_limit_bytes=16 * MIB),
            cost_estimate=cost(init.size // 4, 5 * init.size // 4 * size),
        )(mask, init, *([] if solved is None else [solved]), *[changes[k] for k in group])
    return solved


def solution(mesh):
    return jax.shard_map(
        local,
        mesh=mesh,
        in_specs=(P("gz", None, "gy"), P(None, None, "gz", "gy"), P(), P(), P()),
        out_specs=P("gz", None, "gy"),
        check_vma=False,
    )
```

time: 115 us -> 79.6 us (0.69)
  local copies, waits for them, and re-layouts: 19.6 us -> 0.02 us
  blocking collectives: 0 us -> 13 us
  matrix products: 8.54 us -> 0 us
  waiting for transfers between devices: 31.6 us -> 26.1 us
  starting transfers between devices: 18 us -> 12.6 us
  other arithmetic: 4.43 us -> 0 us
  Pallas kernels: 31 us -> 27.5 us
    unnamed x27 -> x10, local copies, waits for them, and re-layouts: 16.8 us -> 0.02 us
    all_to_all x0 -> x1, blocking collectives: none -> 13 us  [local(): lax.all_to_all(moments, ('gz', 'gy'), split_axis=0, concat_axis=0, tiled=...]
    dot_general x14 -> x0, matrix products: 8.54 us -> none  [the longest x1 3 us: blur_tables(): return jnp.einsum('vzbt,zwt->vbzw', row_taps, tap_select, precision=HIGHEST)]
    all_to_all x1 -> x0, waiting for transfers between devices: 6.2 us -> none  [local(): lax.all_to_all(moments, ('gz', 'gy'), split_axis=0, concat_axis=0, tiled=...]
    all_to_all x1 -> x0, starting transfers between devices: 6.09 us -> none  [local(): lax.all_to_all(moments, ('gz', 'gy'), split_axis=0, concat_axis=0, tiled=...]
    mul x1 -> x0, other arithmetic: 2.85 us -> none  [local(): top = jnp.max(jnp.sum(blurs * row_sums[..., None], axis=(0, 2)))]
    another operation x1 -> x0, local copies, waits for them, and re-layouts: 2.55 us -> none
    pallas_call x1, Pallas kernels: 4.76 us -> 2.25 us  [local(): pl.pallas_call(correct_kernel, name='correction', out_shape=[chunk] * til...]
  transfers between devices with their start and end apart: 15 -> 14, of which waited for: 6 -> 5; matrix products, arithmetic and copies ran while one was open for 15% -> 0% of each run, Pallas kernels for 11% -> 20%
where the time goes in v2:
time: 79.6 us; the launch traced here: 79.4 us
  Pallas kernels  27.5 us (35%)
  waiting for transfers between devices  26.1 us (33%)
  blocking collectives  13 us (16%)
  starting transfers between devices  12.6 us (16%)
    ppermute x14, waiting for transfers between devices, send(): return lax.ppermute(block, 'gz', [(j, j ^ k) for j in range(tiles)])  26.1 us
    all_to_all x1, blocking collectives, local(): lax.all_to_all(moments, ('gz', 'gy'), split_axis=0, concat_axis=0, tiled=...  13 us
    ppermute x14, starting transfers between devices, send(): return lax.ppermute(block, 'gz', [(j, j ^ k) for j in range(tiles)])  12.6 us
    pallas_call x1, Pallas kernels, local(): pl.pallas_call(project_kernel, name='project_views', out_shape=shape((col...  8.83 us
    pallas_call x3, Pallas kernels, local(): pl.pallas_call(functools.partial(unpack_kernel, group, solved is not None...  5.97 us
    pallas_call x1, Pallas kernels, local(): pl.pallas_call(residual_kernel, name='first_residual', out_shape=[shape((...  3.8 us
    pallas_call x1, Pallas kernels, local(): pl.pallas_call(pack_kernel, name='pack_blocks', out_shape=[chunk] * tiles...  3.58 us
    pallas_call x1, Pallas kernels, local(): pl.pallas_call(tables_kernel, name='blur_tables', out_shape=[shape((2 * d...  3.05 us
  transfers between devices with their start and end apart: 14, of which 5 were waited for; matrix products, arithmetic and copies ran while one was open for 0% of the time, Pallas kernels for 20%

profile of v2, /device:TPU:0, one launch (start us, length us, event | category | flops | bytes accessed | tf_op | source)
XLA Modules:
  0.0 79.4 jit_solution(4744869838189301889)
XLA Ops:
  0.0 0.0 copy-start.2
  0.0 0.0 copy-start.4
  0.0 0.0 copy-start.3
  0.0 3.6 %pack_blocks.1 = (f32[16,32,128]{2,1,0:T(8,128)}, f32[16,32,128]{2,1,0:T(8,128)}, f32[16,32,128]{2,1,0:T(8,128)}, f32[16,32,128]{2,1,0:T(8,128)}, f32[16,32,128]...) custom-call(s32[8,8]{1,0:T(8,128)} %mask_ref.9, f32[16,512,128]{2,1,0:T(8,128)} %init_ref.7), custom_call_target="tpu_custom_call" | custom-call | flops 1048576 | bytes 6291456 | tf_op jit(solution)/shard_map/pack_blocks/pallas_call | solution.py:393
  3.6 0.5 collective-permute-start
  4.1 3.5 %collective-permute-start.2 = (f32[16,32,128]{2,1,0:T(8,128)}, f32[16,32,128]{2,1,0:T(8,128)S(1)}, u32[]{:S(2)}, u32[]{:S(2)}) collective-permute-start(f32[16,32,128]{2,1,0:T(8,128)} %get-tuple-element.41), channel_id=1, source_target_pairs={{0,24},{4,28},{8,16},{12,20},{16,8},{20,12},{24,0},{28,4},{1,25},{... | collective-permute-start | bytes 786440 | tf_op jit(solution)/shard_map/ppermute | solution.py:391
  7.6 0.5 collective-permute-start.1
  8.2 0.1 collective-permute-start.4
  8.3 2.0 %collective-permute-start.6 = (f32[16,32,128]{2,1,0:T(8,128)}, f32[16,32,128]{2,1,0:T(8,128)S(1)}, u32[]{:S(2)}, u32[]{:S(2)}) collective-permute-start(f32[16,32,128]{2,1,0:T(8,128)} %get-tuple-element.46), channel_id=1, source_target_pairs={{0,28},{4,24},{8,20},{12,16},{16,12},{20,8},{24,4},{28,0},{1,29},{... | collective-permute-start | bytes 786440 | tf_op jit(solution)/shard_map/ppermute | solution.py:391
  10.3 0.0 collective-permute-done.refs_1_
  10.3 1.0 %collective-permute-start.5 = (f32[16,32,128]{2,1,0:T(8,128)}, f32[16,32,128]{2,1,0:T(8,128)S(1)}, u32[]{:S(2)}, u32[]{:S(2)}) collective-permute-start(f32[16,32,128]{2,1,0:T(8,128)} %get-tuple-element.44), channel_id=1, source_target_pairs={{0,20},{4,16},{8,28},{12,24},{16,4},{20,0},{24,12},{28,8},{1,21},{... | collective-permute-start | bytes 786440 | tf_op jit(solution)/shard_map/ppermute | solution.py:391
  11.4 3.7 %collective-permute-done.2.refs_6_ = f32[16,32,128]{2,1,0:T(8,128)S(1)} collective-permute-done((f32[16,32,128]{2,1,0:T(8,128)}, f32[16,32,128]{2,1,0:T(8,128)S(1)}, u32[]{:S(2)}, u32[]{:S(2)}) %collective-permute-start.2) | collective-permute-done | bytes 262176 | tf_op jit(solution)/shard_map/ppermute | solution.py:391
  15.0 0.7 collective-permute-start.3
  15.8 0.0 copy-done.4
  15.8 0.0 copy-done.3
  15.8 3.0 %blur_tables.1 = (bf16[256,1024]{1,0:T(8,128)(2,1)S(1)}, bf16[256,256]{1,0:T(8,128)(2,1)S(1)}, f32[8,128,128]{2,1,0:T(8,128)S(1)}, f32[8,128]{1,0:T(8,128)S(1)}) custom-call(s32[4,8,8]{2,1,0:T(8,128)S(1)} %copy-done.3, f32[16,31]{1,0:T(8,128)S(1)} %copy-done.4), custom_call_target="tpu_custom_call" | custom-call | flops 503316480 | bytes 4194304 | tf_op jit(solution)/shard_map/blur_tables/pallas_call | solution.py:420
  18.8 0.0 copy-done.2
  18.8 0.0 copy-start.1
  18.8 8.8 %project_views.1.projected_ref = f32[32,128,128]{2,1,0:T(8,128)S(1)} custom-call(s32[8,8]{1,0:T(8,128)S(1)} %copy-done.2, bf16[256,1024]{1,0:T(8,128)(2,1)S(1)} %get-tuple-element.34.left_ref, f32[4,128,64,128]{3,2,1,0:T(8,128)} %measured_ref.1), custom_call_target="tpu_custom_call" | custom-call | flops 2147483648 | bytes 16777216 | tf_op jit(solution)/shard_map/project_views/pallas_call | solution.py:442
  27.7 0.0 copy-start
  27.7 0.0 collective-permute-done.1.refs_2_
  27.7 0.0 collective-permute-done.4.refs_4_
  27.7 0.0 collective-permute-done.6.refs_7_
  27.7 3.8 %collective-permute-done.5.refs_5_ = f32[16,32,128]{2,1,0:T(8,128)S(1)} collective-permute-done((f32[16,32,128]{2,1,0:T(8,128)}, f32[16,32,128]{2,1,0:T(8,128)S(1)}, u32[]{:S(2)}, u32[]{:S(2)}) %collective-permute-start.5) | collective-permute-done | bytes 262176 | tf_op jit(solution)/shard_map/ppermute | solution.py:391
  31.5 0.0 collective-permute-done.3.refs_3_
  31.5 0.0 copy-done.1
  31.5 3.8 %first_residual.1 = (bf16[16,256,256]{2,1,0:T(8,128)(2,1)S(1)}, f32[32,128]{1,0:T(8,128)S(1)}) custom-call(bf16[256,256]{1,0:T(8,128)(2,1)S(1)} %get-tuple-element.32.gram_ref, f32[8,128,128]{2,1,0:T(8,128)S(1)} %get-tuple-element.33.poly_ref, f32[32,128,128]{2,1,0:T(8,128)S(1)} %project_views.1.projected_ref, f32[16,32,128]{2,1,0:T(8,128)S(1)} %copy-done.1, ...), custom_call_target="tpu_custom_call" | custom-call | flops 1073741824 | bytes 6291456 | tf_op jit(solution)/shard_map/first_residual/pallas_call | solution.py:458
  35.3 13.0 %all_to_all.11 = f32[32,1,128]{2,1,0:T(1,128)S(1)} all-to-all(f32[32,1,128]{2,1,0:T(1,128)S(1)} %bitcast.5), channel_id=1, replica_groups=mesh['gz'=8,'gy'=4] {'gz','gy'}, dimensions={0} | all-to-all | bytes 32768 | tf_op jit(solution)/shard_map/all_to_all | solution.py:474
  48.3 2.3 %correction.1 = (f32[16,32,128]{2,1,0:T(8,128)S(1)}, f32[16,32,128]{2,1,0:T(8,128)S(1)}, f32[16,32,128]{2,1,0:T(8,128)S(1)}, f32[16,32,128]{2,1,0:T(8,128)S(1)},...) custom-call(f32[8,128]{1,0:T(8,128)S(1)} %get-tuple-element.31.top_r, ...), custom_call_target="tpu_custom_call" | custom-call | flops 536870912 | bytes 4194304 | tf_op jit(solution)/shard_map/correction/pallas_call | solution.py:476
  50.6 0.1 collective-permute-start.7
  50.7 0.6 collective-permute-start.8
  51.3 1.2 %collective-permute-start.9 = (f32[16,32,128]{2,1,0:T(8,128)S(1)}, f32[16,32,128]{2,1,0:T(8,128)S(1)}, u32[]{:S(2)}, u32[]{:S(2)}) collective-permute-start(f32[16,32,128]{2,1,0:T(8,128)S(1)} %get-tuple-element.52), channel_id=1, source_target_pairs={{0,12},{4,8},{8,4},{12,0},{16,28},{20,24},{24,20},{28,16},{1,13},{... | collective-permute-start | bytes 786440 | tf_op jit(solution)/shard_map/ppermute | solution.py:391
  52.5 0.6 collective-permute-start.10
  53.1 1.1 %collective-permute-start.11 = (f32[16,32,128]{2,1,0:T(8,128)S(1)}, f32[16,32,128]{2,1,0:T(8,128)S(1)}, u32[]{:S(2)}, u32[]{:S(2)}) collective-permute-start(f32[16,32,128]{2,1,0:T(8,128)S(1)} %get-tuple-element.54), channel_id=1, source_target_pairs={{0,20},{4,16},{8,28},{12,24},{16,4},{20,0},{24,12},{28,8},{1,21},{... | collective-permute-start | bytes 786440 | tf_op jit(solution)/shard_map/ppermute | solution.py:391
  54.2 0.0 collective-permute-done.7.refs_1_
  54.2 0.6 collective-permute-start.12
  54.8 5.1 %collective-permute-done.8.refs_2_ = f32[16,32,128]{2,1,0:T(8,128)S(1)} collective-permute-done((f32[16,32,128]{2,1,0:T(8,128)S(1)}, f32[16,32,128]{2,1,0:T(8,128)S(1)}, u32[]{:S(2)}, u32[]{:S(2)}) %collective-permute-start.8) | collective-permute-done | bytes 262176 | tf_op jit(solution)/shard_map/ppermute | solution.py:391
  59.8 0.0 collective-permute-start.13
  59.8 4.7 %collective-permute-done.9.refs_3_ = f32[16,32,128]{2,1,0:T(8,128)S(1)} collective-permute-done((f32[16,32,128]{2,1,0:T(8,128)S(1)}, f32[16,32,128]{2,1,0:T(8,128)S(1)}, u32[]{:S(2)}, u32[]{:S(2)}) %collective-permute-start.9) | collective-permute-done | bytes 262176 | tf_op jit(solution)/shard_map/ppermute | solution.py:391
  64.6 0.0 copy-done
  64.6 2.3 %add_correction.3.refs_0_ = f32[16,512,128]{2,1,0:T(8,128)} custom-call(s32[8,8]{1,0:T(8,128)S(1)} %copy-done.2, f32[16,512,128]{2,1,0:T(8,128)S(1)} %copy-done, f32[16,32,128]{2,1,0:T(8,128)S(1)} %get-tuple-element.49.refs_0_, f32[16,32,128]{2,1,0:T(8,128)S(1)} %collective-permute-done.7.refs_1_, f32[16,32,128]{2,1,0:T(8,128)S(1)} %collective-permute-done.8.refs_2_, ...), custom_call_target="tpu_custom_call" | custom-call | flops 262144 | bytes 5242880 | tf_op jit(solution)/shard_map/add_correction/pallas_call | solution.py:496
  66.9 0.0 collective-permute-done.10.refs_1_
  66.9 1.6 %add_correction.4.refs_0_ = f32[16,512,128]{2,1,0:T(8,128)} custom-call(s32[8,8]{1,0:T(8,128)S(1)} %copy-done.2, f32[16,512,128]{2,1,0:T(8,128)S(1)} %copy-done, f32[16,512,128]{2,1,0:T(8,128)} %add_correction.3.refs_0_, f32[16,32,128]{2,1,0:T(8,128)S(1)} %collective-permute-done.10.refs_1_), custom_call_target="tpu_custom_call", output_to_operand_aliasing={{}: (2, {})} | custom-call | flops 262144 | bytes 1310720 | tf_op jit(solution)/shard_map/add_correction/pallas_call | solution.py:496
  68.5 8.9 %collective-permute-done.11.refs_1_ = f32[16,32,128]{2,1,0:T(8,128)S(1)} collective-permute-done((f32[16,32,128]{2,1,0:T(8,128)S(1)}, f32[16,32,128]{2,1,0:T(8,128)S(1)}, u32[]{:S(2)}, u32[]{:S(2)}) %collective-permute-start.11) | collective-permute-done | bytes 262176 | tf_op jit(solution)/shard_map/ppermute | solution.py:391
  77.4 0.0 collective-permute-done.12.refs_2_
  77.4 0.0 collective-permute-done.13.refs_3_
  77.4 2.1 %add_correction.5 = f32[16,512,128]{2,1,0:T(8,128)} custom-call(s32[8,8]{1,0:T(8,128)S(1)} %copy-done.2, f32[16,512,128]{2,1,0:T(8,128)S(1)} %copy-done, f32[16,512,128]{2,1,0:T(8,128)} %add_correction.4.refs_0_, f32[16,32,128]{2,1,0:T(8,128)S(1)} %collective-permute-done.11.refs_1_, ...), custom_call_target="tpu_custom_call", output_to_operand_aliasing={{}: (2, {})} | custom-call | flops 262144 | bytes 3932160 | tf_op jit(solution)/shard_map/add_correction/pallas_call | solution.py:496
Async XLA Ops:
  0.0 18.8 %copy-start.2 = (s32[8,8]{1,0:T(8,128)S(1)}, s32[8,8]{1,0:T(8,128)}, u32[]{:S(2)}) copy-start(s32[8,8]{1,0:T(8,128)} %mask_ref.9) | copy-start | bytes 772
  0.0 15.8 %copy-start.4 = (f32[16,31]{1,0:T(8,128)S(1)}, f32[16,31]{1,0:T(8,128)}, u32[]{:S(2)}) copy-start(f32[16,31]{1,0:T(8,128)} %kernels_ref.1) | copy-start | bytes 5956
  0.0 15.8 %copy-start.3 = (s32[4,8,8]{2,1,0:T(8,128)S(1)}, s32[4,8,8]{2,1,0:T(8,128)}, u32[]{:S(2)}) copy-start(s32[4,8,8]{2,1,0:T(8,128)} %index_ref.1) | copy-start | bytes 3076
  3.6 6.7 %collective-permute-start = (f32[16,32,128]{2,1,0:T(8,128)}, f32[16,32,128]{2,1,0:T(8,128)S(1)}, u32[]{:S(2)}, u32[]{:S(2)}) collective-permute-start(f32[16,32,128]{2,1,0:T(8,128)} %get-tuple-element.37), channel_id=1, source_target_pairs={{0,4},{4,0},{8,12},{12,8},{16,20},{20,16},{24,28},{28,24},{1,5},{5... | collective-permute-start | bytes 786440 | tf_op jit(solution)/shard_map/ppermute | solution.py:391
  4.1 10.9 %collective-permute-start.2 = (f32[16,32,128]{2,1,0:T(8,128)}, f32[16,32,128]{2,1,0:T(8,128)S(1)}, u32[]{:S(2)}, u32[]{:S(2)}) collective-permute-start(f32[16,32,128]{2,1,0:T(8,128)} %get-tuple-element.41), channel_id=1, source_target_pairs={{0,24},{4,28},{8,16},{12,20},{16,8},{20,12},{24,0},{28,4},{1,25},{... | collective-permute-start | bytes 786440 | tf_op jit(solution)/shard_map/ppermute | solution.py:391
  7.6 20.1 %collective-permute-start.1 = (f32[16,32,128]{2,1,0:T(8,128)}, f32[16,32,128]{2,1,0:T(8,128)S(1)}, u32[]{:S(2)}, u32[]{:S(2)}) collective-permute-start(f32[16,32,128]{2,1,0:T(8,128)} %get-tuple-element.39), channel_id=1, source_target_pairs={{0,8},{4,12},{8,0},{12,4},{16,24},{20,28},{24,16},{28,20},{1,9},{5... | collective-permute-start | bytes 786440 | tf_op jit(solution)/shard_map/ppermute | solution.py:391
  8.2 19.5 %collective-permute-start.4 = (f32[16,32,128]{2,1,0:T(8,128)}, f32[16,32,128]{2,1,0:T(8,128)S(1)}, u32[]{:S(2)}, u32[]{:S(2)}) collective-permute-start(f32[16,32,128]{2,1,0:T(8,128)} %get-tuple-element.43), channel_id=1, source_target_pairs={{0,16},{4,20},{8,24},{12,28},{16,0},{20,4},{24,8},{28,12},{1,17},{... | collective-permute-start | bytes 786440 | tf_op jit(solution)/shard_map/ppermute | solution.py:391
  8.3 19.4 %collective-permute-start.6 = (f32[16,32,128]{2,1,0:T(8,128)}, f32[16,32,128]{2,1,0:T(8,128)S(1)}, u32[]{:S(2)}, u32[]{:S(2)}) collective-permute-start(f32[16,32,128]{2,1,0:T(8,128)} %get-tuple-element.46), channel_id=1, source_target_pairs={{0,28},{4,24},{8,20},{12,16},{16,12},{20,8},{24,4},{28,0},{1,29},{... | collective-permute-start | bytes 786440 | tf_op jit(solution)/shard_map/ppermute | solution.py:391
  10.3 21.2 %collective-permute-start.5 = (f32[16,32,128]{2,1,0:T(8,128)}, f32[16,32,128]{2,1,0:T(8,128)S(1)}, u32[]{:S(2)}, u32[]{:S(2)}) collective-permute-start(f32[16,32,128]{2,1,0:T(8,128)} %get-tuple-element.44), channel_id=1, source_target_pairs={{0,20},{4,16},{8,28},{12,24},{16,4},{20,0},{24,12},{28,8},{1,21},{... | collective-permute-start | bytes 786440 | tf_op jit(solution)/shard_map/ppermute | solution.py:391
  15.0 16.5 %collective-permute-start.3 = (f32[16,32,128]{2,1,0:T(8,128)}, f32[16,32,128]{2,1,0:T(8,128)S(1)}, u32[]{:S(2)}, u32[]{:S(2)}) collective-permute-start(f32[16,32,128]{2,1,0:T(8,128)} %get-tuple-element.42), channel_id=1, source_target_pairs={{0,12},{4,8},{8,4},{12,0},{16,28},{20,24},{24,20},{28,16},{1,13},{... | collective-permute-start | bytes 786440 | tf_op jit(solution)/shard_map/ppermute | solution.py:391
  18.8 12.7 %copy-start.1 = (f32[16,32,128]{2,1,0:T(8,128)S(1)}, f32[16,32,128]{2,1,0:T(8,128)}, u32[]{:S(2)}) copy-start(f32[16,32,128]{2,1,0:T(8,128)} %get-tuple-element.35.refs_0_) | copy-start | bytes 786436
  27.7 36.9 %copy-start = (f32[16,512,128]{2,1,0:T(8,128)S(1)}, f32[16,512,128]{2,1,0:T(8,128)}, u32[]{:S(2)}) copy-start(f32[16,512,128]{2,1,0:T(8,128)} %init_ref.7) | copy-start | bytes 12582916
  50.6 3.6 %collective-permute-start.7 = (f32[16,32,128]{2,1,0:T(8,128)S(1)}, f32[16,32,128]{2,1,0:T(8,128)S(1)}, u32[]{:S(2)}, u32[]{:S(2)}) collective-permute-start(f32[16,32,128]{2,1,0:T(8,128)S(1)} %get-tuple-element.50), channel_id=1, source_target_pairs={{0,4},{4,0},{8,12},{12,8},{16,20},{20,16},{24,28},{28,24},{1,5},{5... | collective-permute-start | bytes 786440 | tf_op jit(solution)/shard_map/ppermute | solution.py:391
  50.7 9.2 %collective-permute-start.8 = (f32[16,32,128]{2,1,0:T(8,128)S(1)}, f32[16,32,128]{2,1,0:T(8,128)S(1)}, u32[]{:S(2)}, u32[]{:S(2)}) collective-permute-start(f32[16,32,128]{2,1,0:T(8,128)S(1)} %get-tuple-element.51), channel_id=1, source_target_pairs={{0,8},{4,12},{8,0},{12,4},{16,24},{20,28},{24,16},{28,20},{1,9},{5... | collective-permute-start | bytes 786440 | tf_op jit(solution)/shard_map/ppermute | solution.py:391
  51.3 13.2 %collective-permute-start.9 = (f32[16,32,128]{2,1,0:T(8,128)S(1)}, f32[16,32,128]{2,1,0:T(8,128)S(1)}, u32[]{:S(2)}, u32[]{:S(2)}) collective-permute-start(f32[16,32,128]{2,1,0:T(8,128)S(1)} %get-tuple-element.52), channel_id=1, source_target_pairs={{0,12},{4,8},{8,4},{12,0},{16,28},{20,24},{24,20},{28,16},{1,13},{... | collective-permute-start | bytes 786440 | tf_op jit(solution)/shard_map/ppermute | solution.py:391
  52.5 14.3 %collective-permute-start.10 = (f32[16,32,128]{2,1,0:T(8,128)S(1)}, f32[16,32,128]{2,1,0:T(8,128)S(1)}, u32[]{:S(2)}, u32[]{:S(2)}) collective-permute-start(f32[16,32,128]{2,1,0:T(8,128)S(1)} %get-tuple-element.53), channel_id=1, source_target_pairs={{0,16},{4,20},{8,24},{12,28},{16,0},{20,4},{24,8},{28,12},{1,17},{... | collective-permute-start | bytes 786440 | tf_op jit(solution)/shard_map/ppermute | solution.py:391
  53.1 24.2 %collective-permute-start.11 = (f32[16,32,128]{2,1,0:T(8,128)S(1)}, f32[16,32,128]{2,1,0:T(8,128)S(1)}, u32[]{:S(2)}, u32[]{:S(2)}) collective-permute-start(f32[16,32,128]{2,1,0:T(8,128)S(1)} %get-tuple-element.54), channel_id=1, source_target_pairs={{0,20},{4,16},{8,28},{12,24},{16,4},{20,0},{24,12},{28,8},{1,21},{... | collective-permute-start | bytes 786440 | tf_op jit(solution)/shard_map/ppermute | solution.py:391
  54.2 23.1 %collective-permute-start.12 = (f32[16,32,128]{2,1,0:T(8,128)S(1)}, f32[16,32,128]{2,1,0:T(8,128)S(1)}, u32[]{:S(2)}, u32[]{:S(2)}) collective-permute-start(f32[16,32,128]{2,1,0:T(8,128)S(1)} %get-tuple-element.55), channel_id=1, source_target_pairs={{0,24},{4,28},{8,16},{12,20},{16,8},{20,12},{24,0},{28,4},{1,25},{... | collective-permute-start | bytes 786440 | tf_op jit(solution)/shard_map/ppermute | solution.py:391
  59.8 17.5 %collective-permute-start.13 = (f32[16,32,128]{2,1,0:T(8,128)S(1)}, f32[16,32,128]{2,1,0:T(8,128)S(1)}, u32[]{:S(2)}, u32[]{:S(2)}) collective-permute-start(f32[16,32,128]{2,1,0:T(8,128)S(1)} %get-tuple-element.56), channel_id=1, source_target_pairs={{0,28},{4,24},{8,20},{12,16},{16,12},{20,8},{24,4},{28,0},{1,29},{... | collective-permute-start | bytes 786440 | tf_op jit(solution)/shard_map/ppermute | solution.py:391

commit v3 on v2

--- a/solution.py
+++ b/solution.py
@@ -13,7 +13,6 @@
 HIGHEST = lax.Precision.HIGHEST
 damping = 1.0
 MIB = 1 << 20
-UNROLL = 4
 IN_FLIGHT = 5
 
 
@@ -39,6 +38,30 @@
     return both[:rows] + both[rows:]
 
 
+def slots(tiles):
+    high = (tiles.bit_length() - 2) // 2
+
+    def swapped(k):
+        across = k >> 1
+        if 4 ** high * 2 != tiles:
+            return k
+        return ((((across & (2**high - 1)) << high) | (across >> high)) << 1) | (k & 1)
+
+    same, other = list(range(2, tiles, 2)), list(range(3, tiles, 2))
+    order = [0, 1] + same + other
+    return [(k, swapped(k)) for k in order]
+
+
+def receiver(me, slot):
+    even, odd = slot
+    return jnp.bitwise_xor(me, even if even == odd else jnp.where(me % 2 == 0, even, odd))
+
+
+def sender(me, slot):
+    even, odd = slot
+    return receiver(me, slot if even % 2 == 0 else (odd, even))
+
+
 def tissue_half(mask_ref, tile):
     return mask_ref[tile, 2 * lax.axis_index("gy") + 1]
 
@@ -48,31 +71,32 @@
     return (lane >= shape[-1] // 2) == (half == 1)
 
 
-def pack_kernel(mask_ref, init_ref, *refs):
-    count = len(refs) - 4
+def pack_kernel(targets, mask_ref, init_ref, *refs):
+    count = len(targets)
     out_refs, (staged, flags, sems, flag_sem) = refs[:count], refs[count:]
-    slab, columns, lanes = out_refs[0].shape
-    width = 2 * columns
+    _, slab, width, lanes = staged.shape
+    columns = width // 2
     me = lax.axis_index("gz")
 
-    def copy(k):
-        start = pl.multiple_of(jnp.bitwise_xor(me, k) * width, width)
+    def copy(n):
+        start = pl.multiple_of(receiver(me, targets[n]) * width, width)
         return pltpu.make_async_copy(
-            init_ref.at[:, pl.ds(start, width), :], staged.at[k], sems.at[k]
+            init_ref.at[:, pl.ds(start, width), :], staged.at[n], sems.at[n]
         )
 
     flag_copy = pltpu.make_async_copy(mask_ref, flags, flag_sem)
     flag_copy.start()
-    for k in range(count):
-        copy(k).start()
+    for n in range(count):
+        copy(n).start()
     flag_copy.wait()
-    for k in range(count):
-        copy(k).wait()
-        half = tissue_half(flags, jnp.bitwise_xor(me, k))
-        here = tissue_lanes((slab, columns, lanes), half)
-        first = staged[k, :, :columns, :]
-        second = pltpu.roll(staged[k, :, columns:, :], lanes // 2, 2)
-        out_refs[k][...] = jnp.where(here, first, second)
+    for n in range(count):
+        copy(n).wait()
+        half = tissue_half(flags, receiver(me, targets[n]))
+        here = tissue_lanes((columns, lanes), half)
+        for z in range(slab):
+            first = staged[n, z, :columns, :]
+            second = pltpu.roll(staged[n, z, columns:, :], lanes // 2, 1)
+            out_refs[n][pl.ds(z, columns, stride=slab), :] = jnp.where(here, first, second)
 
 
 def tables_kernel(
@@ -129,7 +153,10 @@
     tiles = xbands
     slab = depth // tiles
     swapped = jnp.concatenate(
-        [square[pl.ds(pl.multiple_of(jnp.bitwise_xor(me, k) * slab, slab), slab), :] for k in range(tiles)],
+        [
+            square[pl.ds(pl.multiple_of(sender(me, slot) * slab, slab), slab), :]
+            for slot in slots(tiles)
+        ],
         axis=0,
     )
     gram_ref[...] = left_operand(swapped.T)
@@ -205,31 +232,24 @@
 def residual_kernel(gram_ref, poly_ref, projected_ref, *refs):
     count = len(refs) - 3
     chunks, (residual_ref, moments_ref, square_ref) = refs[:count], refs[count:]
-    slab, columns, lanes = chunks[0].shape
-    depth = poly_ref.shape[-1]
+    columns, depth, lanes = projected_ref.shape
+    slab = depth // count
     square_ref[...] = jnp.zeros_like(square_ref)
-    flat = [chunk.reshape(slab * columns, lanes) for chunk in chunks]
 
     def field(x):
-        return jnp.concatenate([ref[pl.ds(x, slab, stride=columns), :] for ref in flat], axis=0)
-
-    @pl.loop(0, columns // 2, step=UNROLL)
-    def _(first):
-        total = None
-        for i in range(UNROLL):
-            pair = first + i
-            x = 2 * pair
-            image = product(
-                gram_ref[...], right_operand(jnp.concatenate([field(x), field(x + 1)], axis=1))
-            )
-            start = jnp.concatenate([projected_ref[x], projected_ref[x + 1]], axis=1)
-            both = right_operand(start - image)
-            residual_ref[pair] = both
-            square = lax.dot_general(
-                both, both, (((1,), (1,)), ((), ())), preferred_element_type=jnp.float32
-            )
-            total = square if total is None else total + square
-        square_ref[...] += total
+        return jnp.concatenate([ref[x * slab : (x + 1) * slab, :] for ref in chunks], axis=0)
+
+    for pair in range(columns // 2):
+        x = 2 * pair
+        image = product(
+            gram_ref[...], right_operand(jnp.concatenate([field(x), field(x + 1)], axis=1))
+        )
+        start = jnp.concatenate([projected_ref[x], projected_ref[x + 1]], axis=1)
+        both = right_operand(start - image)
+        residual_ref[pair] = both
+        square_ref[...] += lax.dot_general(
+            both, both, (((1,), (1,)), ((), ())), preferred_element_type=jnp.float32
+        )
 
     square = square_ref[...]
     square = (square[:depth, :depth] + square[depth:, depth:]) + (
@@ -294,7 +314,10 @@
 def correct_kernel(top_ref, moments_ref, poly_ref, residual_ref, *refs):
     count = len(refs) - 2
     out_refs, (matrix_ref, left_ref) = refs[:count], refs[count:]
-    slab, columns, lanes = out_refs[0].shape
+    depth = matrix_ref.shape[0]
+    slab = depth // count
+    pairs, _, lanes = residual_ref.shape
+    lanes = lanes // 2
     me = lax.axis_index("gz")
     row = jnp.sum(moments_ref[...], axis=0, keepdims=True)
     lane = lax.broadcasted_iota(jnp.int32, row.shape, 1)
@@ -310,57 +333,51 @@
     left_ref[...] = left_operand(
         jnp.concatenate(
             [
-                matrix_ref[pl.ds(pl.multiple_of(jnp.bitwise_xor(me, k) * slab, slab), slab), :]
-                for k in range(count)
+                matrix_ref[pl.ds(pl.multiple_of(receiver(me, slot) * slab, slab), slab), :]
+                for slot in slots(count)
             ],
             axis=0,
         )
     )
-    flat = [ref.reshape(slab * columns, lanes) for ref in out_refs]
-
-    @pl.loop(0, columns // 2, step=UNROLL)
-    def _(first):
-        for i in range(UNROLL):
-            pair = first + i
-            result = product(left_ref[...], residual_ref[pair])
-            for k in range(count):
-                rows = result[slab * k : slab * (k + 1)]
-                for side in range(2):
-                    flat[k][pl.ds(2 * pair + side, slab, stride=columns), :] = rows[
-                        :, lanes * side : lanes * (side + 1)
-                    ]
-
-
-def unpack_kernel(group, aliased, mask_ref, init_ref, *refs):
-    if aliased:
-        refs = refs[1:]
-    chunks, (out_ref, staged, in_sems, out_sems) = refs[:-4], refs[-4:]
-    slab, columns, lanes = chunks[0].shape
-    width = 2 * columns
+    for pair in range(pairs):
+        result = product(left_ref[...], residual_ref[pair])
+        for k in range(count):
+            rows = result[slab * k : slab * (k + 1)]
+            for side in range(2):
+                start = (2 * pair + side) * slab
+                out_refs[k][start : start + slab, :] = rows[:, lanes * side : lanes * (side + 1)]
+
+
+def unpack_kernel(group, mask_ref, init_ref, *refs):
+    count = len(group)
+    chunks, (out_ref, staged, sems) = refs[:count], refs[-3:]
+    _, slab, width, lanes = staged.shape
+    columns = width // 2
     me = lax.axis_index("gz")
-
-    def tile(k):
-        return jnp.bitwise_xor(me, k)
-
-    def columns_of(ref, k):
-        return ref.at[:, pl.ds(pl.multiple_of(tile(k) * width, width), width), :]
-
-    loads = [
-        pltpu.make_async_copy(columns_of(init_ref, k), staged.at[n], in_sems.at[n])
-        for n, k in enumerate(group)
-    ]
-    stores = [
-        pltpu.make_async_copy(staged.at[n], columns_of(out_ref, k), out_sems.at[n])
-        for n, k in enumerate(group)
-    ]
-    for load in loads:
-        load.start()
-    for n, k in enumerate(group):
-        here = tissue_lanes((slab, columns, lanes), tissue_half(mask_ref, tile(k)))
-        change = chunks[n][...]
-        loads[n].wait()
-        staged[n, :, :columns, :] += jnp.where(here, change, 0.0)
-        staged[n, :, columns:, :] += pltpu.roll(jnp.where(here, 0.0, change), lanes // 2, 2)
+    flags = mask_ref[...]
+    block = lax.broadcasted_iota(jnp.int32, flags.shape, 1)
+    region = lax.broadcasted_iota(jnp.int32, flags.shape, 0)
+    lane = lax.broadcasted_iota(jnp.int32, (columns, lanes), 1)
+    stores = []
+    for n, slot in enumerate(group):
+        tile = sender(me, slot)
+        start = pl.multiple_of(tile * width, width)
+        chosen = (region == tile) & (block == 2 * lax.axis_index("gy") + 1)
+        half = jnp.max(jnp.where(chosen, flags, 0), keepdims=True)
+        here = (lane // (lanes // 2)) == half
+        for z in range(slab):
+            change = chunks[n][pl.ds(z, columns, stride=slab), :]
+            staged[n, z, :columns, :] = init_ref[z, pl.ds(start, columns), :] + jnp.where(
+                here, change, 0.0
+            )
+            staged[n, z, columns:, :] = init_ref[
+                z, pl.ds(pl.multiple_of(start + columns, columns), columns), :
+            ] + pltpu.roll(jnp.where(here, 0.0, change), lanes // 2, 1)
+        stores.append(
+            pltpu.make_async_copy(
+                staged.at[n], out_ref.at[:, pl.ds(start, width), :], sems.at[n]
+            )
+        )
         stores[n].start()
     for store in stores:
         store.wait()
@@ -385,36 +402,40 @@
     columns = width // 2
     f32, bf16 = jnp.float32, jnp.bfloat16
     shape = jax.ShapeDtypeStruct
-    chunk = shape((slab, columns, lanes), f32)
-
-    def send(block, k):
-        return lax.ppermute(block, "gz", [(j, j ^ k) for j in range(tiles)])
-
-    packed = pl.pallas_call(
-        pack_kernel,
-        name="pack_blocks",
-        out_shape=[chunk] * tiles,
-        in_specs=[HBM, HBM],
-        out_specs=[VMEM] * tiles,
-        scratch_shapes=[
-            pltpu.VMEM((tiles, slab, width, lanes), f32),
-            pltpu.SMEM(mask.shape, jnp.int32),
-            pltpu.SemaphoreType.DMA((tiles,)),
-            pltpu.SemaphoreType.DMA,
-        ],
-        compiler_params=pltpu.CompilerParams(vmem_limit_bytes=60 * MIB),
-        cost_estimate=cost(init.size, 6 * init.size),
-    )(mask, init)
-
-    order = [1] + [k for k in range(tiles - 2, 1, -1) if k % 2 == 0]
-    order += [k for k in range(tiles - 1, 1, -1) if k % 2 == 1]
-    fields = [packed[0]] + [None] * (tiles - 1)
-    for n, k in enumerate(order):
-        block = packed[k]
-        if n >= IN_FLIGHT:
-            before = order[n - IN_FLIGHT]
-            block, fields[before] = lax.optimization_barrier((block, fields[before]))
-        fields[k] = send(block, k)
+    chunk = shape((columns * slab, lanes), f32)
+
+    plan = slots(tiles)
+
+    def exchange(blocks):
+        arrived = list(blocks)
+        for n in range(1, tiles):
+            block = blocks[n]
+            if n > IN_FLIGHT:
+                before = n - IN_FLIGHT
+                block, arrived[before] = lax.optimization_barrier((block, arrived[before]))
+            route = [(j, j ^ plan[n][j % 2]) for j in range(tiles)]
+            arrived[n] = lax.ppermute(block, "gz", route)
+        return arrived
+
+    packed = []
+    for targets in (plan[1:4], [plan[0]] + plan[4:]):
+        size = len(targets)
+        packed += pl.pallas_call(
+            functools.partial(pack_kernel, targets),
+            name="pack_blocks",
+            out_shape=[chunk] * size,
+            in_specs=[HBM, HBM],
+            out_specs=[VMEM] * size,
+            scratch_shapes=[
+                pltpu.VMEM((size, slab, width, lanes), f32),
+                pltpu.SMEM(mask.shape, jnp.int32),
+                pltpu.SemaphoreType.DMA((size,)),
+                pltpu.SemaphoreType.DMA,
+            ],
+            compiler_params=pltpu.CompilerParams(vmem_limit_bytes=60 * MIB),
+            cost_estimate=cost(init.size, 6 * init.size * size // tiles),
+        )(mask, init)
+    fields = exchange([packed[3]] + packed[:3] + packed[4:])
 
     poly_shape = shape((MOMENTS, depth, depth), f32)
     left, gram, poly, top = pl.pallas_call(
@@ -486,28 +507,27 @@
         compiler_params=pltpu.CompilerParams(vmem_limit_bytes=16 * MIB),
         cost_estimate=cost(8 * depth * depth * columns * lanes, 8 * depth * columns * lanes),
     )(top, moments, poly, residual)
-    changes = [changes[0]] + [send(changes[k], k) for k in range(1, tiles)]
-
-    cut = [0, tiles // 2, tiles // 2 + 1, tiles]
-    groups = [list(range(first, last)) for first, last in zip(cut, cut[1:])]
+    changes = exchange(changes)
+
     solved = None
-    for group in groups:
-        size = len(group)
+    cut = [0, tiles // 2, tiles - 2, tiles]
+    for first, last in zip(cut, cut[1:]):
+        size = last - first
+        earlier = [] if solved is None else [solved]
         solved = pl.pallas_call(
-            functools.partial(unpack_kernel, group, solved is not None),
+            functools.partial(unpack_kernel, plan[first:last]),
             name="add_correction",
             out_shape=shape(init.shape, f32),
-            in_specs=[SMEM, ANY] + [ANY] * (solved is not None) + [VMEM] * size,
+            in_specs=[VMEM] * (2 + size) + [ANY] * len(earlier),
             out_specs=ANY,
-            input_output_aliases={} if solved is None else {2: 0},
+            input_output_aliases={2 + size: 0} if earlier else {},
             scratch_shapes=[
                 pltpu.VMEM((size, slab, width, lanes), f32),
                 pltpu.SemaphoreType.DMA((size,)),
-                pltpu.SemaphoreType.DMA((size,)),
             ],
             compiler_params=pltpu.CompilerParams(vmem_limit_bytes=16 * MIB),
-            cost_estimate=cost(init.size // 4, 5 * init.size // 4 * size),
-        )(mask, init, *([] if solved is None else [solved]), *[changes[k] for k in group])
+            cost_estimate=cost(init.size // 4, 5 * init.size * size // tiles),
+        )(mask, init, *changes[first:last], *earlier)
     return solved
 
 

time: 79.6 us -> 72.9 us (0.916)
  waiting for transfers between devices: 26.1 us -> 21.1 us
  Pallas kernels: 27.5 us -> 24.2 us
  starting transfers between devices: 12.6 us -> 13.6 us
    ppermute x14, waiting for transfers between devices: 26.1 us -> 21.1 us  [exchange(): arrived[n] = lax.ppermute(block, 'gz', route)]
    pallas_call x1, Pallas kernels: 3.8 us -> 1.61 us  [local(): pl.pallas_call(residual_kernel, name='first_residual', out_shape=[shape((...]
    pallas_call x1, Pallas kernels: 2.25 us -> 0.95 us  [local(): pl.pallas_call(correct_kernel, name='correction', out_shape=[chunk] * til...]
    ppermute x14, starting transfers between devices: 12.6 us -> 13.6 us  [exchange(): arrived[n] = lax.ppermute(block, 'gz', route)]
    pallas_call x4 -> x5, Pallas kernels: 9.55 us -> 9.79 us  [the longest x2 5.23 us: local(): pl.pallas_call(functools.partial(pack_kernel, targets), name='pack_blocks...]
  transfers between devices with their start and end apart: 14 -> 14, of which waited for: 5 -> 7; matrix products, arithmetic and copies ran while one was open for 0% -> 0% of each run, Pallas kernels for 20% -> 25%
where the time goes in v3:
time: 72.9 us; the launch traced here: 72.7 us
  Pallas kernels  24.2 us (33%)
  waiting for transfers between devices  21.1 us (29%)
  starting transfers between devices  13.6 us (19%)
  blocking collectives  13.6 us (19%)
    ppermute x14, waiting for transfers between devices, exchange(): arrived[n] = lax.ppermute(block, 'gz', route)  21.1 us
    all_to_all x1, blocking collectives, local(): lax.all_to_all(moments, ('gz', 'gy'), split_axis=0, concat_axis=0, tiled=...  13.6 us
    ppermute x14, starting transfers between devices, exchange(): arrived[n] = lax.ppermute(block, 'gz', route)  13.6 us
    pallas_call x1, Pallas kernels, local(): pl.pallas_call(project_kernel, name='project_views', out_shape=shape((col...  8.83 us
    pallas_call x2, Pallas kernels, local(): pl.pallas_call(functools.partial(pack_kernel, targets), name='pack_blocks...  5.23 us
    pallas_call x3, Pallas kernels, local(): pl.pallas_call(functools.partial(unpack_kernel, plan[first:last]), name='...  4.56 us
    pallas_call x1, Pallas kernels, local(): pl.pallas_call(tables_kernel, name='blur_tables', out_shape=[shape((2 * d...  3.05 us
    pallas_call x1, Pallas kernels, local(): pl.pallas_call(residual_kernel, name='first_residual', out_shape=[shape((...  1.61 us
  transfers between devices with their start and end apart: 14, of which 7 were waited for; matrix products, arithmetic and copies ran while one was open for 0% of the time, Pallas kernels for 25%

profile of v3, /device:TPU:0, one launch (start us, length us, event | category | flops | bytes accessed | tf_op | source)
XLA Modules:
  0.0 72.7 jit_solution(3354170086004817765)
XLA Ops:
  0.0 0.0 copy-start.2
  0.0 0.0 copy-start.4
  0.0 0.0 copy-start.3
  0.0 2.4 %pack_blocks.3 = (f32[512,128]{1,0:T(8,128)}, f32[512,128]{1,0:T(8,128)}, f32[512,128]{1,0:T(8,128)}) custom-call(s32[8,8]{1,0:T(8,128)} %mask_ref.11, f32[16,512,128]{2,1,0:T(8,128)} %init_ref.9), custom_call_target="tpu_custom_call" | custom-call | flops 1048576 | bytes 2359296 | tf_op jit(solution)/shard_map/pack_blocks/pallas_call | solution.py:423
  2.4 0.5 collective-permute-start
  2.9 2.6 %collective-permute-start.1 = (f32[512,128]{1,0:T(8,128)}, f32[512,128]{1,0:T(8,128)S(1)}, u32[]{:S(2)}, u32[]{:S(2)}) collective-permute-start(f32[512,128]{1,0:T(8,128)} %get-tuple-element.44), channel_id=1, source_target_pairs={{0,8},{4,20},{8,0},{12,28},{16,24},{20,4},{24,16},{28,12},{1,9},{5... | collective-permute-start | bytes 786440 | tf_op jit(solution)/shard_map/ppermute | solution.py:417
  5.5 1.5 %collective-permute-start.2 = (f32[512,128]{1,0:T(8,128)}, f32[512,128]{1,0:T(8,128)S(1)}, u32[]{:S(2)}, u32[]{:S(2)}) collective-permute-start(f32[512,128]{1,0:T(8,128)} %get-tuple-element.46), channel_id=1, source_target_pairs={{0,16},{4,12},{8,24},{12,4},{16,0},{20,28},{24,8},{28,20},{1,17},{... | collective-permute-start | bytes 786440 | tf_op jit(solution)/shard_map/ppermute | solution.py:417
  7.0 2.8 %pack_blocks.2 = (f32[512,128]{1,0:T(8,128)}, f32[512,128]{1,0:T(8,128)}, f32[512,128]{1,0:T(8,128)}, f32[512,128]{1,0:T(8,128)}, f32[512,128]{1,0:T(8,128)}) custom-call(s32[8,8]{1,0:T(8,128)} %mask_ref.11, f32[16,512,128]{2,1,0:T(8,128)} %init_ref.9), custom_call_target="tpu_custom_call" | custom-call | flops 1048576 | bytes 3932160 | tf_op jit(solution)/shard_map/pack_blocks/pallas_call | solution.py:423
  9.9 0.1 collective-permute-start.3
  9.9 1.1 %collective-permute-start.4 = (f32[512,128]{1,0:T(8,128)}, f32[512,128]{1,0:T(8,128)S(1)}, u32[]{:S(2)}, u32[]{:S(2)}) collective-permute-start(f32[512,128]{1,0:T(8,128)} %get-tuple-element.48), channel_id=1, source_target_pairs={{0,12},{4,16},{8,4},{12,24},{16,28},{20,0},{24,20},{28,8},{1,13},{... | collective-permute-start | bytes 786440 | tf_op jit(solution)/shard_map/ppermute | solution.py:417
  11.1 0.0 collective-permute-done.refs_1_
  11.1 0.7 %collective-permute-done.1.refs_2_ = f32[512,128]{1,0:T(8,128)S(1)} collective-permute-done((f32[512,128]{1,0:T(8,128)}, f32[512,128]{1,0:T(8,128)S(1)}, u32[]{:S(2)}, u32[]{:S(2)}) %collective-permute-start.1) | collective-permute-done | bytes 262176 | tf_op jit(solution)/shard_map/ppermute | solution.py:417
  11.8 2.1 %collective-permute-start.6 = (f32[512,128]{1,0:T(8,128)}, f32[512,128]{1,0:T(8,128)S(1)}, u32[]{:S(2)}, u32[]{:S(2)}) collective-permute-start(f32[512,128]{1,0:T(8,128)} %get-tuple-element.50), channel_id=1, source_target_pairs={{0,28},{4,24},{8,20},{12,16},{16,12},{20,8},{24,4},{28,0},{1,29},{... | collective-permute-start | bytes 786440 | tf_op jit(solution)/shard_map/ppermute | solution.py:417
  13.9 1.5 %collective-permute-start.5 = (f32[512,128]{1,0:T(8,128)}, f32[512,128]{1,0:T(8,128)S(1)}, u32[]{:S(2)}, u32[]{:S(2)}) collective-permute-start(f32[512,128]{1,0:T(8,128)} %get-tuple-element.49), channel_id=1, source_target_pairs={{0,20},{4,8},{8,28},{12,0},{16,4},{20,24},{24,12},{28,16},{1,21},{... | collective-permute-start | bytes 786440 | tf_op jit(solution)/shard_map/ppermute | solution.py:417
  15.4 0.0 copy-done.4
  15.4 0.0 copy-done.3
  15.4 3.0 %blur_tables.1 = (bf16[256,1024]{1,0:T(8,128)(2,1)S(1)}, bf16[256,256]{1,0:T(8,128)(2,1)S(1)}, f32[8,128,128]{2,1,0:T(8,128)S(1)}, f32[8,128]{1,0:T(8,128)S(1)}) custom-call(s32[4,8,8]{2,1,0:T(8,128)S(1)} %copy-done.3, f32[16,31]{1,0:T(8,128)S(1)} %copy-done.4), custom_call_target="tpu_custom_call" | custom-call | flops 503316480 | bytes 4194304 | tf_op jit(solution)/shard_map/blur_tables/pallas_call | solution.py:441
  18.5 0.0 copy-done.2
  18.5 0.0 copy-start.1
  18.5 8.8 %project_views.1.projected_ref = f32[32,128,128]{2,1,0:T(8,128)S(1)} custom-call(s32[8,8]{1,0:T(8,128)S(1)} %copy-done.2, bf16[256,1024]{1,0:T(8,128)(2,1)S(1)} %get-tuple-element.38.left_ref, f32[4,128,64,128]{3,2,1,0:T(8,128)} %measured_ref.1), custom_call_target="tpu_custom_call" | custom-call | flops 2147483648 | bytes 16777216 | tf_op jit(solution)/shard_map/project_views/pallas_call | solution.py:463
  27.3 0.0 copy-start
  27.3 0.0 collective-permute-done.2.refs_3_
  27.3 0.0 collective-permute-done.3.refs_4_
  27.4 0.0 collective-permute-done.4.refs_5_
  27.4 1.4 %collective-permute-done.6.refs_7_ = f32[512,128]{1,0:T(8,128)S(1)} collective-permute-done((f32[512,128]{1,0:T(8,128)}, f32[512,128]{1,0:T(8,128)S(1)}, u32[]{:S(2)}, u32[]{:S(2)}) %collective-permute-start.6) | collective-permute-done | bytes 262176 | tf_op jit(solution)/shard_map/ppermute | solution.py:417
  28.7 0.2 collective-permute-done.5.refs_6_
  28.9 0.0 copy-done.1
  28.9 1.6 %first_residual.1 = (bf16[16,256,256]{2,1,0:T(8,128)(2,1)S(1)}, f32[32,128]{1,0:T(8,128)S(1)}) custom-call(bf16[256,256]{1,0:T(8,128)(2,1)S(1)} %get-tuple-element.36.gram_ref, f32[8,128,128]{2,1,0:T(8,128)S(1)} %get-tuple-element.37.poly_ref, f32[32,128,128]{2,1,0:T(8,128)S(1)} %project_views.1.projected_ref, f32[512,128]{1,0:T(8,128)S(1)} %copy-done.1, ...), custom_call_target="tpu_custom_call" | custom-call | flops 1073741824 | bytes 6291456 | tf_op jit(solution)/shard_map/first_residual/pallas_call | solution.py:479
  30.5 13.6 %all_to_all.11 = f32[32,1,128]{2,1,0:T(1,128)S(1)} all-to-all(f32[32,1,128]{2,1,0:T(1,128)S(1)} %bitcast.5), channel_id=1, replica_groups=mesh['gz'=8,'gy'=4] {'gz','gy'}, dimensions={0} | all-to-all | bytes 32768 | tf_op jit(solution)/shard_map/all_to_all | solution.py:495
  44.1 0.9 %correction.1 = (f32[512,128]{1,0:T(8,128)S(1)}, f32[512,128]{1,0:T(8,128)S(1)}, f32[512,128]{1,0:T(8,128)S(1)}, f32[512,128]{1,0:T(8,128)S(1)}, f32[512,128]{1,...) custom-call(f32[8,128]{1,0:T(8,128)S(1)} %get-tuple-element.35.top_ref, ...), custom_call_target="tpu_custom_call" | custom-call | flops 536870912 | bytes 4194304 | tf_op jit(solution)/shard_map/correction/pallas_call | solution.py:497
  45.1 0.1 collective-permute-start.7
  45.2 0.6 collective-permute-start.9
  45.8 1.5 %collective-permute-start.11 = (f32[512,128]{1,0:T(8,128)S(1)}, f32[512,128]{1,0:T(8,128)S(1)}, u32[]{:S(2)}, u32[]{:S(2)}) collective-permute-start(f32[512,128]{1,0:T(8,128)S(1)} %get-tuple-element.59), channel_id=1, source_target_pairs={{0,24},{4,28},{8,16},{12,20},{16,8},{20,12},{24,0},{28,4},{1,25},{... | collective-permute-start | bytes 786440 | tf_op jit(solution)/shard_map/ppermute | solution.py:417
  47.3 0.9 %collective-permute-start.12 = (f32[512,128]{1,0:T(8,128)S(1)}, f32[512,128]{1,0:T(8,128)S(1)}, u32[]{:S(2)}, u32[]{:S(2)}) collective-permute-start(f32[512,128]{1,0:T(8,128)S(1)} %get-tuple-element.60), channel_id=1, source_target_pairs={{0,12},{4,16},{8,4},{12,24},{16,28},{20,0},{24,20},{28,8},{1,13},{... | collective-permute-start | bytes 786440 | tf_op jit(solution)/shard_map/ppermute | solution.py:417
  48.2 0.6 collective-permute-start.13
  48.8 0.0 collective-permute-done.7.refs_1_
  48.8 0.5 collective-permute-start.8
  49.3 4.5 %collective-permute-done.9.refs_2_ = f32[512,128]{1,0:T(8,128)S(1)} collective-permute-done((f32[512,128]{1,0:T(8,128)S(1)}, f32[512,128]{1,0:T(8,128)S(1)}, u32[]{:S(2)}, u32[]{:S(2)}) %collective-permute-start.9) | collective-permute-done | bytes 262176 | tf_op jit(solution)/shard_map/ppermute | solution.py:417
  53.8 0.0 collective-permute-start.10
  53.8 8.1 %collective-permute-done.13.refs_3_ = f32[512,128]{1,0:T(8,128)S(1)} collective-permute-done((f32[512,128]{1,0:T(8,128)S(1)}, f32[512,128]{1,0:T(8,128)S(1)}, u32[]{:S(2)}, u32[]{:S(2)}) %collective-permute-start.13) | collective-permute-done | bytes 262176 | tf_op jit(solution)/shard_map/ppermute | solution.py:417
  61.9 0.0 copy-done
  61.9 1.8 %add_correction.3.refs_2_ = f32[16,512,128]{2,1,0:T(8,128)} custom-call(s32[8,8]{1,0:T(8,128)S(1)} %copy-done.2, f32[16,512,128]{2,1,0:T(8,128)S(1)} %copy-done, f32[512,128]{1,0:T(8,128)S(1)} %get-tuple-element.61.refs_0_, f32[512,128]{1,0:T(8,128)S(1)} %collective-permute-done.7.refs_1_, f32[512,128]{1,0:T(8,128)S(1)} %collective-permute-done.9.refs_2_, ...), custom_call_target="tpu_custom_call" | custom-call | flops 262144 | bytes 2621440 | tf_op jit(solution)/shard_map/add_correction/pallas_call | solution.py:517
  63.7 0.0 collective-permute-done.11.refs_0_
  63.7 0.0 collective-permute-done.12.refs_1_
  63.7 1.4 %add_correction.4.refs_2_ = f32[16,512,128]{2,1,0:T(8,128)} custom-call(s32[8,8]{1,0:T(8,128)S(1)} %copy-done.2, f32[16,512,128]{2,1,0:T(8,128)S(1)} %copy-done, f32[512,128]{1,0:T(8,128)S(1)} %collective-permute-done.11.refs_0_, f32[512,128]{1,0:T(8,128)S(1)} %collective-permute-done.12.refs_1_, ...), custom_call_target="tpu_custom_call", output_to_operand_aliasing={{}: (4, {})} | custom-call | flops 262144 | bytes 1310720 | tf_op jit(solution)/shard_map/add_correction/pallas_call | solution.py:517
  65.1 1.1 %collective-permute-done.8.refs_0_ = f32[512,128]{1,0:T(8,128)S(1)} collective-permute-done((f32[512,128]{1,0:T(8,128)S(1)}, f32[512,128]{1,0:T(8,128)S(1)}, u32[]{:S(2)}, u32[]{:S(2)}) %collective-permute-start.8) | collective-permute-done | bytes 262176 | tf_op jit(solution)/shard_map/ppermute | solution.py:417
  66.2 5.1 %collective-permute-done.10.refs_1_ = f32[512,128]{1,0:T(8,128)S(1)} collective-permute-done((f32[512,128]{1,0:T(8,128)S(1)}, f32[512,128]{1,0:T(8,128)S(1)}, u32[]{:S(2)}, u32[]{:S(2)}) %collective-permute-start.10) | collective-permute-done | bytes 262176 | tf_op jit(solution)/shard_map/ppermute | solution.py:417
  71.3 1.4 %add_correction.5 = f32[16,512,128]{2,1,0:T(8,128)} custom-call(s32[8,8]{1,0:T(8,128)S(1)} %copy-done.2, f32[16,512,128]{2,1,0:T(8,128)S(1)} %copy-done, f32[512,128]{1,0:T(8,128)S(1)} %collective-permute-done.8.refs_0_, f32[512,128]{1,0:T(8,128)S(1)} %collective-permute-done.10.refs_1_, ...), custom_call_target="tpu_custom_call", output_to_operand_aliasing={{}: (4, {})} | custom-call | flops 262144 | bytes 1310720 | tf_op jit(solution)/shard_map/add_correction/pallas_call | solution.py:517
Async XLA Ops:
  0.0 18.5 %copy-start.2 = (s32[8,8]{1,0:T(8,128)S(1)}, s32[8,8]{1,0:T(8,128)}, u32[]{:S(2)}) copy-start(s32[8,8]{1,0:T(8,128)} %mask_ref.11) | copy-start | bytes 772
  0.0 15.4 %copy-start.4 = (f32[16,31]{1,0:T(8,128)S(1)}, f32[16,31]{1,0:T(8,128)}, u32[]{:S(2)}) copy-start(f32[16,31]{1,0:T(8,128)} %kernels_ref.1) | copy-start | bytes 5956
  0.0 15.4 %copy-start.3 = (s32[4,8,8]{2,1,0:T(8,128)S(1)}, s32[4,8,8]{2,1,0:T(8,128)}, u32[]{:S(2)}) copy-start(s32[4,8,8]{2,1,0:T(8,128)} %index_ref.1) | copy-start | bytes 3076
  2.4 8.7 %collective-permute-start = (f32[512,128]{1,0:T(8,128)}, f32[512,128]{1,0:T(8,128)S(1)}, u32[]{:S(2)}, u32[]{:S(2)}) collective-permute-start(f32[512,128]{1,0:T(8,128)} %get-tuple-element.41), channel_id=1, source_target_pairs={{0,4},{4,0},{8,12},{12,8},{16,20},{20,16},{24,28},{28,24},{1,5},{5... | collective-permute-start | bytes 786440 | tf_op jit(solution)/shard_map/ppermute | solution.py:417
  2.9 8.9 %collective-permute-start.1 = (f32[512,128]{1,0:T(8,128)}, f32[512,128]{1,0:T(8,128)S(1)}, u32[]{:S(2)}, u32[]{:S(2)}) collective-permute-start(f32[512,128]{1,0:T(8,128)} %get-tuple-element.44), channel_id=1, source_target_pairs={{0,8},{4,20},{8,0},{12,28},{16,24},{20,4},{24,16},{28,12},{1,9},{5... | collective-permute-start | bytes 786440 | tf_op jit(solution)/shard_map/ppermute | solution.py:417
  5.5 21.9 %collective-permute-start.2 = (f32[512,128]{1,0:T(8,128)}, f32[512,128]{1,0:T(8,128)S(1)}, u32[]{:S(2)}, u32[]{:S(2)}) collective-permute-start(f32[512,128]{1,0:T(8,128)} %get-tuple-element.46), channel_id=1, source_target_pairs={{0,16},{4,12},{8,24},{12,4},{16,0},{20,28},{24,8},{28,20},{1,17},{... | collective-permute-start | bytes 786440 | tf_op jit(solution)/shard_map/ppermute | solution.py:417
  9.9 17.5 %collective-permute-start.3 = (f32[512,128]{1,0:T(8,128)}, f32[512,128]{1,0:T(8,128)S(1)}, u32[]{:S(2)}, u32[]{:S(2)}) collective-permute-start(f32[512,128]{1,0:T(8,128)} %get-tuple-element.47), channel_id=1, source_target_pairs={{0,24},{4,28},{8,16},{12,20},{16,8},{20,12},{24,0},{28,4},{1,25},{... | collective-permute-start | bytes 786440 | tf_op jit(solution)/shard_map/ppermute | solution.py:417
  9.9 17.4 %collective-permute-start.4 = (f32[512,128]{1,0:T(8,128)}, f32[512,128]{1,0:T(8,128)S(1)}, u32[]{:S(2)}, u32[]{:S(2)}) collective-permute-start(f32[512,128]{1,0:T(8,128)} %get-tuple-element.48), channel_id=1, source_target_pairs={{0,12},{4,16},{8,4},{12,24},{16,28},{20,0},{24,20},{28,8},{1,13},{... | collective-permute-start | bytes 786440 | tf_op jit(solution)/shard_map/ppermute | solution.py:417
  11.8 16.9 %collective-permute-start.6 = (f32[512,128]{1,0:T(8,128)}, f32[512,128]{1,0:T(8,128)S(1)}, u32[]{:S(2)}, u32[]{:S(2)}) collective-permute-start(f32[512,128]{1,0:T(8,128)} %get-tuple-element.50), channel_id=1, source_target_pairs={{0,28},{4,24},{8,20},{12,16},{16,12},{20,8},{24,4},{28,0},{1,29},{... | collective-permute-start | bytes 786440 | tf_op jit(solution)/shard_map/ppermute | solution.py:417
  13.9 15.0 %collective-permute-start.5 = (f32[512,128]{1,0:T(8,128)}, f32[512,128]{1,0:T(8,128)S(1)}, u32[]{:S(2)}, u32[]{:S(2)}) collective-permute-start(f32[512,128]{1,0:T(8,128)} %get-tuple-element.49), channel_id=1, source_target_pairs={{0,20},{4,8},{8,28},{12,0},{16,4},{20,24},{24,12},{28,16},{1,21},{... | collective-permute-start | bytes 786440 | tf_op jit(solution)/shard_map/ppermute | solution.py:417
  18.5 10.4 %copy-start.1 = (f32[512,128]{1,0:T(8,128)S(1)}, f32[512,128]{1,0:T(8,128)}, u32[]{:S(2)}) copy-start(f32[512,128]{1,0:T(8,128)} %get-tuple-element.39.refs_0_) | copy-start | bytes 786436
  27.3 34.6 %copy-start = (f32[16,512,128]{2,1,0:T(8,128)S(1)}, f32[16,512,128]{2,1,0:T(8,128)}, u32[]{:S(2)}) copy-start(f32[16,512,128]{2,1,0:T(8,128)} %init_ref.9) | copy-start | bytes 12582916
  45.1 3.7 %collective-permute-start.7 = (f32[512,128]{1,0:T(8,128)S(1)}, f32[512,128]{1,0:T(8,128)S(1)}, u32[]{:S(2)}, u32[]{:S(2)}) collective-permute-start(f32[512,128]{1,0:T(8,128)S(1)} %get-tuple-element.54), channel_id=1, source_target_pairs={{0,4},{4,0},{8,12},{12,8},{16,20},{20,16},{24,28},{28,24},{1,5},{5... | collective-permute-start | bytes 786440 | tf_op jit(solution)/shard_map/ppermute | solution.py:417
  45.2 8.6 %collective-permute-start.9 = (f32[512,128]{1,0:T(8,128)S(1)}, f32[512,128]{1,0:T(8,128)S(1)}, u32[]{:S(2)}, u32[]{:S(2)}) collective-permute-start(f32[512,128]{1,0:T(8,128)S(1)} %get-tuple-element.57), channel_id=1, source_target_pairs={{0,8},{4,20},{8,0},{12,28},{16,24},{20,4},{24,16},{28,12},{1,9},{5... | collective-permute-start | bytes 786440 | tf_op jit(solution)/shard_map/ppermute | solution.py:417
  45.8 17.9 %collective-permute-start.11 = (f32[512,128]{1,0:T(8,128)S(1)}, f32[512,128]{1,0:T(8,128)S(1)}, u32[]{:S(2)}, u32[]{:S(2)}) collective-permute-start(f32[512,128]{1,0:T(8,128)S(1)} %get-tuple-element.59), channel_id=1, source_target_pairs={{0,24},{4,28},{8,16},{12,20},{16,8},{20,12},{24,0},{28,4},{1,25},{... | collective-permute-start | bytes 786440 | tf_op jit(solution)/shard_map/ppermute | solution.py:417
  47.3 16.4 %collective-permute-start.12 = (f32[512,128]{1,0:T(8,128)S(1)}, f32[512,128]{1,0:T(8,128)S(1)}, u32[]{:S(2)}, u32[]{:S(2)}) collective-permute-start(f32[512,128]{1,0:T(8,128)S(1)} %get-tuple-element.60), channel_id=1, source_target_pairs={{0,12},{4,16},{8,4},{12,24},{16,28},{20,0},{24,20},{28,8},{1,13},{... | collective-permute-start | bytes 786440 | tf_op jit(solution)/shard_map/ppermute | solution.py:417
  48.2 13.7 %collective-permute-start.13 = (f32[512,128]{1,0:T(8,128)S(1)}, f32[512,128]{1,0:T(8,128)S(1)}, u32[]{:S(2)}, u32[]{:S(2)}) collective-permute-start(f32[512,128]{1,0:T(8,128)S(1)} %get-tuple-element.64), channel_id=1, source_target_pairs={{0,16},{4,12},{8,24},{12,4},{16,0},{20,28},{24,8},{28,20},{1,17},{... | collective-permute-start | bytes 786440 | tf_op jit(solution)/shard_map/ppermute | solution.py:417
  48.8 17.4 %collective-permute-start.8 = (f32[512,128]{1,0:T(8,128)S(1)}, f32[512,128]{1,0:T(8,128)S(1)}, u32[]{:S(2)}, u32[]{:S(2)}) collective-permute-start(f32[512,128]{1,0:T(8,128)S(1)} %get-tuple-element.55), channel_id=1, source_target_pairs={{0,20},{4,8},{8,28},{12,0},{16,4},{20,24},{24,12},{28,16},{1,21},{... | collective-permute-start | bytes 786440 | tf_op jit(solution)/shard_map/ppermute | solution.py:417
  53.8 17.5 %collective-permute-start.10 = (f32[512,128]{1,0:T(8,128)S(1)}, f32[512,128]{1,0:T(8,128)S(1)}, u32[]{:S(2)}, u32[]{:S(2)}) collective-permute-start(f32[512,128]{1,0:T(8,128)S(1)} %get-tuple-element.58), channel_id=1, source_target_pairs={{0,28},{4,24},{8,20},{12,16},{16,12},{20,8},{24,4},{28,0},{1,29},{... | collective-permute-start | bytes 786440 | tf_op jit(solution)/shard_map/ppermute | solution.py:417

commit v4 on v3

--- a/solution.py
+++ b/solution.py
@@ -417,13 +417,16 @@
             arrived[n] = lax.ppermute(block, "gz", route)
         return arrived
 
+    init_hbm, measured, mask_hbm = (
+        pltpu.with_memory_space_constraint(x, pltpu.HBM) for x in (init, measured, mask)
+    )
     packed = []
     for targets in (plan[1:4], [plan[0]] + plan[4:]):
         size = len(targets)
         packed += pl.pallas_call(
             functools.partial(pack_kernel, targets),
             name="pack_blocks",
-            out_shape=[chunk] * size,
+            out_shape=[pltpu.VMEM(chunk.shape, f32)] * size,
             in_specs=[HBM, HBM],
             out_specs=[VMEM] * size,
             scratch_shapes=[
@@ -432,9 +435,9 @@
                 pltpu.SemaphoreType.DMA((size,)),
                 pltpu.SemaphoreType.DMA,
             ],
-            compiler_params=pltpu.CompilerParams(vmem_limit_bytes=60 * MIB),
+            compiler_params=pltpu.CompilerParams(vmem_limit_bytes=16 * MIB),
             cost_estimate=cost(init.size, 6 * init.size * size // tiles),
-        )(mask, init)
+        )(mask_hbm, init_hbm)
     fields = exchange([packed[3]] + packed[:3] + packed[4:])
 
     poly_shape = shape((MOMENTS, depth, depth), f32)
@@ -470,7 +473,7 @@
             pltpu.VMEM((2, 2, views, depth, step, lanes), f32),
             pltpu.SemaphoreType.DMA((2, 2)),
         ],
-        compiler_params=pltpu.CompilerParams(vmem_limit_bytes=48 * MIB),
+        compiler_params=pltpu.CompilerParams(vmem_limit_bytes=16 * MIB),
         cost_estimate=cost(8 * views * depth * depth * columns * lanes, 4 * measured.size),
     )(mask, left, measured)
 
@@ -510,7 +513,7 @@
     changes = exchange(changes)
 
     solved = None
-    cut = [0, tiles // 2, tiles - 2, tiles]
+    cut = [0, tiles // 2, tiles - 3, tiles - 1, tiles]
     for first, last in zip(cut, cut[1:]):
         size = last - first
         earlier = [] if solved is None else [solved]

time: 72.9 us -> 71.5 us (0.981)
  starting transfers between devices: 13.6 us -> 15.2 us
  waiting for transfers between devices: 21.1 us -> 19.8 us
  blocking collectives: 13.6 us -> 12.7 us
    pallas_call x2, Pallas kernels: 5.23 us -> 3.61 us  [local(): pl.pallas_call(functools.partial(pack_kernel, targets), name='pack_blocks...]
    ppermute x14, starting transfers between devices: 13.6 us -> 15.2 us  [exchange(): arrived[n] = lax.ppermute(block, 'gz', route)]
    ppermute x14, waiting for transfers between devices: 21.1 us -> 19.8 us  [exchange(): arrived[n] = lax.ppermute(block, 'gz', route)]
    pallas_call x3 -> x4, Pallas kernels: 4.56 us -> 5.51 us  [local(): pl.pallas_call(functools.partial(unpack_kernel, plan[first:last]), name='...]
    all_to_all x1, blocking collectives: 13.6 us -> 12.7 us  [local(): lax.all_to_all(moments, ('gz', 'gy'), split_axis=0, concat_axis=0, tiled=...]
  transfers between devices with their start and end apart: 14 -> 14, of which waited for: 7 -> 8; matrix products, arithmetic and copies ran while one was open for 0% -> 0% of each run, Pallas kernels for 25% -> 26%
where the time goes in v4:
time: 71.5 us; the launch traced here: 71.3 us
  Pallas kernels  23.5 us (33%)
  waiting for transfers between devices  19.8 us (28%)
  starting transfers between devices  15.2 us (21%)
  blocking collectives  12.7 us (18%)
    ppermute x14, waiting for transfers between devices, exchange(): arrived[n] = lax.ppermute(block, 'gz', route)  19.8 us
    ppermute x14, starting transfers between devices, exchange(): arrived[n] = lax.ppermute(block, 'gz', route)  15.2 us
    all_to_all x1, blocking collectives, local(): lax.all_to_all(moments, ('gz', 'gy'), split_axis=0, concat_axis=0, tiled=...  12.7 us
    pallas_call x1, Pallas kernels, local(): pl.pallas_call(project_kernel, name='project_views', out_shape=shape((col...  8.83 us
    pallas_call x4, Pallas kernels, local(): pl.pallas_call(functools.partial(unpack_kernel, plan[first:last]), name='...  5.51 us
    pallas_call x2, Pallas kernels, local(): pl.pallas_call(functools.partial(pack_kernel, targets), name='pack_blocks...  3.61 us
    pallas_call x1, Pallas kernels, local(): pl.pallas_call(tables_kernel, name='blur_tables', out_shape=[shape((2 * d...  3.05 us
    pallas_call x1, Pallas kernels, local(): pl.pallas_call(residual_kernel, name='first_residual', out_shape=[shape((...  1.56 us
  transfers between devices with their start and end apart: 14, of which 8 were waited for; matrix products, arithmetic and copies ran while one was open for 0% of the time, Pallas kernels for 26%

profile of v4, /device:TPU:0, one launch (start us, length us, event | category | flops | bytes accessed | tf_op | source)
XLA Modules:
  0.0 71.3 jit_solution(11983844163183131973)
XLA Ops:
  0.0 0.0 copy-start.1
  0.0 0.0 copy-start.3
  0.0 0.0 copy-start.2
  0.0 1.6 %pack_blocks.3 = (f32[512,128]{1,0:T(8,128)S(1)}, f32[512,128]{1,0:T(8,128)S(1)}, f32[512,128]{1,0:T(8,128)S(1)}) custom-call(s32[8,8]{1,0:T(8,128)} %mask_ref.13, f32[16,512,128]{2,1,0:T(8,128)} %init_ref.11), custom_call_target="tpu_custom_call" | custom-call | flops 1048576 | bytes 2359296 | tf_op jit(solution)/shard_map/pack_blocks/pallas_call | solution.py:426
  1.7 0.5 collective-permute-start
  2.2 2.6 %collective-permute-start.1 = (f32[512,128]{1,0:T(8,128)S(1)}, f32[512,128]{1,0:T(8,128)S(1)}, u32[]{:S(2)}, u32[]{:S(2)}) collective-permute-start(f32[512,128]{1,0:T(8,128)S(1)} %get-tuple-element.44), channel_id=1, source_target_pairs={{0,8},{4,20},{8,0},{12,28},{16,24},{20,4},{24,16},{28,12},{1,9},{5... | collective-permute-start | bytes 786440 | tf_op jit(solution)/shard_map/ppermute | solution.py:417
  4.7 1.5 %collective-permute-start.2 = (f32[512,128]{1,0:T(8,128)S(1)}, f32[512,128]{1,0:T(8,128)S(1)}, u32[]{:S(2)}, u32[]{:S(2)}) collective-permute-start(f32[512,128]{1,0:T(8,128)S(1)} %get-tuple-element.46), channel_id=1, source_target_pairs={{0,16},{4,12},{8,24},{12,4},{16,0},{20,28},{24,8},{28,20},{1,17},{... | collective-permute-start | bytes 786440 | tf_op jit(solution)/shard_map/ppermute | solution.py:417
  6.3 2.0 %pack_blocks.2 = (f32[512,128]{1,0:T(8,128)S(1)}, f32[512,128]{1,0:T(8,128)S(1)}, f32[512,128]{1,0:T(8,128)S(1)}, f32[512,128]{1,0:T(8,128)S(1)}, f32[512,128]{1,0:T(8,128)S(1)}) custom-call(s32[8,8]{1,0:T(8,128)} %mask_ref.13, f32[16,512,128]{2,1,0:T(8,128)} %init_ref.11), custom_call_target="tpu_custom_call" | custom-call | flops 1048576 | bytes 3932160 | tf_op jit(solution)/shard_map/pack_blocks/pallas_call | solution.py:426
  8.2 0.1 collective-permute-start.3
  8.3 1.1 %collective-permute-start.4 = (f32[512,128]{1,0:T(8,128)S(1)}, f32[512,128]{1,0:T(8,128)S(1)}, u32[]{:S(2)}, u32[]{:S(2)}) collective-permute-start(f32[512,128]{1,0:T(8,128)S(1)} %get-tuple-element.48), channel_id=1, source_target_pairs={{0,12},{4,16},{8,4},{12,24},{16,28},{20,0},{24,20},{28,8},{1,13},{... | collective-permute-start | bytes 786440 | tf_op jit(solution)/shard_map/ppermute | solution.py:417
  9.5 0.0 collective-permute-done.refs_1_
  9.5 1.3 %collective-permute-done.1.refs_2_ = f32[512,128]{1,0:T(8,128)S(1)} collective-permute-done((f32[512,128]{1,0:T(8,128)S(1)}, f32[512,128]{1,0:T(8,128)S(1)}, u32[]{:S(2)}, u32[]{:S(2)}) %collective-permute-start.1) | collective-permute-done | bytes 262176 | tf_op jit(solution)/shard_map/ppermute | solution.py:417
  10.8 2.2 %collective-permute-start.6 = (f32[512,128]{1,0:T(8,128)S(1)}, f32[512,128]{1,0:T(8,128)S(1)}, u32[]{:S(2)}, u32[]{:S(2)}) collective-permute-start(f32[512,128]{1,0:T(8,128)S(1)} %get-tuple-element.50), channel_id=1, source_target_pairs={{0,28},{4,24},{8,20},{12,16},{16,12},{20,8},{24,4},{28,0},{1,29},{... | collective-permute-start | bytes 786440 | tf_op jit(solution)/shard_map/ppermute | solution.py:417
  13.0 1.5 %collective-permute-start.5 = (f32[512,128]{1,0:T(8,128)S(1)}, f32[512,128]{1,0:T(8,128)S(1)}, u32[]{:S(2)}, u32[]{:S(2)}) collective-permute-start(f32[512,128]{1,0:T(8,128)S(1)} %get-tuple-element.49), channel_id=1, source_target_pairs={{0,20},{4,8},{8,28},{12,0},{16,4},{20,24},{24,12},{28,16},{1,21},{... | collective-permute-start | bytes 786440 | tf_op jit(solution)/shard_map/ppermute | solution.py:417
  14.4 0.0 copy-done.3
  14.5 0.0 copy-done.2
  14.5 3.0 %blur_tables.1 = (bf16[256,1024]{1,0:T(8,128)(2,1)S(1)}, bf16[256,256]{1,0:T(8,128)(2,1)S(1)}, f32[8,128,128]{2,1,0:T(8,128)S(1)}, f32[8,128]{1,0:T(8,128)S(1)}) custom-call(s32[4,8,8]{2,1,0:T(8,128)S(1)} %copy-done.2, f32[16,31]{1,0:T(8,128)S(1)} %copy-done.3), custom_call_target="tpu_custom_call" | custom-call | flops 503316480 | bytes 4194304 | tf_op jit(solution)/shard_map/blur_tables/pallas_call | solution.py:444
  17.5 0.0 copy-done.1
  17.5 8.8 %project_views.1.projected_ref = f32[32,128,128]{2,1,0:T(8,128)S(1)} custom-call(s32[8,8]{1,0:T(8,128)S(1)} %copy-done.1, bf16[256,1024]{1,0:T(8,128)(2,1)S(1)} %get-tuple-element.38.left_ref, f32[4,128,64,128]{3,2,1,0:T(8,128)} %measured_ref.1), custom_call_target="tpu_custom_call" | custom-call | flops 2147483648 | bytes 16777216 | tf_op jit(solution)/shard_map/project_views/pallas_call | solution.py:466
  26.4 0.0 copy-start
  26.4 0.0 collective-permute-done.2.refs_3_
  26.4 0.0 collective-permute-done.3.refs_4_
  26.4 0.0 collective-permute-done.4.refs_5_
  26.4 1.3 %collective-permute-done.6.refs_7_ = f32[512,128]{1,0:T(8,128)S(1)} collective-permute-done((f32[512,128]{1,0:T(8,128)S(1)}, f32[512,128]{1,0:T(8,128)S(1)}, u32[]{:S(2)}, u32[]{:S(2)}) %collective-permute-start.6) | collective-permute-done | bytes 262176 | tf_op jit(solution)/shard_map/ppermute | solution.py:417
  27.7 1.1 %collective-permute-done.5.refs_6_ = f32[512,128]{1,0:T(8,128)S(1)} collective-permute-done((f32[512,128]{1,0:T(8,128)S(1)}, f32[512,128]{1,0:T(8,128)S(1)}, u32[]{:S(2)}, u32[]{:S(2)}) %collective-permute-start.5) | collective-permute-done | bytes 262176 | tf_op jit(solution)/shard_map/ppermute | solution.py:417
  28.8 1.6 %first_residual.1 = (bf16[16,256,256]{2,1,0:T(8,128)(2,1)S(1)}, f32[32,128]{1,0:T(8,128)S(1)}) custom-call(bf16[256,256]{1,0:T(8,128)(2,1)S(1)} %get-tuple-element.36.gram_ref, f32[8,128,128]{2,1,0:T(8,128)S(1)} %get-tuple-element.37.poly_ref, f32[32,128,128]{2,1,0:T(8,128)S(1)} %project_views.1.projected_ref, f32[512,128]{1,0:T(8,128)S(1)} %get-tuple-element.39.refs_0_, ...), custom_call_target="tpu_custom_call" | custom-call | flops 1073741824 | bytes 6291456 | tf_op jit(solution)/shard_map/first_residual/pallas_call | solution.py:482
  30.4 12.7 %all_to_all.11 = f32[32,1,128]{2,1,0:T(1,128)S(1)} all-to-all(f32[32,1,128]{2,1,0:T(1,128)S(1)} %bitcast.5), channel_id=1, replica_groups=mesh['gz'=8,'gy'=4] {'gz','gy'}, dimensions={0} | all-to-all | bytes 32768 | tf_op jit(solution)/shard_map/all_to_all | solution.py:498
  43.1 0.9 %correction.1 = (f32[512,128]{1,0:T(8,128)S(1)}, f32[512,128]{1,0:T(8,128)S(1)}, f32[512,128]{1,0:T(8,128)S(1)}, f32[512,128]{1,0:T(8,128)S(1)}, f32[512,128]{1,...) custom-call(f32[8,128]{1,0:T(8,128)S(1)} %get-tuple-element.35.top_ref, ...), custom_call_target="tpu_custom_call" | custom-call | flops 536870912 | bytes 4194304 | tf_op jit(solution)/shard_map/correction/pallas_call | solution.py:500
  44.0 0.6 collective-permute-start.7
  44.7 0.0 collective-permute-start.10
  44.7 1.6 %collective-permute-start.9 = (f32[512,128]{1,0:T(8,128)S(1)}, f32[512,128]{1,0:T(8,128)S(1)}, u32[]{:S(2)}, u32[]{:S(2)}) collective-permute-start(f32[512,128]{1,0:T(8,128)S(1)} %get-tuple-element.56), channel_id=1, source_target_pairs={{0,12},{4,16},{8,4},{12,24},{16,28},{20,0},{24,20},{28,8},{1,13},{... | collective-permute-start | bytes 786440 | tf_op jit(solution)/shard_map/ppermute | solution.py:417
  46.3 0.5 collective-permute-start.12
  46.8 1.5 %collective-permute-start.13 = (f32[512,128]{1,0:T(8,128)S(1)}, f32[512,128]{1,0:T(8,128)S(1)}, u32[]{:S(2)}, u32[]{:S(2)}) collective-permute-start(f32[512,128]{1,0:T(8,128)S(1)} %get-tuple-element.64), channel_id=1, source_target_pairs={{0,16},{4,12},{8,24},{12,4},{16,0},{20,28},{24,8},{28,20},{1,17},{... | collective-permute-start | bytes 786440 | tf_op jit(solution)/shard_map/ppermute | solution.py:417
  48.3 3.8 %collective-permute-done.7.refs_2_ = f32[512,128]{1,0:T(8,128)S(1)} collective-permute-done((f32[512,128]{1,0:T(8,128)S(1)}, f32[512,128]{1,0:T(8,128)S(1)}, u32[]{:S(2)}, u32[]{:S(2)}) %collective-permute-start.7) | collective-permute-done | bytes 262176 | tf_op jit(solution)/shard_map/ppermute | solution.py:417
  52.1 0.0 collective-permute-done.10.refs_1_
  52.1 0.0 collective-permute-start.11
  52.1 1.4 %collective-permute-start.8 = (f32[512,128]{1,0:T(8,128)S(1)}, f32[512,128]{1,0:T(8,128)S(1)}, u32[]{:S(2)}, u32[]{:S(2)}) collective-permute-start(f32[512,128]{1,0:T(8,128)S(1)} %get-tuple-element.55), channel_id=1, source_target_pairs={{0,28},{4,24},{8,20},{12,16},{16,12},{20,8},{24,4},{28,0},{1,29},{... | collective-permute-start | bytes 786440 | tf_op jit(solution)/shard_map/ppermute | solution.py:417
  53.5 4.6 %collective-permute-done.13.refs_3_ = f32[512,128]{1,0:T(8,128)S(1)} collective-permute-done((f32[512,128]{1,0:T(8,128)S(1)}, f32[512,128]{1,0:T(8,128)S(1)}, u32[]{:S(2)}, u32[]{:S(2)}) %collective-permute-start.13) | collective-permute-done | bytes 262176 | tf_op jit(solution)/shard_map/ppermute | solution.py:417
  58.1 0.0 copy-done
  58.1 1.8 %add_correction.4.refs_1_ = f32[16,512,128]{2,1,0:T(8,128)} custom-call(s32[8,8]{1,0:T(8,128)S(1)} %copy-done.1, f32[16,512,128]{2,1,0:T(8,128)S(1)} %copy-done, f32[512,128]{1,0:T(8,128)S(1)} %get-tuple-element.61.refs_0_, f32[512,128]{1,0:T(8,128)S(1)} %collective-permute-done.10.refs_1_, f32[512,128]{1,0:T(8,128)S(1)} %collective-permute-done.7.refs_2_, ...), custom_call_target="tpu_custom_call" | custom-call | flops 262144 | bytes 2621440 | tf_op jit(solution)/shard_map/add_correction/pallas_call | solution.py:520
  59.9 3.1 %collective-permute-done.12.refs_0_ = f32[512,128]{1,0:T(8,128)S(1)} collective-permute-done((f32[512,128]{1,0:T(8,128)S(1)}, f32[512,128]{1,0:T(8,128)S(1)}, u32[]{:S(2)}, u32[]{:S(2)}) %collective-permute-start.12) | collective-permute-done | bytes 262176 | tf_op jit(solution)/shard_map/ppermute | solution.py:417
  63.0 1.2 %add_correction.5.refs_2_ = f32[16,512,128]{2,1,0:T(8,128)} custom-call(s32[8,8]{1,0:T(8,128)S(1)} %copy-done.1, f32[16,512,128]{2,1,0:T(8,128)S(1)} %copy-done, f32[512,128]{1,0:T(8,128)S(1)} %collective-permute-done.12.refs_0_, f32[16,512,128]{2,1,0:T(8,128)} %add_correction.4.refs_1_), custom_call_target="tpu_custom_call", output_to_operand_aliasing={{}: (3, {})} | custom-call | flops 262144 | bytes 655360 | tf_op jit(solution)/shard_map/add_correction/pallas_call | solution.py:520
  64.1 0.0 collective-permute-done.9.refs_0_
  64.2 1.6 %collective-permute-done.11.refs_1_ = f32[512,128]{1,0:T(8,128)S(1)} collective-permute-done((f32[512,128]{1,0:T(8,128)S(1)}, f32[512,128]{1,0:T(8,128)S(1)}, u32[]{:S(2)}, u32[]{:S(2)}) %collective-permute-start.11) | collective-permute-done | bytes 262176 | tf_op jit(solution)/shard_map/ppermute | solution.py:417
  65.7 1.4 %add_correction.6.refs_1_ = f32[16,512,128]{2,1,0:T(8,128)} custom-call(s32[8,8]{1,0:T(8,128)S(1)} %copy-done.1, f32[16,512,128]{2,1,0:T(8,128)S(1)} %copy-done, f32[512,128]{1,0:T(8,128)S(1)} %collective-permute-done.9.refs_0_, f32[512,128]{1,0:T(8,128)S(1)} %collective-permute-done.11.refs_1_, ...), custom_call_target="tpu_custom_call", output_to_operand_aliasing={{}: (4, {})} | custom-call | flops 262144 | bytes 1310720 | tf_op jit(solution)/shard_map/add_correction/pallas_call | solution.py:520
  67.1 3.0 %collective-permute-done.8.refs_0_ = f32[512,128]{1,0:T(8,128)S(1)} collective-permute-done((f32[512,128]{1,0:T(8,128)S(1)}, f32[512,128]{1,0:T(8,128)S(1)}, u32[]{:S(2)}, u32[]{:S(2)}) %collective-permute-start.8) | collective-permute-done | bytes 262176 | tf_op jit(solution)/shard_map/ppermute | solution.py:417
  70.2 1.2 %add_correction.7 = f32[16,512,128]{2,1,0:T(8,128)} custom-call(s32[8,8]{1,0:T(8,128)S(1)} %copy-done.1, f32[16,512,128]{2,1,0:T(8,128)S(1)} %copy-done, f32[512,128]{1,0:T(8,128)S(1)} %collective-permute-done.8.refs_0_, f32[16,512,128]{2,1,0:T(8,128)} %add_correction.6.refs_1_), custom_call_target="tpu_custom_call", output_to_operand_aliasing={{}: (3, {})} | custom-call | flops 262144 | bytes 655360 | tf_op jit(solution)/shard_map/add_correction/pallas_call | solution.py:520
Async XLA Ops:
  0.0 17.5 %copy-start.1 = (s32[8,8]{1,0:T(8,128)S(1)}, s32[8,8]{1,0:T(8,128)}, u32[]{:S(2)}) copy-start(s32[8,8]{1,0:T(8,128)} %mask_ref.13) | copy-start | bytes 772
  0.0 14.4 %copy-start.3 = (f32[16,31]{1,0:T(8,128)S(1)}, f32[16,31]{1,0:T(8,128)}, u32[]{:S(2)}) copy-start(f32[16,31]{1,0:T(8,128)} %kernels_ref.1) | copy-start | bytes 5956
  0.0 14.4 %copy-start.2 = (s32[4,8,8]{2,1,0:T(8,128)S(1)}, s32[4,8,8]{2,1,0:T(8,128)}, u32[]{:S(2)}) copy-start(s32[4,8,8]{2,1,0:T(8,128)} %index_ref.1) | copy-start | bytes 3076
  1.7 7.8 %collective-permute-start = (f32[512,128]{1,0:T(8,128)S(1)}, f32[512,128]{1,0:T(8,128)S(1)}, u32[]{:S(2)}, u32[]{:S(2)}) collective-permute-start(f32[512,128]{1,0:T(8,128)S(1)} %get-tuple-element.41), channel_id=1, source_target_pairs={{0,4},{4,0},{8,12},{12,8},{16,20},{20,16},{24,28},{28,24},{1,5},{5... | collective-permute-start | bytes 786440 | tf_op jit(solution)/shard_map/ppermute | solution.py:417
  2.2 8.6 %collective-permute-start.1 = (f32[512,128]{1,0:T(8,128)S(1)}, f32[512,128]{1,0:T(8,128)S(1)}, u32[]{:S(2)}, u32[]{:S(2)}) collective-permute-start(f32[512,128]{1,0:T(8,128)S(1)} %get-tuple-element.44), channel_id=1, source_target_pairs={{0,8},{4,20},{8,0},{12,28},{16,24},{20,4},{24,16},{28,12},{1,9},{5... | collective-permute-start | bytes 786440 | tf_op jit(solution)/shard_map/ppermute | solution.py:417
  4.7 21.6 %collective-permute-start.2 = (f32[512,128]{1,0:T(8,128)S(1)}, f32[512,128]{1,0:T(8,128)S(1)}, u32[]{:S(2)}, u32[]{:S(2)}) collective-permute-start(f32[512,128]{1,0:T(8,128)S(1)} %get-tuple-element.46), channel_id=1, source_target_pairs={{0,16},{4,12},{8,24},{12,4},{16,0},{20,28},{24,8},{28,20},{1,17},{... | collective-permute-start | bytes 786440 | tf_op jit(solution)/shard_map/ppermute | solution.py:417
  8.2 18.1 %collective-permute-start.3 = (f32[512,128]{1,0:T(8,128)S(1)}, f32[512,128]{1,0:T(8,128)S(1)}, u32[]{:S(2)}, u32[]{:S(2)}) collective-permute-start(f32[512,128]{1,0:T(8,128)S(1)} %get-tuple-element.47), channel_id=1, source_target_pairs={{0,24},{4,28},{8,16},{12,20},{16,8},{20,12},{24,0},{28,4},{1,25},{... | collective-permute-start | bytes 786440 | tf_op jit(solution)/shard_map/ppermute | solution.py:417
  8.3 18.1 %collective-permute-start.4 = (f32[512,128]{1,0:T(8,128)S(1)}, f32[512,128]{1,0:T(8,128)S(1)}, u32[]{:S(2)}, u32[]{:S(2)}) collective-permute-start(f32[512,128]{1,0:T(8,128)S(1)} %get-tuple-element.48), channel_id=1, source_target_pairs={{0,12},{4,16},{8,4},{12,24},{16,28},{20,0},{24,20},{28,8},{1,13},{... | collective-permute-start | bytes 786440 | tf_op jit(solution)/shard_map/ppermute | solution.py:417
  10.8 16.9 %collective-permute-start.6 = (f32[512,128]{1,0:T(8,128)S(1)}, f32[512,128]{1,0:T(8,128)S(1)}, u32[]{:S(2)}, u32[]{:S(2)}) collective-permute-start(f32[512,128]{1,0:T(8,128)S(1)} %get-tuple-element.50), channel_id=1, source_target_pairs={{0,28},{4,24},{8,20},{12,16},{16,12},{20,8},{24,4},{28,0},{1,29},{... | collective-permute-start | bytes 786440 | tf_op jit(solution)/shard_map/ppermute | solution.py:417
  13.0 15.8 %collective-permute-start.5 = (f32[512,128]{1,0:T(8,128)S(1)}, f32[512,128]{1,0:T(8,128)S(1)}, u32[]{:S(2)}, u32[]{:S(2)}) collective-permute-start(f32[512,128]{1,0:T(8,128)S(1)} %get-tuple-element.49), channel_id=1, source_target_pairs={{0,20},{4,8},{8,28},{12,0},{16,4},{20,24},{24,12},{28,16},{1,21},{... | collective-permute-start | bytes 786440 | tf_op jit(solution)/shard_map/ppermute | solution.py:417
  26.4 31.7 %copy-start = (f32[16,512,128]{2,1,0:T(8,128)S(1)}, f32[16,512,128]{2,1,0:T(8,128)}, u32[]{:S(2)}) copy-start(f32[16,512,128]{2,1,0:T(8,128)} %init_ref.11) | copy-start | bytes 12582916
  44.0 8.0 %collective-permute-start.7 = (f32[512,128]{1,0:T(8,128)S(1)}, f32[512,128]{1,0:T(8,128)S(1)}, u32[]{:S(2)}, u32[]{:S(2)}) collective-permute-start(f32[512,128]{1,0:T(8,128)S(1)} %get-tuple-element.54), channel_id=1, source_target_pairs={{0,8},{4,20},{8,0},{12,28},{16,24},{20,4},{24,16},{28,12},{1,9},{5... | collective-permute-start | bytes 786440 | tf_op jit(solution)/shard_map/ppermute | solution.py:417
  44.7 7.4 %collective-permute-start.10 = (f32[512,128]{1,0:T(8,128)S(1)}, f32[512,128]{1,0:T(8,128)S(1)}, u32[]{:S(2)}, u32[]{:S(2)}) collective-permute-start(f32[512,128]{1,0:T(8,128)S(1)} %get-tuple-element.58), channel_id=1, source_target_pairs={{0,4},{4,0},{8,12},{12,8},{16,20},{20,16},{24,28},{28,24},{1,5},{5... | collective-permute-start | bytes 786440 | tf_op jit(solution)/shard_map/ppermute | solution.py:417
  44.7 19.4 %collective-permute-start.9 = (f32[512,128]{1,0:T(8,128)S(1)}, f32[512,128]{1,0:T(8,128)S(1)}, u32[]{:S(2)}, u32[]{:S(2)}) collective-permute-start(f32[512,128]{1,0:T(8,128)S(1)} %get-tuple-element.56), channel_id=1, source_target_pairs={{0,12},{4,16},{8,4},{12,24},{16,28},{20,0},{24,20},{28,8},{1,13},{... | collective-permute-start | bytes 786440 | tf_op jit(solution)/shard_map/ppermute | solution.py:417
  46.3 16.7 %collective-permute-start.12 = (f32[512,128]{1,0:T(8,128)S(1)}, f32[512,128]{1,0:T(8,128)S(1)}, u32[]{:S(2)}, u32[]{:S(2)}) collective-permute-start(f32[512,128]{1,0:T(8,128)S(1)} %get-tuple-element.60), channel_id=1, source_target_pairs={{0,24},{4,28},{8,16},{12,20},{16,8},{20,12},{24,0},{28,4},{1,25},{... | collective-permute-start | bytes 786440 | tf_op jit(solution)/shard_map/ppermute | solution.py:417
  46.8 11.3 %collective-permute-start.13 = (f32[512,128]{1,0:T(8,128)S(1)}, f32[512,128]{1,0:T(8,128)S(1)}, u32[]{:S(2)}, u32[]{:S(2)}) collective-permute-start(f32[512,128]{1,0:T(8,128)S(1)} %get-tuple-element.64), channel_id=1, source_target_pairs={{0,16},{4,12},{8,24},{12,4},{16,0},{20,28},{24,8},{28,20},{1,17},{... | collective-permute-start | bytes 786440 | tf_op jit(solution)/shard_map/ppermute | solution.py:417
  52.1 13.7 %collective-permute-start.11 = (f32[512,128]{1,0:T(8,128)S(1)}, f32[512,128]{1,0:T(8,128)S(1)}, u32[]{:S(2)}, u32[]{:S(2)}) collective-permute-start(f32[512,128]{1,0:T(8,128)S(1)} %get-tuple-element.59), channel_id=1, source_target_pairs={{0,20},{4,8},{8,28},{12,0},{16,4},{20,24},{24,12},{28,16},{1,21},{... | collective-permute-start | bytes 786440 | tf_op jit(solution)/shard_map/ppermute | solution.py:417
  52.1 18.1 %collective-permute-start.8 = (f32[512,128]{1,0:T(8,128)S(1)}, f32[512,128]{1,0:T(8,128)S(1)}, u32[]{:S(2)}, u32[]{:S(2)}) collective-permute-start(f32[512,128]{1,0:T(8,128)S(1)} %get-tuple-element.55), channel_id=1, source_target_pairs={{0,28},{4,24},{8,20},{12,16},{16,12},{20,8},{24,4},{28,0},{1,29},{... | collective-permute-start | bytes 786440 | tf_op jit(solution)/shard_map/ppermute | solution.py:417

commit v5 on v4

--- a/solution.py
+++ b/solution.py
@@ -14,6 +14,7 @@
 damping = 1.0
 MIB = 1 << 20
 IN_FLIGHT = 5
+EARLY = 3
 
 
 def split(x):
@@ -48,7 +49,7 @@
         return ((((across & (2**high - 1)) << high) | (across >> high)) << 1) | (k & 1)
 
     same, other = list(range(2, tiles, 2)), list(range(3, tiles, 2))
-    order = [0, 1] + same + other
+    order = [0] + same[:2] + [1] + same[2:] + other
     return [(k, swapped(k)) for k in order]
 
 
@@ -311,14 +312,7 @@
     return solved
 
 
-def correct_kernel(top_ref, moments_ref, poly_ref, residual_ref, *refs):
-    count = len(refs) - 2
-    out_refs, (matrix_ref, left_ref) = refs[:count], refs[count:]
-    depth = matrix_ref.shape[0]
-    slab = depth // count
-    pairs, _, lanes = residual_ref.shape
-    lanes = lanes // 2
-    me = lax.axis_index("gz")
+def combine_kernel(top_ref, moments_ref, poly_ref, matrix_ref):
     row = jnp.sum(moments_ref[...], axis=0, keepdims=True)
     lane = lax.broadcasted_iota(jnp.int32, row.shape, 1)
     moments = [
@@ -330,22 +324,39 @@
     for k in range(1, ITERS):
         matrix = matrix + coefficients[k] * poly_ref[k]
     matrix_ref[...] = matrix
+
+
+def correct_blocks(group, slab, matrix_ref, residual_ref, out_refs, left_ref):
+    pairs, _, lanes = residual_ref.shape
+    lanes = lanes // 2
+    me = lax.axis_index("gz")
     left_ref[...] = left_operand(
         jnp.concatenate(
             [
                 matrix_ref[pl.ds(pl.multiple_of(receiver(me, slot) * slab, slab), slab), :]
-                for slot in slots(count)
+                for slot in group
             ],
             axis=0,
         )
     )
     for pair in range(pairs):
         result = product(left_ref[...], residual_ref[pair])
-        for k in range(count):
+        for k in range(len(group)):
             rows = result[slab * k : slab * (k + 1)]
             for side in range(2):
                 start = (2 * pair + side) * slab
                 out_refs[k][start : start + slab, :] = rows[:, lanes * side : lanes * (side + 1)]
+
+
+def first_correct_kernel(group, top_ref, moments_ref, poly_ref, residual_ref, matrix_ref, *refs):
+    combine_kernel(top_ref, moments_ref, poly_ref, matrix_ref)
+    slab = refs[0].shape[0] // (2 * residual_ref.shape[0])
+    correct_blocks(group, slab, matrix_ref, residual_ref, refs[:-1], refs[-1])
+
+
+def correct_kernel(group, matrix_ref, residual_ref, *refs):
+    slab = refs[0].shape[0] // (2 * residual_ref.shape[0])
+    correct_blocks(group, slab, matrix_ref, residual_ref, refs[:-1], refs[-1])
 
 
 def unpack_kernel(group, mask_ref, init_ref, *refs):
@@ -358,6 +369,8 @@
     block = lax.broadcasted_iota(jnp.int32, flags.shape, 1)
     region = lax.broadcasted_iota(jnp.int32, flags.shape, 0)
     lane = lax.broadcasted_iota(jnp.int32, (columns, lanes), 1)
+    pieces = sems.shape[1]
+    piece = slab // pieces
     stores = []
     for n, slot in enumerate(group):
         tile = sender(me, slot)
@@ -373,12 +386,16 @@
             staged[n, z, columns:, :] = init_ref[
                 z, pl.ds(pl.multiple_of(start + columns, columns), columns), :
             ] + pltpu.roll(jnp.where(here, 0.0, change), lanes // 2, 1)
-        stores.append(
-            pltpu.make_async_copy(
-                staged.at[n], out_ref.at[:, pl.ds(start, width), :], sems.at[n]
-            )
-        )
-        stores[n].start()
+            if (z + 1) % piece == 0:
+                part = pl.ds(z + 1 - piece, piece)
+                stores.append(
+                    pltpu.make_async_copy(
+                        staged.at[n, part],
+                        out_ref.at[part, pl.ds(start, width), :],
+                        sems.at[n, z // piece],
+                    )
+                )
+                stores[-1].start()
     for store in stores:
         store.wait()
 
@@ -421,7 +438,7 @@
         pltpu.with_memory_space_constraint(x, pltpu.HBM) for x in (init, measured, mask)
     )
     packed = []
-    for targets in (plan[1:4], [plan[0]] + plan[4:]):
+    for targets in (plan[1:3], [plan[0]] + plan[3:]):
         size = len(targets)
         packed += pl.pallas_call(
             functools.partial(pack_kernel, targets),
@@ -438,7 +455,7 @@
             compiler_params=pltpu.CompilerParams(vmem_limit_bytes=16 * MIB),
             cost_estimate=cost(init.size, 6 * init.size * size // tiles),
         )(mask_hbm, init_hbm)
-    fields = exchange([packed[3]] + packed[:3] + packed[4:])
+    fields = exchange([packed[2]] + packed[:2] + packed[3:])
 
     poly_shape = shape((MOMENTS, depth, depth), f32)
     left, gram, poly, top = pl.pallas_call(
@@ -497,19 +514,29 @@
 
     moments = lax.all_to_all(moments, ("gz", "gy"), split_axis=0, concat_axis=0, tiled=True)
 
-    changes = pl.pallas_call(
-        correct_kernel,
-        name="correction",
-        out_shape=[chunk] * tiles,
+    parameters = pltpu.CompilerParams(vmem_limit_bytes=16 * MIB)
+    soon, later = plan[1:EARLY], plan[:1] + plan[EARLY:]
+    matrix, *changes = pl.pallas_call(
+        functools.partial(first_correct_kernel, soon),
+        name="first_corrections",
+        out_shape=[shape((depth, depth), f32)] + [chunk] * len(soon),
         in_specs=[VMEM] * 4,
-        out_specs=[VMEM] * tiles,
-        scratch_shapes=[
-            pltpu.VMEM((depth, depth), f32),
-            pltpu.VMEM((2 * depth, 2 * depth), bf16),
-        ],
-        compiler_params=pltpu.CompilerParams(vmem_limit_bytes=16 * MIB),
-        cost_estimate=cost(8 * depth * depth * columns * lanes, 8 * depth * columns * lanes),
+        out_specs=[VMEM] * (1 + len(soon)),
+        scratch_shapes=[pltpu.VMEM((2 * slab * len(soon), 2 * depth), bf16)],
+        compiler_params=parameters,
+        cost_estimate=cost(2 * depth * depth * columns * lanes, 2 * depth * columns * lanes),
     )(top, moments, poly, residual)
+    others = pl.pallas_call(
+        functools.partial(correct_kernel, later),
+        name="corrections",
+        out_shape=[chunk] * len(later),
+        in_specs=[VMEM] * 2,
+        out_specs=[VMEM] * len(later),
+        scratch_shapes=[pltpu.VMEM((2 * slab * len(later), 2 * depth), bf16)],
+        compiler_params=parameters,
+        cost_estimate=cost(6 * depth * depth * columns * lanes, 6 * depth * columns * lanes),
+    )(matrix, residual)
+    changes = [others[0], *changes, *others[1:]]
     changes = exchange(changes)
 
     solved = None
@@ -526,7 +553,7 @@
             input_output_aliases={2 + size: 0} if earlier else {},
             scratch_shapes=[
                 pltpu.VMEM((size, slab, width, lanes), f32),
-                pltpu.SemaphoreType.DMA((size,)),
+                pltpu.SemaphoreType.DMA((size, 4)),
             ],
             compiler_params=pltpu.CompilerParams(vmem_limit_bytes=16 * MIB),
             cost_estimate=cost(init.size // 4, 5 * init.size * size // tiles),

time: 71.5 us -> 70.7 us (0.989); the launches traced: 71.3 us -> 69.5 us
  waiting for transfers between devices: 19.8 us -> 17 us
    ppermute x14, waiting for transfers between devices: 19.8 us -> 17 us  [exchange(): arrived[n] = lax.ppermute(block, 'gz', route)]
  transfers between devices with their start and end apart: 14 -> 14, of which waited for: 8 -> 7; matrix products, arithmetic and copies ran while one was open for 0% -> 0% of each run, Pallas kernels for 26% -> 27%
where the time goes in v5:
time: 70.7 us; the launch traced here: 69.5 us
  Pallas kernels  23.7 us (34%)
  waiting for transfers between devices  17 us (24%)
  starting transfers between devices  15.8 us (22%)
  blocking collectives  12.9 us (18%)
    ppermute x14, waiting for transfers between devices, exchange(): arrived[n] = lax.ppermute(block, 'gz', route)  17 us
    ppermute x14, starting transfers between devices, exchange(): arrived[n] = lax.ppermute(block, 'gz', route)  15.8 us
    all_to_all x1, blocking collectives, local(): lax.all_to_all(moments, ('gz', 'gy'), split_axis=0, concat_axis=0, tiled=...  12.9 us
    pallas_call x1, Pallas kernels, local(): pl.pallas_call(project_kernel, name='project_views', out_shape=shape((col...  8.83 us
    pallas_call x4, Pallas kernels, local(): pl.pallas_call(functools.partial(unpack_kernel, plan[first:last]), name='...  5.36 us
    pallas_call x2, Pallas kernels, local(): pl.pallas_call(functools.partial(pack_kernel, targets), name='pack_blocks...  3.61 us
    pallas_call x1, Pallas kernels, local(): pl.pallas_call(tables_kernel, name='blur_tables', out_shape=[shape((2 * d...  3.04 us
    pallas_call x1, Pallas kernels, local(): pl.pallas_call(residual_kernel, name='first_residual', out_shape=[shape((...  1.56 us
  transfers between devices with their start and end apart: 14, of which 7 were waited for; matrix products, arithmetic and copies ran while one was open for 0% of the time, Pallas kernels for 27%

profile of v5, /device:TPU:0, one launch (start us, length us, event | category | flops | bytes accessed | tf_op | source)
XLA Modules:
  0.0 69.5 jit_solution(16736797283126572993)
XLA Ops:
  0.0 0.0 copy-start.1
  0.0 0.0 copy-start.3
  0.0 0.0 copy-start.2
  0.0 1.5 %pack_blocks.3 = (f32[512,128]{1,0:T(8,128)S(1)}, f32[512,128]{1,0:T(8,128)S(1)}) custom-call(s32[8,8]{1,0:T(8,128)} %mask_ref.13, f32[16,512,128]{2,1,0:T(8,128)} %init_ref.11), custom_call_target="tpu_custom_call" | custom-call | flops 1048576 | bytes 1572864 | tf_op jit(solution)/shard_map/pack_blocks/pallas_call | solution.py:443
  1.5 3.0 %collective-permute-start = (f32[512,128]{1,0:T(8,128)S(1)}, f32[512,128]{1,0:T(8,128)S(1)}, u32[]{:S(2)}, u32[]{:S(2)}) collective-permute-start(f32[512,128]{1,0:T(8,128)S(1)} %get-tuple-element.42), channel_id=1, source_target_pairs={{0,8},{4,20},{8,0},{12,28},{16,24},{20,4},{24,16},{28,12},{1,9},{5... | collective-permute-start | bytes 786440 | tf_op jit(solution)/shard_map/ppermute | solution.py:434
  4.5 1.5 %collective-permute-start.1 = (f32[512,128]{1,0:T(8,128)S(1)}, f32[512,128]{1,0:T(8,128)S(1)}, u32[]{:S(2)}, u32[]{:S(2)}) collective-permute-start(f32[512,128]{1,0:T(8,128)S(1)} %get-tuple-element.45), channel_id=1, source_target_pairs={{0,16},{4,12},{8,24},{12,4},{16,0},{20,28},{24,8},{28,20},{1,17},{... | collective-permute-start | bytes 786440 | tf_op jit(solution)/shard_map/ppermute | solution.py:434
  6.0 2.2 %pack_blocks.2 = (f32[512,128]{1,0:T(8,128)S(1)}, f32[512,128]{1,0:T(8,128)S(1)}, f32[512,128]{1,0:T(8,128)S(1)}, f32[512,128]{1,0:T(8,128)S(1)}, f32[512,128]{1,0:T(8,128)S(1)}, /*index=5*/f32[512,128]{1,0:T(8,128)S(1)}) custom-call(s32[8,8]{1,0:T(8,128)} %mask_ref.13, f32[16,512,128]{2,1,0:T(8,128)} %init_ref.11), custom_call_target="tpu_custom_call" | custom-call | flops 1048576 | bytes 4718592 | tf_op jit(solution)/shard_map/pack_blocks/pallas_call | solution.py:443
  8.2 0.1 collective-permute-start.2
  8.2 0.1 collective-permute-start.3
  8.3 1.7 %collective-permute-start.4 = (f32[512,128]{1,0:T(8,128)S(1)}, f32[512,128]{1,0:T(8,128)S(1)}, u32[]{:S(2)}, u32[]{:S(2)}) collective-permute-start(f32[512,128]{1,0:T(8,128)S(1)} %get-tuple-element.49), channel_id=1, source_target_pairs={{0,12},{4,16},{8,4},{12,24},{16,28},{20,0},{24,20},{28,8},{1,13},{... | collective-permute-start | bytes 786440 | tf_op jit(solution)/shard_map/ppermute | solution.py:434
  10.0 1.0 %collective-permute-done.refs_1_ = f32[512,128]{1,0:T(8,128)S(1)} collective-permute-done((f32[512,128]{1,0:T(8,128)S(1)}, f32[512,128]{1,0:T(8,128)S(1)}, u32[]{:S(2)}, u32[]{:S(2)}) %collective-permute-start) | collective-permute-done | bytes 262176 | tf_op jit(solution)/shard_map/ppermute | solution.py:434
  11.1 0.0 collective-permute-done.1.refs_2_
  11.1 1.5 %collective-permute-start.6 = (f32[512,128]{1,0:T(8,128)S(1)}, f32[512,128]{1,0:T(8,128)S(1)}, u32[]{:S(2)}, u32[]{:S(2)}) collective-permute-start(f32[512,128]{1,0:T(8,128)S(1)} %get-tuple-element.51), channel_id=1, source_target_pairs={{0,28},{4,24},{8,20},{12,16},{16,12},{20,8},{24,4},{28,0},{1,29},{... | collective-permute-start | bytes 786440 | tf_op jit(solution)/shard_map/ppermute | solution.py:434
  12.5 2.2 %collective-permute-start.5 = (f32[512,128]{1,0:T(8,128)S(1)}, f32[512,128]{1,0:T(8,128)S(1)}, u32[]{:S(2)}, u32[]{:S(2)}) collective-permute-start(f32[512,128]{1,0:T(8,128)S(1)} %get-tuple-element.50), channel_id=1, source_target_pairs={{0,20},{4,8},{8,28},{12,0},{16,4},{20,24},{24,12},{28,16},{1,21},{... | collective-permute-start | bytes 786440 | tf_op jit(solution)/shard_map/ppermute | solution.py:434
  14.7 0.0 copy-done.3
  14.7 0.0 copy-done.2
  14.7 3.0 %blur_tables.1 = (bf16[256,1024]{1,0:T(8,128)(2,1)S(1)}, bf16[256,256]{1,0:T(8,128)(2,1)S(1)}, f32[8,128,128]{2,1,0:T(8,128)S(1)}, f32[8,128]{1,0:T(8,128)S(1)}) custom-call(s32[4,8,8]{2,1,0:T(8,128)S(1)} %copy-done.2, f32[16,31]{1,0:T(8,128)S(1)} %copy-done.3), custom_call_target="tpu_custom_call" | custom-call | flops 503316480 | bytes 4194304 | tf_op jit(solution)/shard_map/blur_tables/pallas_call | solution.py:461
  17.8 0.0 copy-done.1
  17.8 8.8 %project_views.1.projected_ref = f32[32,128,128]{2,1,0:T(8,128)S(1)} custom-call(s32[8,8]{1,0:T(8,128)S(1)} %copy-done.1, bf16[256,1024]{1,0:T(8,128)(2,1)S(1)} %get-tuple-element.39.left_ref, f32[4,128,64,128]{3,2,1,0:T(8,128)} %measured_ref.1), custom_call_target="tpu_custom_call" | custom-call | flops 2147483648 | bytes 16777216 | tf_op jit(solution)/shard_map/project_views/pallas_call | solution.py:483
  26.6 0.0 collective-permute-done.2.refs_3_
  26.6 0.0 collective-permute-done.3.refs_4_
  26.7 0.0 collective-permute-done.4.refs_5_
  26.7 1.3 %collective-permute-done.6.refs_7_ = f32[512,128]{1,0:T(8,128)S(1)} collective-permute-done((f32[512,128]{1,0:T(8,128)S(1)}, f32[512,128]{1,0:T(8,128)S(1)}, u32[]{:S(2)}, u32[]{:S(2)}) %collective-permute-start.6) | collective-permute-done | bytes 262176 | tf_op jit(solution)/shard_map/ppermute | solution.py:434
  28.0 0.3 collective-permute-done.5.refs_6_
  28.3 0.0 copy-start
  28.3 1.6 %first_residual.1 = (bf16[16,256,256]{2,1,0:T(8,128)(2,1)S(1)}, f32[32,128]{1,0:T(8,128)S(1)}) custom-call(bf16[256,256]{1,0:T(8,128)(2,1)S(1)} %get-tuple-element.37.gram_ref, f32[8,128,128]{2,1,0:T(8,128)S(1)} %get-tuple-element.38.poly_ref, f32[32,128,128]{2,1,0:T(8,128)S(1)} %project_views.1.projected_ref, f32[512,128]{1,0:T(8,128)S(1)} %get-tuple-element.40.refs_0_, ...), custom_call_target="tpu_custom_call" | custom-call | flops 1073741824 | bytes 6291456 | tf_op jit(solution)/shard_map/first_residual/pallas_call | solution.py:499
  29.9 12.9 %all_to_all.11 = f32[32,1,128]{2,1,0:T(1,128)S(1)} all-to-all(f32[32,1,128]{2,1,0:T(1,128)S(1)} %bitcast.5), channel_id=1, replica_groups=mesh['gz'=8,'gy'=4] {'gz','gy'}, dimensions={0} | all-to-all | bytes 32768 | tf_op jit(solution)/shard_map/all_to_all | solution.py:515
  42.7 0.7 %first_corrections.1 = (f32[128,128]{1,0:T(8,128)S(1)}, f32[512,128]{1,0:T(8,128)S(1)}, f32[512,128]{1,0:T(8,128)S(1)}) custom-call(f32[8,128]{1,0:T(8,128)S(1)} %get-tuple-element.36.top_ref, f32[32,128]{1,0:T(8,128)S(1)} %bitcast.4, f32[8,128,128]{2,1,0:T(8,128)S(1)} %get-tuple-element.38.poly_ref, bf16[16,256,256]{2,1,0:T(8,128)(2,1)S(1)} %get-tuple-element.53.residual_ref), custom_call_target="tpu_custom_call" | custom-call | flops 134217728 | bytes 1048576 | tf_op jit(solution)/shard_map/first_corrections/pallas_call | solution.py:519
  43.4 0.6 collective-permute-start.7
  44.1 0.5 collective-permute-start.10
  44.6 0.6 corrections.1
  45.2 0.4 collective-permute-start.9
  45.5 2.1 %collective-permute-start.12 = (f32[512,128]{1,0:T(8,128)S(1)}, f32[512,128]{1,0:T(8,128)S(1)}, u32[]{:S(2)}, u32[]{:S(2)}) collective-permute-start(f32[512,128]{1,0:T(8,128)S(1)} %get-tuple-element.62), channel_id=1, source_target_pairs={{0,24},{4,28},{8,16},{12,20},{16,8},{20,12},{24,0},{28,4},{1,25},{... | collective-permute-start | bytes 786440 | tf_op jit(solution)/shard_map/ppermute | solution.py:434
  47.7 0.4 collective-permute-start.13
  48.0 6.8 %collective-permute-done.7.refs_2_ = f32[512,128]{1,0:T(8,128)S(1)} collective-permute-done((f32[512,128]{1,0:T(8,128)S(1)}, f32[512,128]{1,0:T(8,128)S(1)}, u32[]{:S(2)}, u32[]{:S(2)}) %collective-permute-start.7) | collective-permute-done | bytes 262176 | tf_op jit(solution)/shard_map/ppermute | solution.py:434
  54.9 0.0 collective-permute-done.10.refs_1_
  54.9 0.0 collective-permute-start.11
  54.9 1.7 %collective-permute-start.8 = (f32[512,128]{1,0:T(8,128)S(1)}, f32[512,128]{1,0:T(8,128)S(1)}, u32[]{:S(2)}, u32[]{:S(2)}) collective-permute-start(f32[512,128]{1,0:T(8,128)S(1)} %get-tuple-element.57), channel_id=1, source_target_pairs={{0,28},{4,24},{8,20},{12,16},{16,12},{20,8},{24,4},{28,0},{1,29},{... | collective-permute-start | bytes 786440 | tf_op jit(solution)/shard_map/ppermute | solution.py:434
  56.6 0.0 collective-permute-done.13.refs_3_
  56.6 0.0 copy-done
  56.6 1.8 %add_correction.4.refs_1_ = f32[16,512,128]{2,1,0:T(8,128)} custom-call(s32[8,8]{1,0:T(8,128)S(1)} %copy-done.1, f32[16,512,128]{2,1,0:T(8,128)S(1)} %copy-done, f32[512,128]{1,0:T(8,128)S(1)} %get-tuple-element.63.refs_0_, f32[512,128]{1,0:T(8,128)S(1)} %collective-permute-done.10.refs_1_, f32[512,128]{1,0:T(8,128)S(1)} %collective-permute-done.7.refs_2_, ...), custom_call_target="tpu_custom_call" | custom-call | flops 262144 | bytes 2621440 | tf_op jit(solution)/shard_map/add_correction/pallas_call | solution.py:547
  58.4 3.5 %collective-permute-done.12.refs_0_ = f32[512,128]{1,0:T(8,128)S(1)} collective-permute-done((f32[512,128]{1,0:T(8,128)S(1)}, f32[512,128]{1,0:T(8,128)S(1)}, u32[]{:S(2)}, u32[]{:S(2)}) %collective-permute-start.12) | collective-permute-done | bytes 262176 | tf_op jit(solution)/shard_map/ppermute | solution.py:434
  61.9 1.1 %add_correction.5.refs_2_ = f32[16,512,128]{2,1,0:T(8,128)} custom-call(s32[8,8]{1,0:T(8,128)S(1)} %copy-done.1, f32[16,512,128]{2,1,0:T(8,128)S(1)} %copy-done, f32[512,128]{1,0:T(8,128)S(1)} %collective-permute-done.12.refs_0_, f32[16,512,128]{2,1,0:T(8,128)} %add_correction.4.refs_1_), custom_call_target="tpu_custom_call", output_to_operand_aliasing={{}: (3, {})} | custom-call | flops 262144 | bytes 655360 | tf_op jit(solution)/shard_map/add_correction/pallas_call | solution.py:547
  63.0 0.0 collective-permute-done.9.refs_0_
  63.0 0.5 collective-permute-done.11.refs_1_
  63.5 1.4 %add_correction.6.refs_1_ = f32[16,512,128]{2,1,0:T(8,128)} custom-call(s32[8,8]{1,0:T(8,128)S(1)} %copy-done.1, f32[16,512,128]{2,1,0:T(8,128)S(1)} %copy-done, f32[512,128]{1,0:T(8,128)S(1)} %collective-permute-done.9.refs_0_, f32[512,128]{1,0:T(8,128)S(1)} %collective-permute-done.11.refs_1_, ...), custom_call_target="tpu_custom_call", output_to_operand_aliasing={{}: (4, {})} | custom-call | flops 262144 | bytes 1310720 | tf_op jit(solution)/shard_map/add_correction/pallas_call | solution.py:547
  64.9 3.5 %collective-permute-done.8.refs_0_ = f32[512,128]{1,0:T(8,128)S(1)} collective-permute-done((f32[512,128]{1,0:T(8,128)S(1)}, f32[512,128]{1,0:T(8,128)S(1)}, u32[]{:S(2)}, u32[]{:S(2)}) %collective-permute-start.8) | collective-permute-done | bytes 262176 | tf_op jit(solution)/shard_map/ppermute | solution.py:434
  68.4 1.1 %add_correction.7 = f32[16,512,128]{2,1,0:T(8,128)} custom-call(s32[8,8]{1,0:T(8,128)S(1)} %copy-done.1, f32[16,512,128]{2,1,0:T(8,128)S(1)} %copy-done, f32[512,128]{1,0:T(8,128)S(1)} %collective-permute-done.8.refs_0_, f32[16,512,128]{2,1,0:T(8,128)} %add_correction.6.refs_1_), custom_call_target="tpu_custom_call", output_to_operand_aliasing={{}: (3, {})} | custom-call | flops 262144 | bytes 655360 | tf_op jit(solution)/shard_map/add_correction/pallas_call | solution.py:547
Async XLA Ops:
  0.0 17.8 %copy-start.1 = (s32[8,8]{1,0:T(8,128)S(1)}, s32[8,8]{1,0:T(8,128)}, u32[]{:S(2)}) copy-start(s32[8,8]{1,0:T(8,128)} %mask_ref.13) | copy-start | bytes 772
  0.0 14.7 %copy-start.3 = (f32[16,31]{1,0:T(8,128)S(1)}, f32[16,31]{1,0:T(8,128)}, u32[]{:S(2)}) copy-start(f32[16,31]{1,0:T(8,128)} %kernels_ref.1) | copy-start | bytes 5956
  0.0 14.7 %copy-start.2 = (s32[4,8,8]{2,1,0:T(8,128)S(1)}, s32[4,8,8]{2,1,0:T(8,128)}, u32[]{:S(2)}) copy-start(s32[4,8,8]{2,1,0:T(8,128)} %index_ref.1) | copy-start | bytes 3076
  1.5 9.6 %collective-permute-start = (f32[512,128]{1,0:T(8,128)S(1)}, f32[512,128]{1,0:T(8,128)S(1)}, u32[]{:S(2)}, u32[]{:S(2)}) collective-permute-start(f32[512,128]{1,0:T(8,128)S(1)} %get-tuple-element.42), channel_id=1, source_target_pairs={{0,8},{4,20},{8,0},{12,28},{16,24},{20,4},{24,16},{28,12},{1,9},{5... | collective-permute-start | bytes 786440 | tf_op jit(solution)/shard_map/ppermute | solution.py:434
  4.5 6.6 %collective-permute-start.1 = (f32[512,128]{1,0:T(8,128)S(1)}, f32[512,128]{1,0:T(8,128)S(1)}, u32[]{:S(2)}, u32[]{:S(2)}) collective-permute-start(f32[512,128]{1,0:T(8,128)S(1)} %get-tuple-element.45), channel_id=1, source_target_pairs={{0,16},{4,12},{8,24},{12,4},{16,0},{20,28},{24,8},{28,20},{1,17},{... | collective-permute-start | bytes 786440 | tf_op jit(solution)/shard_map/ppermute | solution.py:434
  8.2 18.5 %collective-permute-start.2 = (f32[512,128]{1,0:T(8,128)S(1)}, f32[512,128]{1,0:T(8,128)S(1)}, u32[]{:S(2)}, u32[]{:S(2)}) collective-permute-start(f32[512,128]{1,0:T(8,128)S(1)} %get-tuple-element.47), channel_id=1, source_target_pairs={{0,4},{4,0},{8,12},{12,8},{16,20},{20,16},{24,28},{28,24},{1,5},{5... | collective-permute-start | bytes 786440 | tf_op jit(solution)/shard_map/ppermute | solution.py:434
  8.2 18.4 %collective-permute-start.3 = (f32[512,128]{1,0:T(8,128)S(1)}, f32[512,128]{1,0:T(8,128)S(1)}, u32[]{:S(2)}, u32[]{:S(2)}) collective-permute-start(f32[512,128]{1,0:T(8,128)S(1)} %get-tuple-element.48), channel_id=1, source_target_pairs={{0,24},{4,28},{8,16},{12,20},{16,8},{20,12},{24,0},{28,4},{1,25},{... | collective-permute-start | bytes 786440 | tf_op jit(solution)/shard_map/ppermute | solution.py:434
  8.3 18.3 %collective-permute-start.4 = (f32[512,128]{1,0:T(8,128)S(1)}, f32[512,128]{1,0:T(8,128)S(1)}, u32[]{:S(2)}, u32[]{:S(2)}) collective-permute-start(f32[512,128]{1,0:T(8,128)S(1)} %get-tuple-element.49), channel_id=1, source_target_pairs={{0,12},{4,16},{8,4},{12,24},{16,28},{20,0},{24,20},{28,8},{1,13},{... | collective-permute-start | bytes 786440 | tf_op jit(solution)/shard_map/ppermute | solution.py:434
  11.1 16.9 %collective-permute-start.6 = (f32[512,128]{1,0:T(8,128)S(1)}, f32[512,128]{1,0:T(8,128)S(1)}, u32[]{:S(2)}, u32[]{:S(2)}) collective-permute-start(f32[512,128]{1,0:T(8,128)S(1)} %get-tuple-element.51), channel_id=1, source_target_pairs={{0,28},{4,24},{8,20},{12,16},{16,12},{20,8},{24,4},{28,0},{1,29},{... | collective-permute-start | bytes 786440 | tf_op jit(solution)/shard_map/ppermute | solution.py:434
  12.5 15.8 %collective-permute-start.5 = (f32[512,128]{1,0:T(8,128)S(1)}, f32[512,128]{1,0:T(8,128)S(1)}, u32[]{:S(2)}, u32[]{:S(2)}) collective-permute-start(f32[512,128]{1,0:T(8,128)S(1)} %get-tuple-element.50), channel_id=1, source_target_pairs={{0,20},{4,8},{8,28},{12,0},{16,4},{20,24},{24,12},{28,16},{1,21},{... | collective-permute-start | bytes 786440 | tf_op jit(solution)/shard_map/ppermute | solution.py:434
  28.3 28.3 %copy-start = (f32[16,512,128]{2,1,0:T(8,128)S(1)}, f32[16,512,128]{2,1,0:T(8,128)}, u32[]{:S(2)}) copy-start(f32[16,512,128]{2,1,0:T(8,128)} %init_ref.11) | copy-start | bytes 12582916
  43.4 11.4 %collective-permute-start.7 = (f32[512,128]{1,0:T(8,128)S(1)}, f32[512,128]{1,0:T(8,128)S(1)}, u32[]{:S(2)}, u32[]{:S(2)}) collective-permute-start(f32[512,128]{1,0:T(8,128)S(1)} %get-tuple-element.56), channel_id=1, source_target_pairs={{0,16},{4,12},{8,24},{12,4},{16,0},{20,28},{24,8},{28,20},{1,17},{... | collective-permute-start | bytes 786440 | tf_op jit(solution)/shard_map/ppermute | solution.py:434
  44.1 10.8 %collective-permute-start.10 = (f32[512,128]{1,0:T(8,128)S(1)}, f32[512,128]{1,0:T(8,128)S(1)}, u32[]{:S(2)}, u32[]{:S(2)}) collective-permute-start(f32[512,128]{1,0:T(8,128)S(1)} %get-tuple-element.60), channel_id=1, source_target_pairs={{0,8},{4,20},{8,0},{12,28},{16,24},{20,4},{24,16},{28,12},{1,9},{5... | collective-permute-start | bytes 786440 | tf_op jit(solution)/shard_map/ppermute | solution.py:434
  45.2 17.8 %collective-permute-start.9 = (f32[512,128]{1,0:T(8,128)S(1)}, f32[512,128]{1,0:T(8,128)S(1)}, u32[]{:S(2)}, u32[]{:S(2)}) collective-permute-start(f32[512,128]{1,0:T(8,128)S(1)} %get-tuple-element.58), channel_id=1, source_target_pairs={{0,12},{4,16},{8,4},{12,24},{16,28},{20,0},{24,20},{28,8},{1,13},{... | collective-permute-start | bytes 786440 | tf_op jit(solution)/shard_map/ppermute | solution.py:434
  45.5 16.3 %collective-permute-start.12 = (f32[512,128]{1,0:T(8,128)S(1)}, f32[512,128]{1,0:T(8,128)S(1)}, u32[]{:S(2)}, u32[]{:S(2)}) collective-permute-start(f32[512,128]{1,0:T(8,128)S(1)} %get-tuple-element.62), channel_id=1, source_target_pairs={{0,24},{4,28},{8,16},{12,20},{16,8},{20,12},{24,0},{28,4},{1,25},{... | collective-permute-start | bytes 786440 | tf_op jit(solution)/shard_map/ppermute | solution.py:434
  47.7 8.9 %collective-permute-start.13 = (f32[512,128]{1,0:T(8,128)S(1)}, f32[512,128]{1,0:T(8,128)S(1)}, u32[]{:S(2)}, u32[]{:S(2)}) collective-permute-start(f32[512,128]{1,0:T(8,128)S(1)} %get-tuple-element.66), channel_id=1, source_target_pairs={{0,4},{4,0},{8,12},{12,8},{16,20},{20,16},{24,28},{28,24},{1,5},{5... | collective-permute-start | bytes 786440 | tf_op jit(solution)/shard_map/ppermute | solution.py:434
  54.9 8.7 %collective-permute-start.11 = (f32[512,128]{1,0:T(8,128)S(1)}, f32[512,128]{1,0:T(8,128)S(1)}, u32[]{:S(2)}, u32[]{:S(2)}) collective-permute-start(f32[512,128]{1,0:T(8,128)S(1)} %get-tuple-element.61), channel_id=1, source_target_pairs={{0,20},{4,8},{8,28},{12,0},{16,4},{20,24},{24,12},{28,16},{1,21},{... | collective-permute-start | bytes 786440 | tf_op jit(solution)/shard_map/ppermute | solution.py:434
  54.9 13.5 %collective-permute-start.8 = (f32[512,128]{1,0:T(8,128)S(1)}, f32[512,128]{1,0:T(8,128)S(1)}, u32[]{:S(2)}, u32[]{:S(2)}) collective-permute-start(f32[512,128]{1,0:T(8,128)S(1)} %get-tuple-element.57), channel_id=1, source_target_pairs={{0,28},{4,24},{8,20},{12,16},{16,12},{20,8},{24,4},{28,0},{1,29},{... | collective-permute-start | bytes 786440 | tf_op jit(solution)/shard_map/ppermute | solution.py:434
